TPU v7x, 32 devices: a whole 2x2x4 slice. The times are simulated.
32 devices in a mesh: view: 4 (over y, x), tile: 8 (over z, core).
Axes of the slice: x: 2, y: 2, z: 4, core: 2. Of those that a mesh axis runs over, the one named last changes fastest.
Arguments:
- estimate: float32 [128, 192, 512], P(None, 'tile'), may hold values from 0.5 to 2
- view_stacks: float32 [4, 128, 192, 512], P('view', 'tile'), may hold values from 0 to 4
- profile_z: float32 [4, 31], P('view'), may hold values from 0.2 to 1
- profile_y: float32 [4, 15], P('view'), may hold values from 0.2 to 1
- profile_x: float32 [4, 15], P('view'), may hold values from 0.2 to 1
- offsets: int32 [4], P('view'), may hold values from -16 to 16, as said below
- coverage: int32 [8, 4], P('tile'), may hold values from 0 to 1, as said below
Outputs:
- new_estimate: float32 [128, 192, 512], P(None, 'tile')
Inputs may be any that keep to these rules, and one draw needn't show every extreme that they name: `offsets`: some view has offset 16 and some view has offset -16. `coverage`: every tile is intersected by at least one view.
All inputs are finite; a program needn't handle non-finite values.
Results may differ from a plain program's by a relative error of at most 0.0001.
Values sent between devices are 32-bit elements; how exact they have to be, the bound alone decides.
No kernel may reach another device: no remote copies, remote signals or barrier semaphores. Data moves between devices by JAX's collectives and lax.ppermute only.
A program may use at most 192 MiB of HBM per device.

v0:
```python
import jax
import jax.numpy as jnp
from jax import lax
from jax.sharding import PartitionSpec as P

MAXOFF = 16


def with_halo(cells, sides, width):
    for axis, dim in sides:
        count = lax.axis_size(axis)
        ends = count - 1
        head = lax.slice_in_dim(cells, 0, width, axis=dim)
        tail = lax.slice_in_dim(cells, cells.shape[dim] - width, cells.shape[dim], axis=dim)
        cells = jnp.concatenate(
            [
                lax.ppermute(tail, axis, [(i, (i + 1) % count) for i in range(ends)]),
                cells,
                lax.ppermute(head, axis, [((i + 1) % count, i) for i in range(ends)]),
            ],
            axis=dim,
        )
    return cells


def band_matrix(kernel, rows_out):
    taps_count = kernel.shape[0]
    rows_in = rows_out + taps_count - 1
    out_index = jnp.arange(rows_out, dtype=jnp.int32)
    in_index = jnp.arange(rows_in, dtype=jnp.int32)
    distance = in_index[None, :] - out_index[:, None]
    tap_index = jnp.arange(taps_count, dtype=jnp.int32)
    hits = (distance[None, :, :] == tap_index[:, None, None]).astype(jnp.float32)
    return jnp.sum(hits * kernel[:, None, None], axis=0)


def band_blur(field, kernel, along):
    highest = lax.Precision.HIGHEST
    taps_count = kernel.shape[0]
    half = (taps_count - 1) // 2
    extent = field.shape[along]
    block = min(128, extent)
    count = extent // block
    widths = [(0, 0), (0, 0), (0, 0)]
    widths[along] = (half, block - half)
    padded = jnp.pad(field, widths)
    band = band_matrix(kernel, block)
    head_band = band[:, :block]
    tail_band = band[:, block:]
    head = lax.slice_in_dim(padded, 0, count * block, axis=along)
    tail = lax.slice_in_dim(padded, block, (count + 1) * block, axis=along)
    if along == 0:
        head = head.reshape((count, block) + field.shape[1:])
        tail = tail.reshape((count, block) + field.shape[1:])[:, : taps_count - 1]
        result = jnp.einsum(
            "jbyx,ob->joyx", head, head_band, precision=highest, preferred_element_type=jnp.float32
        )
        result = result + jnp.einsum(
            "jbyx,ob->joyx", tail, tail_band, precision=highest, preferred_element_type=jnp.float32
        )
        return result.reshape(field.shape)
    head = head.reshape(field.shape[:2] + (count, block))
    tail = tail.reshape(field.shape[:2] + (count, block))[..., : taps_count - 1]
    result = jnp.einsum(
        "zyjb,ob->zyjo", head, head_band, precision=highest, preferred_element_type=jnp.float32
    )
    result = result + jnp.einsum(
        "zyjb,ob->zyjo", tail, tail_band, precision=highest, preferred_element_type=jnp.float32
    )
    return result.reshape(field.shape)


def blur_rows(field, matrix_y, weights_z, weights_x):
    highest = lax.Precision.HIGHEST
    result = band_blur(field, weights_z, 0)
    result = jnp.einsum(
        "ya,zax->zyx", matrix_y, result, precision=highest, preferred_element_type=jnp.float32
    )
    return band_blur(result, weights_x, 2)


def on_device(estimate, view_stacks, profile_z, profile_y, profile_x, offsets, coverage):
    weights_z = profile_z[0] / jnp.sum(profile_z[0])
    weights_y = profile_y[0] / jnp.sum(profile_y[0])
    weights_x = profile_x[0] / jnp.sum(profile_x[0])
    row_count = estimate.shape[1]
    x_cells = estimate.shape[2]
    half_y = (weights_y.shape[0] - 1) // 2
    padded = jnp.pad(view_stacks[0], ((0, 0), (0, 0), (MAXOFF, MAXOFF)))
    shifted = lax.dynamic_slice_in_dim(padded, MAXOFF + offsets[0], x_cells, 2)
    stacked = lax.all_to_all(shifted, "tile", split_axis=1, concat_axis=0, tiled=True)
    flipped = weights_y[::-1]
    back_z = weights_z[::-1]
    back_x = weights_x[::-1]
    estimate_ext = with_halo(estimate, (("tile", 1),), 2 * half_y)
    measured_ext = with_halo(stacked, (("tile", 1),), half_y)
    blurred = blur_rows(
        estimate_ext, band_matrix(weights_y, row_count + 2 * half_y), weights_z, weights_x
    )
    quotient = measured_ext / blurred
    back_blur = blur_rows(quotient, band_matrix(flipped, row_count), back_z, back_x)
    view_index = lax.axis_index("view")
    covered = lax.dynamic_index_in_dim(coverage[0], view_index, 0, keepdims=False).astype(
        jnp.float32
    )
    view_count = jnp.sum(coverage[0]).astype(jnp.float32)
    weighted = covered * back_blur
    summed = lax.psum(weighted, "view")
    return estimate * summed / view_count


def solution(mesh):
    return jax.shard_map(
        on_device,
        mesh=mesh,
        in_specs=(
            P(None, "tile", None),
            P("view", "tile", None, None),
            P("view", None),
            P("view", None),
            P("view", None),
            P("view"),
            P("tile", None),
        ),
        out_specs=P(None, "tile", None),
        check_vma=False,
    )
```

profile of v0, /device:TPU:16, one launch (start us, length us, event | category | flops | bytes accessed | tf_op | source)
XLA Modules:
  0.0 547.3 jit_solution(4031677347015346435)
XLA Ops:
  6.5 6.6 %copy.75 = f32[128,24,512]{2,0,1:T(8,128)S(1)} copy(f32[128,24,512]{2,1,0:T(8,128)} %param.7) | data formatting | bytes 12582912 | tf_op args[0]
  13.1 4.4 fusion.33
  17.5 1.9 collective-permute-start.2
  19.4 3.6 collective-permute-start.3
  23.8 6.3 %copy.113 = f32[1,16,192,512]{3,1,2,0:T(8,128)} copy(f32[1,16,192,512]{3,2,1,0:T(8,128)S(1)} %bitcast.88) | data formatting | bytes 12582912 | tf_op args[1]
  30.1 7.1 %pad_dynamic-slice_fusion = f32[16,192,512]{2,0,1:T(8,128)} fusion(s32[]{:T(128)S(6)} %select_n.8, f32[16,192,512]{2,0,1:T(8,128)} %bitcast.82), kind=kLoop, calls=%fused_computation.22 | loop fusion | bytes 12582916 | tf_op jit(solution)/shard_map/dynamic_slice | solution.py:90
  37.2 5.7 %all-to-all-start = ((f32[16,192,512]{2,0,1:T(8,128)}), f32[16,192,512]{2,0,1:T(8,128)}, u32[]{:S(2)}, u32[]{:S(2)}) async-start(f32[16,192,512]{2,0,1:T(8,128)} %pad_dynamic-slice_fusion), calls=%async_computation | async-start | bytes 12582912 | tf_op jit(solution)/shard_map/all_to_all | solution.py:91
  43.3 0.7 reduce_sum.90
  44.1 0.6 reduce_sum.93
  44.7 0.7 reduce_sum.95
  45.6 0.6 fusion.34
  46.2 0.6 broadcast_divide_fusion.2
  46.9 0.6 broadcast_divide_fusion.3
  47.7 0.6 broadcast_divide_fusion
  48.6 0.6 broadcast_divide_fusion.4
  49.2 0.6 select_reduce_fusion.1
  49.8 63.4 %collective-permute-done.2 = f32[128,14,512]{2,0,1:T(8,128)} collective-permute-done((f32[128,14,512]{2,0,1:T(8,128)}, f32[128,14,512]{2,0,1:T(8,128)}, u32[]{:S(2)}, u32[]{:S(2)}) %collective-permute-start.2) | collective-permute-done | bytes 3670048 | tf_op jit(solution)/shard_map/ppermute | solution.py:17
  113.2 18.3 %select_maximum_fusion = f32[256,52,512]{2,0,1:T(8,128)} fusion(f32[128,14,512]{2,0,1:T(8,128)} %collective-permute-done.3, f32[128,24,512]{2,0,1:T(8,128)} %copy-done, f32[128,14,512]{2,0,1:T(8,128)} %collective-permute-done.2), kind=kLoop, calls=%fused_computation.2 | loop fusion | flops 54525952 | bytes 40894464 | tf_op jit(solution)/shard_map/concatenate | solution.py:15
  131.4 12.7 %slice_bitcast_fusion = f32[1,128,52,512]{3,1,2,0:T(8,128)} fusion(f32[256,52,512]{2,0,1:T(8,128)} %select_maximum_fusion), kind=kLoop, calls=%fused_computation.11 | loop fusion | bytes 27262976 | tf_op jit(solution)/shard_map/reshape | solution.py:54
  144.1 15.3 %fusion.18 = f32[128,52,512]{2,0,1:T(8,128)} fusion(f32[1,128,52,512]{3,1,2,0:T(8,128)} %slice_bitcast_fusion, f32[128,158]{0,1:T(8,128)S(1)} %get-tuple-element.6), kind=kOutput, calls=%fused_computation.32 | convolution fusion | flops 1226833920 | bytes 17055744 | tf_op jit(solution)/shard_map/jbyx,ob->joyx/dot_general | solution.py:58
  159.4 19.9 %fusion.9 = f32[128,52,512]{2,0,1:T(8,128)} fusion(f32[128,52,512]{2,0,1:T(8,128)} %fusion.18, f32[256,52,512]{2,0,1:T(8,128)} %select_maximum_fusion, f32[128,158]{0,1:T(8,128)S(1)} %get-tuple-element.6), kind=kOutput, calls=%fused_computation.19 | convolution fusion | flops 5237899264 | bytes 40960000 | tf_op jit(solution)/shard_map/jbyx,ob->joyx/dot_general | solution.py:55
  179.4 27.5 %fusion.14 = f32[128,38,512]{2,1,0:T(8,128)} fusion(f32[128,52,512]{2,0,1:T(8,128)} %fusion.9, f32[38,52]{1,0:T(8,128)S(1)} %select_reduce_fusion.4), kind=kOutput, calls=%fused_computation.28 | convolution fusion | flops 1553989632 | bytes 23600864 | tf_op jit(solution)/shard_map/ya,zax->zyx/dot_general | solution.py:76
  206.9 6.5 %copy.70 = f32[8,16,24,512]{3,2,1,0:T(8,128)S(1)} copy(f32[8,16,24,512]{3,1,2,0:T(8,128)} %bitcast.8) | data formatting | bytes 12582912 | tf_op jit(solution)/shard_map/all_to_all | solution.py:91
  213.4 3.6 copy.71
  217.1 2.7 copy-done.1
  219.8 2.2 fusion.32
  221.9 1.9 collective-permute-start
  223.8 3.6 collective-permute-start.1
  227.5 10.1 %pad_slice_fusion.2 = (f32[128,38,512]{2,1,0:T(8,128)}, f32[128,38,512]{2,1,0:T(8,128)}) fusion(f32[128,38,512]{2,1,0:T(8,128)S(1)} %bitcast.79), kind=kLoop, calls=%fused_computation.9 | loop fusion | bytes 29884416 | tf_op jit(solution)/shard_map/slice | solution.py:51
  237.6 11.3 %copy.79 = f32[128,38,512]{0,2,1:T(8,128)} copy(f32[128,38,512]{2,1,0:T(8,128)} %get-tuple-element.10) | data formatting | bytes 19922944 | tf_op jit(solution)/shard_map/slice | solution.py:50
  248.9 11.3 %copy.82 = f32[128,38,512]{0,2,1:T(8,128)} copy(f32[128,38,512]{2,1,0:T(8,128)} %get-tuple-element.9) | data formatting | bytes 19922944 | tf_op jit(solution)/shard_map/slice | solution.py:51
  260.2 12.6 %fusion.28 = f32[128,38,4,128]{0,3,2,1:T(8,128)S(1)} fusion(f32[128,38,4,128]{0,3,2,1:T(8,128)} %bitcast.80, f32[128,142]{0,1:T(8,128)S(1)} %get-tuple-element.8), kind=kOutput, calls=%fused_computation.53 | convolution fusion | flops 3825205248 | bytes 19988480 | tf_op jit(solution)/shard_map/zyjb,ob->zyjo/dot_general | solution.py:64
  272.8 12.2 %convolution_add_fusion = f32[128,38,4,128]{0,3,2,1:T(8,128)} fusion(f32[128,38,4,128]{0,3,2,1:T(8,128)S(1)} %fusion.28, f32[128,38,4,128]{0,3,2,1:T(8,128)} %bitcast.85, f32[128,142]{0,1:T(8,128)S(1)} %get-tuple-element.8), kind=kOutput, calls=%fused_computation.30 | convolution fusion | flops 420872192 | bytes 21176320 | tf_op jit(solution)/shard_map/zyjb,ob->zyjo/dot_general | solution.py:67
  285.0 10.6 %copy.83 = f32[128,38,512]{2,0,1:T(8,128)} copy(f32[128,38,512]{0,2,1:T(8,128)} %bitcast.81) | data formatting | bytes 19922944 | tf_op jit(solution)/shard_map/reshape | solution.py:70
  295.6 7.6 %maximum_divide_fusion = f32[128,38,512]{2,0,1:T(8,128)S(1)} fusion(f32[128,38,512]{2,0,1:T(8,128)} %copy.83, f32[128,7,512]{2,0,1:T(8,128)} %collective-permute-done.1, f32[128,24,512]{2,0,1:T(8,128)} %copy-done.1, f32[128,7,512]{2,0,1:T(8,128)S(1)} %collective-permute-done), kind=kLoop, calls=%fused_computation.18 | loop fusion | flops 7471104 | bytes 29884416 | tf_op jit(solution)/shard_map/div | solution.py:100
  303.2 1.3 fusion.8
  304.5 10.6 %fusion.24 = f32[128,38,512]{2,0,1:T(8,128)} fusion(f32[1,128,38,512]{3,1,2,0:T(8,128)S(1)} %fusion.8, f32[128,158]{0,1:T(8,128)S(1)} %get-tuple-element.5), kind=kOutput, calls=%fused_computation.38 | convolution fusion | flops 896532480 | bytes 12468224 | tf_op jit(solution)/shard_map/jbyx,ob->joyx/dot_general | solution.py:58
  315.1 14.3 %fusion.17 = f32[128,38,512]{2,0,1:T(8,128)S(1)} fusion(f32[128,38,512]{2,0,1:T(8,128)} %fusion.24, f32[128,38,512]{2,0,1:T(8,128)S(1)} %maximum_divide_fusion, f32[128,158]{0,1:T(8,128)S(1)} %get-tuple-element.5), kind=kOutput, calls=%fused_computation.29 | convolution fusion | flops 3827695616 | bytes 29949952 | tf_op jit(solution)/shard_map/jbyx,ob->joyx/dot_general | solution.py:55
  329.4 18.2 %fusion.21 = f32[128,24,512]{2,1,0:T(8,128)S(1)} fusion(f32[128,38,512]{2,0,1:T(8,128)S(1)} %fusion.17, f32[24,38]{1,0:T(8,128)S(1)} %select_reduce_fusion.5), kind=kOutput, calls=%fused_computation.33 | convolution fusion | flops 717225984 | bytes 16256576 | tf_op jit(solution)/shard_map/ya,zax->zyx/dot_general | solution.py:76
  347.6 6.4 %pad_slice_fusion.6 = (f32[128,24,512]{2,1,0:T(8,128)}, f32[128,24,512]{2,1,0:T(8,128)}) fusion(f32[128,24,512]{2,1,0:T(8,128)S(1)} %fusion.21), kind=kLoop, calls=%fused_computation.21 | loop fusion | bytes 18874368 | tf_op jit(solution)/shard_map/slice | solution.py:50
  354.0 6.5 %copy.95 = f32[128,24,512]{0,2,1:T(8,128)} copy(f32[128,24,512]{2,1,0:T(8,128)} %get-tuple-element.12) | data formatting | bytes 12582912 | tf_op jit(solution)/shard_map/reshape | solution.py:63
  360.5 7.6 %reshape.130 = f32[128,24,4,128]{3,2,1,0:T(4,128)} reshape(f32[128,24,512]{2,1,0:T(8,128)} %get-tuple-element.11) | data formatting | bytes 12582912 | tf_op jit(solution)/shard_map/reshape | solution.py:62
  368.1 6.5 %fusion.26 = f32[128,24,4,128]{0,3,2,1:T(8,128)S(1)} fusion(f32[128,24,4,128]{0,3,2,1:T(8,128)} %bitcast.86, f32[128,142]{0,1:T(8,128)S(1)} %get-tuple-element.7), kind=kOutput, calls=%fused_computation.43 | convolution fusion | flops 264241152 | bytes 7086080 | tf_op jit(solution)/shard_map/zyjb,ob->zyjo/dot_general | solution.py:67
  374.6 11.4 %add_multiply_fusion = f32[128,24,4,128]{0,3,2,1:T(8,128)} fusion(f32[128,24,4,128]{0,3,2,1:T(8,128)S(1)} %fusion.26, f32[]{:T(128)} %bitcast, f32[128,24,4,128]{3,2,1,0:T(4,128)S(1)} %copy-done.2, f32[128,142]{0,1:T(8,128)S(1)} %get-tuple-element.7), kind=kOutput, calls=%fused_computation.27 | convolution fusion | flops 2419064832 | bytes 18939908 | tf_op jit(solution)/shard_map/zyjb,ob->zyjo/dot_general | solution.py:64
  386.0 6.7 %copy.88 = f32[128,24,512]{2,1,0:T(8,128)} copy(f32[128,24,512]{0,2,1:T(8,128)} %bitcast.84) | data formatting | bytes 12582912 | tf_op jit(solution)/shard_map/mul | solution.py:107
  392.7 0.6 reduce_sum.99
  394.0 137.4 %all-reduce.7.cloned.1.call-done = f32[128,24,512]{2,1,0:T(8,128)} async-done(((f32[128,24,512]{2,1,0:T(8,128)}), f32[128,24,512]{2,1,0:T(8,128)}) %all-reduce.7.cloned.1.call-update) | async-done | bytes 6291472 | tf_op jit(solution)/shard_map/psum | solution.py:108
  531.3 8.9 %multiply_divide_fusion = f32[128,24,512]{2,1,0:T(8,128)} fusion(f32[128,24,512]{2,1,0:T(8,128)} %param.7, f32[128,24,512]{2,1,0:T(8,128)} %all-reduce.7.cloned.1.call-done, f32[]{:T(128)S(6)} %convert_element_type.27), kind=kLoop, calls=%fused_computation.26 | loop fusion | flops 3145728 | bytes 18874372 | tf_op jit(solution)/shard_map/div | solution.py:109
  (41 shorter events, 1.3 us)
Async XLA Ops:
  6.5 17.2 %slice-start.3 = ((s8[6291456]{0:T(1024)(128)(4,1)}), s8[4194304]{0:T(1024)(128)(4,1)S(1)}, s32[]{:S(2)}) async-start(s8[6291456]{0:T(1024)(128)(4,1)} %bitcast.87), calls=%async_computation.5 | async-start | bytes 8388608
  13.1 16.9 %copy-start = (f32[128,24,512]{2,0,1:T(8,128)}, f32[128,24,512]{2,0,1:T(8,128)S(1)}, u32[]{:S(2)}) copy-start(f32[128,24,512]{2,0,1:T(8,128)S(1)} %copy.75) | copy-start | bytes 18874372
  13.1 10.6 %slice-start.4 = ((s8[6291456]{0:T(1024)(128)(4,1)}), s8[2097152]{0:T(1024)(128)(4,1)S(1)}, s32[]{:S(2)}) async-start(s8[6291456]{0:T(1024)(128)(4,1)} %bitcast.87), calls=%async_computation.6 | async-start | bytes 4194304
  17.5 95.6 %collective-permute-start.2 = (f32[128,14,512]{2,0,1:T(8,128)}, f32[128,14,512]{2,0,1:T(8,128)}, u32[]{:S(2)}, u32[]{:S(2)}) collective-permute-start(f32[128,14,512]{2,0,1:T(8,128)} %get-tuple-element.15), channel_id=1, source_target_pairs={{0,1},{1,2},{2,3},{3,4},{4,5},{5,6},{6,7},{8,9},{9,10},{10,11},{11... | collective-permute-start | bytes 11010056 | tf_op jit(solution)/shard_map/ppermute | solution.py:17
  19.4 93.7 %collective-permute-start.3 = (f32[128,14,512]{2,0,1:T(8,128)}, f32[128,14,512]{2,0,1:T(8,128)}, u32[]{:S(2)}, u32[]{:S(2)}) collective-permute-start(f32[128,14,512]{2,0,1:T(8,128)} %get-tuple-element.16), channel_id=1, source_target_pairs={{1,0},{2,1},{3,2},{4,3},{5,4},{6,5},{7,6},{9,8},{10,9},{11,10},{12... | collective-permute-start | bytes 11010056 | tf_op jit(solution)/shard_map/ppermute | solution.py:19
  37.2 6.1 %copy-start.4 = (f32[1,31]{1,0:T(1,128)S(1)}, f32[1,31]{1,0:T(1,128)}, u32[]{:S(2)}) copy-start(f32[1,31]{1,0:T(1,128)} %param.9) | copy-start | bytes 376
  37.2 6.9 %copy-start.5 = (f32[1,15]{1,0:T(1,128)S(1)}, f32[1,15]{1,0:T(1,128)}, u32[]{:S(2)}) copy-start(f32[1,15]{1,0:T(1,128)} %param.10) | copy-start | bytes 184
  37.2 7.5 %copy-start.3 = (f32[1,15]{1,0:T(1,128)S(1)}, f32[1,15]{1,0:T(1,128)}, u32[]{:S(2)}) copy-start(f32[1,15]{1,0:T(1,128)} %param.11) | copy-start | bytes 184
  37.2 8.4 %copy-start.6 = (s32[1,4]{1,0:T(1,128)S(1)}, s32[1,4]{1,0:T(1,128)}, u32[]{:S(2)}) copy-start(s32[1,4]{1,0:T(1,128)} %param.13) | copy-start | bytes 52
  37.2 169.7 %all-to-all-start = ((f32[16,192,512]{2,0,1:T(8,128)}), f32[16,192,512]{2,0,1:T(8,128)}, u32[]{:S(2)}, u32[]{:S(2)}) async-start(f32[16,192,512]{2,0,1:T(8,128)} %pad_dynamic-slice_fusion), calls=%async_computation | async-start | bytes 12582912 | tf_op jit(solution)/shard_map/all_to_all | solution.py:91
  42.8 488.5 %all-reduce.7.cloned.1.call-start = ((), (), s32[]{:S(2)}) async-start(), calls=%async_computation.1 | async-start | bytes 12582912 | tf_op jit(solution)/shard_map/psum | solution.py:108
  206.9 20.6 %slice-start = ((s8[10485760]{0:T(1024)(128)(4,1)}), s8[4194304]{0:T(1024)(128)(4,1)S(1)}, s32[]{:S(2)}) async-start(s8[10485760]{0:T(1024)(128)(4,1)} %bitcast.78), calls=%async_computation.2 | async-start | bytes 8388608
  206.9 20.6 %slice-start.1 = ((s8[10485760]{0:T(1024)(128)(4,1)}), s8[4194304]{0:T(1024)(128)(4,1)S(1)}, s32[]{:S(2)}) async-start(s8[10485760]{0:T(1024)(128)(4,1)} %bitcast.78), calls=%async_computation.3 | async-start | bytes 8388608
  213.4 14.1 %slice-start.2 = ((s8[10485760]{0:T(1024)(128)(4,1)}), s8[2097152]{0:T(1024)(128)(4,1)S(1)}, s32[]{:S(2)}) async-start(s8[10485760]{0:T(1024)(128)(4,1)} %bitcast.78), calls=%async_computation.4 | async-start | bytes 4194304
  217.0 2.7 copy-start.1
  221.9 73.7 %collective-permute-start = (f32[128,7,512]{2,0,1:T(8,128)}, f32[128,7,512]{2,0,1:T(8,128)S(1)}, u32[]{:S(2)}, u32[]{:S(2)}) collective-permute-start(f32[128,7,512]{2,0,1:T(8,128)} %get-tuple-element.13), channel_id=1, source_target_pairs={{0,1},{1,2},{2,3},{3,4},{4,5},{5,6},{6,7},{8,9},{9,10},{10,11},{11... | collective-permute-start | bytes 5505032 | tf_op jit(solution)/shard_map/ppermute | solution.py:17
  223.8 71.8 %collective-permute-start.1 = (f32[128,7,512]{2,0,1:T(8,128)}, f32[128,7,512]{2,0,1:T(8,128)}, u32[]{:S(2)}, u32[]{:S(2)}) collective-permute-start(f32[128,7,512]{2,0,1:T(8,128)} %get-tuple-element.14), channel_id=1, source_target_pairs={{1,0},{2,1},{3,2},{4,3},{5,4},{6,5},{7,6},{9,8},{10,9},{11,10},{12... | collective-permute-start | bytes 5505032 | tf_op jit(solution)/shard_map/ppermute | solution.py:19
  368.1 6.5 %copy-start.2 = (f32[128,24,4,128]{3,2,1,0:T(4,128)S(1)}, f32[128,24,4,128]{3,2,1,0:T(4,128)}, u32[]{:S(2)}) copy-start(f32[128,24,4,128]{3,2,1,0:T(4,128)} %reshape.130) | copy-start | bytes 18874372
Sparse Core Ops, SparseCore 0:
  392.8 138.5 all-reduce.6
where the time goes:
time: 558 us; the launch traced here: 547 us
  waiting for transfers between devices  201 us (36%)
  matrix products  148 us (27%)
  local copies, waits for them, and re-layouts  124 us (22%)
  other arithmetic  41.4 us (7%)
  starting transfers between devices  17.2 us (3%)
  between operations  15.2 us (3%)
    psum x1, waiting for transfers between devices, on_device(): summed = lax.psum(weighted, 'view')  137 us
    ppermute x2, waiting for transfers between devices, with_halo(): lax.ppermute(tail, axis, [(i, (i + 1) % count) for i in range(ends)])  63.4 us
    dot_general x2, matrix products, blur_rows(): jnp.einsum('ya,zax->zyx', matrix_y, result, precision=highest, preferred_...  45.7 us
    dot_general x2, matrix products, band_blur(): jnp.einsum('jbyx,ob->joyx', head, head_band, precision=highest, preferred...  34.2 us
    dot_general x2, matrix products, band_blur(): jnp.einsum('jbyx,ob->joyx', tail, tail_band, precision=highest, preferred...  25.9 us
    dot_general x2, matrix products, band_blur(): jnp.einsum('zyjb,ob->zyjo', head, head_band, precision=highest, preferred...  24 us
    slice x2, local copies, waits for them, and re-layouts, band_blur(): tail = lax.slice_in_dim(padded, block, (count + 1) * block, axis=along)  21.4 us
    dot_general x2, matrix products, band_blur(): jnp.einsum('zyjb,ob->zyjo', tail, tail_band, precision=highest, preferred...  18.6 us
  transfers between devices with their start and end apart: 6, of which 2 were waited for; matrix products, arithmetic and copies ran while one was open for 33% of the time, Pallas kernels for 0%

commit v1 on v0

v1 whole, which is shorter than its diff:
```python
import functools

import jax
import jax.numpy as jnp
from jax import lax
from jax.experimental import pallas as pl
from jax.experimental.pallas import tpu as pltpu
from jax.sharding import PartitionSpec as P

LANES = 128
F32 = jnp.float32
BF16 = jnp.bfloat16
SMEM = pl.BlockSpec(memory_space=pltpu.SMEM)
VMEM = pl.BlockSpec(memory_space=pltpu.VMEM)
ANY = pl.BlockSpec(memory_space=pl.ANY)


def sds(shape, dtype=F32):
    return jax.ShapeDtypeStruct(shape, dtype)


def params(mib):
    return pltpu.CompilerParams(vmem_limit_bytes=mib << 20)


def split(value):
    high = value.astype(BF16)
    return high, (value - high.astype(F32)).astype(BF16)


def dot(a, b):
    return jnp.dot(a, b, preferred_element_type=F32)


def prep_kernel(lead, scalars, stack_ref, *out_refs):
    planes, rows, cells = stack_ref.shape
    offset = scalars[0]
    lane = lax.broadcasted_iota(jnp.int32, (1, 1, cells), 2)
    column = lane + lead
    column = jnp.where(column >= cells, column - cells, column)
    source = column + offset
    inside = (source >= 0) & (source < cells)
    shift = lax.rem(2 * cells - lead - offset, cells)
    rolled = pltpu.roll(stack_ref[...].reshape(planes * rows, cells), shift, 1)
    rolled = jnp.where(inside, rolled.reshape(planes, rows, cells), 0.0)
    for index, out_ref in enumerate(out_refs):
        out_ref[0] = rolled[:, :, index * LANES : (index + 1) * LANES]


def prep(stack, offset, tiles, lead):
    planes, all_rows, cells = stack.shape
    rows = all_rows // tiles
    count = cells // LANES
    return pl.pallas_call(
        functools.partial(prep_kernel, lead),
        grid=(tiles,),
        in_specs=[SMEM, pl.BlockSpec((planes, rows, cells), lambda i: (0, i, 0))],
        out_specs=[pl.BlockSpec((1, planes, rows, LANES), lambda i: (i, 0, 0, 0))] * count,
        out_shape=[sds((tiles, planes, rows, LANES))] * count,
        compiler_params=params(32),
        name="prep",
    )(offset, stack)


def swap_kernel(in_ref, out_ref):
    out_ref[...] = jnp.swapaxes(in_ref[...], 0, 1)


def swap(cells):
    planes, rows, width = cells.shape
    return pl.pallas_call(
        swap_kernel,
        grid=(planes // 16,),
        in_specs=[pl.BlockSpec((16, rows, width), lambda i: (i, 0, 0))],
        out_specs=pl.BlockSpec((rows, 16, width), lambda i: (0, i, 0)),
        out_shape=sds((rows, planes, width)),
        name="swap",
    )(cells)


def place_rows(even, own, inner, outer, buffer, sems, half):
    rows = own.shape[0]
    inner_at = jnp.where(even == 1, half + rows, 0)
    outer_at = jnp.where(even == 1, 0, half + rows)
    copies = [
        pltpu.make_async_copy(own, buffer.at[pl.ds(half, rows)], sems.at[0]),
        pltpu.make_async_copy(inner, buffer.at[pl.ds(inner_at, half)], sems.at[1]),
        pltpu.make_async_copy(outer, buffer.at[pl.ds(outer_at, half)], sems.at[2]),
    ]
    for copy in copies:
        copy.start()
    for copy in copies:
        copy.wait()


def blur_y(buffer, weights, taps, rows, planes_at, lanes_at):
    at = (pl.ds(planes_at, 16), pl.ds(lanes_at, LANES))
    cells = [buffer[(r, *at)] for r in range(rows + taps - 1)]
    for r in range(rows):
        total = weights[0] * cells[r]
        for tap in range(1, taps):
            total = total + weights[tap] * cells[r + tap]
        yield r, split(total)


def forward_kernel(taps, scalars, weights, own, inner, outer, along_z, high_x, low_x, out_ref, buffer, halves, sems):
    rows, planes, cells = own.shape
    half = (taps - 1) // 2
    place_rows(scalars[0], own, inner, outer, buffer, sems, half)

    def step_y(index, carry):
        planes_at = pl.multiple_of((index // (cells // LANES)) * 16, 16)
        lanes_at = pl.multiple_of((index % (cells // LANES)) * LANES, LANES)
        for r, (high, low) in blur_y(buffer, weights, taps, rows, planes_at, lanes_at):
            halves[r, pl.ds(planes_at, 16), pl.ds(lanes_at, LANES)] = high
            halves[r, pl.ds(planes + planes_at, 16), pl.ds(lanes_at, LANES)] = low
        return carry

    lax.fori_loop(0, (planes // 16) * (cells // LANES), step_y, 0)
    group = 4

    def step_zx(index, carry):
        parts = []
        for g in range(group):
            both = dot(along_z[...], halves[index * group + g])
            parts.append(both[:planes] + both[planes:])
        high, low = split(jnp.concatenate(parts, axis=0))
        result = dot(high, high_x[...]) + dot(low, high_x[...]) + dot(high, low_x[...])
        out_ref[pl.ds(index * group, group)] = result.reshape(group, planes, cells)
        return carry

    lax.fori_loop(0, rows // group, step_zx, 0)


def forward(even, weights, own, inner, outer, along_z, high_x, low_x):
    rows, planes, cells = own.shape
    taps = weights.shape[0]
    return pl.pallas_call(
        functools.partial(forward_kernel, taps),
        in_specs=[SMEM, SMEM, ANY, ANY, ANY, VMEM, VMEM, VMEM],
        out_specs=VMEM,
        out_shape=sds((rows, planes, cells)),
        scratch_shapes=[
            pltpu.VMEM((rows + taps - 1, planes, cells), F32),
            pltpu.VMEM((rows, 2 * planes, cells), BF16),
            pltpu.SemaphoreType.DMA((3,)),
        ],
        compiler_params=params(48),
        cost_estimate=pl.CostEstimate(flops=20_000_000_000, bytes_accessed=20_000_000, transcendentals=0),
        name="forward",
    )(even, weights, own, inner, outer, along_z, high_x, low_x)


def ratio_kernel(half, scalars, measured_ref, blurred_ref, out_ref, inner_ref, outer_ref):
    rows = out_ref.shape[0]
    ratio = jnp.swapaxes(measured_ref[...], 0, 1) / blurred_ref[...]
    out_ref[...] = ratio
    even = scalars[0]
    first, last = ratio[:half], ratio[rows - half :]
    inner_ref[...] = jnp.where(even == 1, last, first)
    outer_ref[...] = jnp.where(even == 1, first, last)


def ratio(even, measured, blurred, half, chunk):
    planes, rows, _ = measured.shape
    return pl.pallas_call(
        functools.partial(ratio_kernel, half),
        grid=(planes // 16,),
        in_specs=[
            SMEM,
            pl.BlockSpec((16, rows, LANES), lambda i: (i, 0, 0)),
            pl.BlockSpec((rows, 16, LANES), lambda i: (0, i, chunk)),
        ],
        out_specs=[
            pl.BlockSpec((rows, 16, LANES), lambda i: (0, i, 0)),
            pl.BlockSpec((half, 16, LANES), lambda i: (0, i, 0)),
            pl.BlockSpec((half, 16, LANES), lambda i: (0, i, 0)),
        ],
        out_shape=[
            sds((rows, planes, LANES)),
            sds((half, planes, LANES)),
            sds((half, planes, LANES)),
        ],
        cost_estimate=pl.CostEstimate(flops=1_000_000, bytes_accessed=6_000_000, transcendentals=0),
        name="ratio",
    )(even, measured, blurred)


def back_kernel(taps, blocks, scalars, weights, own, inner, outer, along_z, *refs):
    rows, planes, _ = own.shape
    half = (taps - 1) // 2
    ins = 3 * len(blocks)
    extra, refs = refs[:ins], refs[ins:]
    high_ref, low_ref, refs = refs[0], refs[1], refs[2:]
    quarters, refs = refs[: 4 * len(blocks)], refs[4 * len(blocks) :]
    buffer, halves, totals, sems, out_sems = refs
    place_rows(scalars[0], own, inner, outer, buffer, sems, half)

    def step_y(index, carry):
        planes_at = pl.multiple_of(index * 16, 16)
        for r, (high, low) in blur_y(buffer, weights, taps, rows, planes_at, 0):
            lanes = slice((r % 2) * LANES, (r % 2 + 1) * LANES)
            halves[r // 2, pl.ds(planes_at, 16), lanes] = high
            halves[r // 2, pl.ds(planes + planes_at, 16), lanes] = low
        return carry

    lax.fori_loop(0, planes // 16, step_y, 0)
    group = 4

    def step_zx(index, carry):
        parts = []
        for g in range(group // 2):
            both = dot(along_z[...], halves[index * (group // 2) + g])
            both = both[:planes] + both[planes:]
            parts += [both[:, :LANES], both[:, LANES:]]
        high, low = split(jnp.concatenate(parts, axis=0))
        at = pl.ds(index * group, group)
        high_ref[at] = high.reshape(group, planes, LANES)
        low_ref[at] = low.reshape(group, planes, LANES)
        for number, (_, after) in enumerate(blocks):
            other_high, other_low, along_x = extra[3 * number : 3 * number + 3]
            others = [other_high[at].reshape(-1, LANES), other_low[at].reshape(-1, LANES)]
            result = 0.0
            for mine, other in zip((high, low), others):
                pair = [mine, other] if after else [other, mine]
                result = result + dot(jnp.concatenate(pair, axis=1), along_x[...])
            result = result[:, :LANES] + result[:, LANES:]
            totals[number, at] = result.reshape(group, planes, LANES)
        return carry

    lax.fori_loop(0, rows // group, step_zx, 0)
    copies = []
    size = planes // 4
    for number in range(len(blocks)):
        for k in range(4):
            start = pl.multiple_of((scalars[1] ^ k) * size, size)
            copies.append(
                pltpu.make_async_copy(
                    totals.at[number, :, pl.ds(start, size)], quarters[4 * number + k], out_sems.at[number, k]
                )
            )
    for copy in copies:
        copy.start()
    for copy in copies:
        copy.wait()


def back(scalars, weights, own, inner, outer, along_z, blocks, extra):
    rows, planes, _ = own.shape
    taps = weights.shape[0]
    count = len(blocks)
    outs = pl.pallas_call(
        functools.partial(back_kernel, taps, blocks),
        in_specs=[SMEM, SMEM, ANY, ANY, ANY, VMEM] + [VMEM] * (3 * count),
        out_specs=[VMEM] * 2 + [ANY] * (4 * count),
        out_shape=[sds((rows, planes, LANES), BF16)] * 2
        + [sds((rows, planes // 4, LANES))] * (4 * count),
        scratch_shapes=[
            pltpu.VMEM((rows + taps - 1, planes, LANES), F32),
            pltpu.VMEM((rows // 2, 2 * planes, 2 * LANES), BF16),
            pltpu.VMEM((max(count, 1), rows, planes, LANES), F32),
            pltpu.SemaphoreType.DMA((3,)),
            pltpu.SemaphoreType.DMA((max(count, 1), 4)),
        ],
        compiler_params=params(32),
        cost_estimate=pl.CostEstimate(flops=5_000_000_000, bytes_accessed=6_000_000, transcendentals=0),
        name="back",
    )(scalars, weights, own, inner, outer, along_z, *extra)
    return outs[0], outs[1], [outs[2 + 4 * n : 6 + 4 * n] for n in range(count)]


def merge_kernel(scalars, estimate_ref, a, b, c, d, out_ref):
    total = (a[...] + b[...]) + (c[...] + d[...])
    count = scalars[2].astype(F32)
    out_ref[...] = estimate_ref[...] * jnp.swapaxes(total, 0, 1) / count


def merge(scalars, estimate, parts, chunk):
    rows, size, _ = parts[0].shape
    step = 16
    steps = size // step
    piece = pl.BlockSpec((rows, step, LANES), lambda i, s: (0, i, 0))
    return pl.pallas_call(
        merge_kernel,
        grid_spec=pltpu.PrefetchScalarGridSpec(
            num_scalar_prefetch=1,
            grid=(steps,),
            in_specs=[pl.BlockSpec((step, rows, LANES), lambda i, s: (s[1] * steps + i, 0, chunk))]
            + [piece] * 4,
            out_specs=pl.BlockSpec((step, rows, LANES), lambda i, s: (i, 0, 0)),
        ),
        out_shape=sds((size, rows, LANES)),
        cost_estimate=pl.CostEstimate(flops=1_000_000, bytes_accessed=3_000_000, transcendentals=0),
        name="merge",
    )(scalars, estimate, *parts)


def assemble_kernel(chunk, scalars, *refs):
    pieces, out_ref, sems = refs[:4], refs[-2], refs[-1]
    size = pieces[0].shape[0]
    copies = [
        pltpu.make_async_copy(
            piece,
            out_ref.at[pl.ds((scalars[1] ^ k) * size, size), :, pl.ds(chunk * LANES, LANES)],
            sems.at[k],
        )
        for k, piece in enumerate(pieces)
    ]
    for copy in copies:
        copy.start()
    for copy in copies:
        copy.wait()


def assemble(scalars, pieces, shape, chunk, result):
    earlier = [] if result is None else [result]
    return pl.pallas_call(
        functools.partial(assemble_kernel, chunk),
        in_specs=[SMEM] + [VMEM] * 4 + [ANY] * len(earlier),
        out_specs=ANY,
        out_shape=sds(shape),
        scratch_shapes=[pltpu.SemaphoreType.DMA((4,))],
        input_output_aliases={} if result is None else {5: 0},
        cost_estimate=pl.CostEstimate(flops=0, bytes_accessed=3_000_000, transcendentals=0),
        name="assemble",
    )(scalars, *pieces, *earlier)


def taps_at(distance, profile):
    result = jnp.zeros(distance.shape, F32)
    for tap in range(profile.shape[1]):
        result = jnp.where(distance == tap, profile[0, tap], result)
    return result


def total_of(profile):
    total = profile[0, 0]
    for tap in range(1, profile.shape[1]):
        total = total + profile[0, tap]
    return total


def bands_kernel(scalars, profile_z, profile_y, profile_x, forward_z, back_z, high_x, low_x, back_x):
    planes = forward_z.shape[0] // 2
    cells = high_x.shape[0]
    half_z = (profile_z.shape[1] - 1) // 2
    lead = (profile_x.shape[1] - 1) // 2
    total_z, total_y, total_x = total_of(profile_z), total_of(profile_y), total_of(profile_x)
    row = lax.broadcasted_iota(jnp.int32, (planes, planes), 0)
    column = lax.broadcasted_iota(jnp.int32, (planes, planes), 1)
    for out, distance in ((forward_z, column - row), (back_z, row - column)):
        high, low = split(taps_at(distance + half_z, profile_z) / total_z / total_y)
        for side in (slice(0, planes), slice(planes, 2 * planes)):
            out[:planes, side] = high
            out[planes:, side] = low

    step = 32

    def step_x(index, carry):
        at = pl.multiple_of(index * step, step)
        row = lax.broadcasted_iota(jnp.int32, (step, cells), 0) + at
        column = lax.broadcasted_iota(jnp.int32, (step, cells), 1) + lead
        column = jnp.where(column >= cells, column - cells, column)
        high, low = split(taps_at(row - column + lead, profile_x) / total_x)
        high_x[pl.ds(at, step), :] = high
        low_x[pl.ds(at, step), :] = low
        return carry

    lax.fori_loop(0, cells // step, step_x, 0)
    row = lax.broadcasted_iota(jnp.int32, (2 * LANES, LANES), 0)
    column = lax.broadcasted_iota(jnp.int32, (2 * LANES, LANES), 1)
    matrix = taps_at(column + LANES - row, profile_x) / total_x * scalars[3].astype(F32)
    for block in range(back_x.shape[0]):
        source = row + ((block - 1) * LANES + lead)
        high, low = split(jnp.where((source >= 0) & (source < cells), matrix, 0.0))
        back_x[block, :, :LANES] = high
        back_x[block, :, LANES:] = low


def bands(scalars, profile_z, profile_y, profile_x, planes, cells):
    return pl.pallas_call(
        bands_kernel,
        in_specs=[SMEM] * 4,
        out_specs=[VMEM] * 5,
        out_shape=[
            sds((2 * planes, 2 * planes), BF16),
            sds((2 * planes, 2 * planes), BF16),
            sds((cells, cells), BF16),
            sds((cells, cells), BF16),
            sds((cells // LANES, 2 * LANES, 2 * LANES), BF16),
        ],
        name="bands",
    )(scalars, profile_z, profile_y, profile_x)


def swap_views(cells, mask):
    return lax.ppermute(cells, "view", [(i, i ^ mask) for i in range(4)])


def on_device(estimate, view_stacks, profile_z, profile_y, profile_x, offsets, coverage):
    planes, rows, cells = estimate.shape
    half = (profile_y.shape[1] - 1) // 2
    lead = (profile_x.shape[1] - 1) // 2
    tiles = lax.axis_size("tile")
    tile = lax.axis_index("tile")
    view = lax.axis_index("view")
    chunks = cells // LANES
    even = (tile + 1) % 2
    covered = lax.dynamic_index_in_dim(coverage[0], view, 0, keepdims=False)
    scalars = jnp.stack([even, view, jnp.sum(coverage[0]), covered]).astype(jnp.int32)
    inner_pairs = [(i, i ^ 1) for i in range(tiles)]
    outer_pairs = [(i, i + 1) for i in range(1, tiles - 1, 2)] + [(i + 1, i) for i in range(1, tiles - 1, 2)]

    def exchange(inner, outer):
        return lax.ppermute(inner, "tile", inner_pairs), lax.ppermute(outer, "tile", outer_pairs)

    registered = prep(view_stacks[0], offsets, tiles, lead)

    forward_z, back_z, high_x, low_x, back_x = bands(scalars, profile_z, profile_y, profile_x, planes, cells)
    transposed = swap(estimate)
    first, last = transposed[:half], transposed[rows - half :]
    is_even = even == 1
    inner, outer = exchange(jnp.where(is_even, last, first), jnp.where(is_even, first, last))
    blurred = forward(scalars, profile_y[0], transposed, inner, outer, forward_z, high_x, low_x)

    flipped = profile_y[0, ::-1]
    order = [chunks - 1] + list(range(chunks - 1))
    done = {}
    result = None
    for chunk in order:
        measured = lax.all_to_all(registered[chunk], "tile", split_axis=0, concat_axis=0)
        measured = measured.reshape(planes, rows, LANES)
        quotient, inner, outer = ratio(scalars, measured, blurred, half, chunk)
        inner, outer = exchange(inner, outer)
        blocks, extra = [], []
        for block in (chunk, (chunk + 1) % chunks):
            other = (block - 1) % chunks if block == chunk else block
            if other in done:
                blocks.append((block, block != chunk))
                extra += [done[other][0], done[other][1], back_x[block]]
        high, low, sums = back(scalars, flipped, quotient, inner, outer, back_z, tuple(blocks), extra)
        done[chunk] = (high, low)
        for (block, _), parts in zip(blocks, sums):
            received = [parts[0]] + [swap_views(parts[k], k) for k in (1, 2, 3)]
            new = merge(scalars, estimate, received, block)
            pieces = [new] + [swap_views(new, k) for k in (1, 2, 3)]
            result = assemble(scalars, pieces, estimate.shape, block, result)
    return result


def solution(mesh):
    return jax.shard_map(
        on_device,
        mesh=mesh,
        in_specs=(
            P(None, "tile", None),
            P("view", "tile", None, None),
            P("view", None),
            P("view", None),
            P("view", None),
            P("view"),
            P("tile", None),
        ),
        out_specs=P(None, "tile", None),
        check_vma=False,
    )
```

time: 558 us -> 398 us (0.71); the launches traced: 547 us -> 394 us
  matrix products: 148 us -> 0 us
  Pallas kernels: 0 us -> 113 us
  local copies, waits for them, and re-layouts: 124 us -> 14.1 us
  waiting for transfers between devices: 201 us -> 116 us
  blocking collectives: 0 us -> 80.6 us
  starting transfers between devices: 17.2 us -> 62.9 us
  other arithmetic: 41.4 us -> 7.02 us
  between operations: 15.2 us -> 1.02 us
    dot_general x10 -> x0, matrix products: 148 us -> none  [the longest x2 45.7 us: blur_rows(): jnp.einsum('ya,zax->zyx', matrix_y, result, precision=highest, preferred_...]
    psum x1 -> x0, waiting for transfers between devices: 137 us -> none  [on_device(): summed = lax.psum(weighted, 'view')]
    pallas_call x0 -> x20, Pallas kernels: none -> 113 us  [the longest x4 26.5 us: back(): pl.pallas_call(functools.partial(back_kernel, taps, blocks), in_specs=[SM...]
    all_to_all x0 -> x2, blocking collectives: none -> 80.6 us  [on_device(): lax.all_to_all(registered[chunk], 'tile', split_axis=0, concat_axis=0)]
    slice x6 -> x0, local copies, waits for them, and re-layouts: 45.7 us -> none  [the longest x2 21.4 us: band_blur(): tail = lax.slice_in_dim(padded, block, (count + 1) * block, axis=along)]
    reshape x5 -> x0, local copies, waits for them, and re-layouts: 38.7 us -> none  [the longest x2 14 us: band_blur(): tail = tail.reshape((count, block) + field.shape[1:])[:, :taps_count - 1]]
    ppermute x4 -> x34, starting transfers between devices: 11.1 us -> 48.5 us  [the longest x24 33.1 us: swap_views(): return lax.ppermute(cells, 'view', [(i, i ^ mask) for i in range(4)])]
    ppermute x4 -> x34, waiting for transfers between devices: 63.4 us -> 97.6 us  [the longest x24 66.3 us: swap_views(): return lax.ppermute(cells, 'view', [(i, i ^ mask) for i in range(4)])]
  transfers between devices with their start and end apart: 6 -> 36, of which waited for: 2 -> 12; matrix products, arithmetic and copies ran while one was open for 33% -> 2% of each run, Pallas kernels for 0% -> 27%
where the time goes in v1:
time: 398 us; the launch traced here: 394 us
  waiting for transfers between devices  116 us (29%)
  Pallas kernels  113 us (28%)
  blocking collectives  80.6 us (20%)
  starting transfers between devices  62.9 us (16%)
  local copies, waits for them, and re-layouts  14.1 us (4%)
  other arithmetic  7.02 us (2%)
    all_to_all x2, blocking collectives, on_device(): lax.all_to_all(registered[chunk], 'tile', split_axis=0, concat_axis=0)  80.6 us
    ppermute x24, waiting for transfers between devices, swap_views(): return lax.ppermute(cells, 'view', [(i, i ^ mask) for i in range(4)])  66.3 us
    ppermute x24, starting transfers between devices, swap_views(): return lax.ppermute(cells, 'view', [(i, i ^ mask) for i in range(4)])  33.1 us
    ppermute x5, waiting for transfers between devices, exchange(): lax.ppermute(outer, 'tile', outer_pairs)  31.3 us
    pallas_call x4, Pallas kernels, back(): pl.pallas_call(functools.partial(back_kernel, taps, blocks), in_specs=[SM...  26.5 us
    pallas_call x4, Pallas kernels, ratio(): pl.pallas_call(functools.partial(ratio_kernel, half), grid=(planes // 16,...  25.4 us
    pallas_call x1, Pallas kernels, forward(): pl.pallas_call(functools.partial(forward_kernel, taps), in_specs=[SMEM, S...  21.7 us
    all_to_all x2, waiting for transfers between devices, on_device(): lax.all_to_all(registered[chunk], 'tile', split_axis=0, concat_axis=0)  18.3 us
  transfers between devices with their start and end apart: 36, of which 12 were waited for; matrix products, arithmetic and copies ran while one was open for 2% of the time, Pallas kernels for 27%

profile of v1, /device:TPU:16, one launch (start us, length us, event | category | flops | bytes accessed | tf_op | source)
XLA Modules:
  0.0 394.4 jit_solution(12040539410696297630)
XLA Ops:
  0.7 2.8 copy-done
  3.4 5.0 %prep.1 = (f32[8,16,24,128]{3,2,1,0:T(8,128)S(1)}, f32[8,16,24,128]{3,2,1,0:T(8,128)S(1)}, f32[8,16,24,128]{3,2,1,0:T(8,128)}, f32[8,16,24,128]{3,2,1,0:T(8,128)}) custom-call(s32[1]{0:T(128)S(6)} %copy.14.scalars, f32[16,192,512]{2,1,0:T(8,128)S(1)} %bitcast.19), custom_call_target="tpu_custom_call" | custom-call | tf_op jit(solution)/shard_map/prep/pallas_call | solution.py:54
  8.4 39.6 %all_to_all.20 = f32[8,16,24,128]{3,2,1,0:T(8,128)} all-to-all(f32[8,16,24,128]{3,2,1,0:T(8,128)S(1)} %get-tuple-element.56), channel_id=1, replica_groups=mesh['view'=4,'tile'=8] {'tile'}, dimensions={0} | all-to-all | bytes 3145728 | tf_op jit(solution)/shard_map/all_to_all | solution.py:431
  48.0 40.9 %all_to_all.21 = f32[8,16,24,128]{3,2,1,0:T(8,128)} all-to-all(f32[8,16,24,128]{3,2,1,0:T(8,128)S(1)} %get-tuple-element.60), channel_id=1, replica_groups=mesh['view'=4,'tile'=8] {'tile'}, dimensions={0} | all-to-all | bytes 3145728 | tf_op jit(solution)/shard_map/all_to_all | solution.py:431
  89.0 6.8 %all-to-all-start.3 = ((f32[8,16,24,128]{3,2,1,0:T(8,128)}), f32[8,16,24,128]{3,2,1,0:T(8,128)S(1)}, u32[]{:S(2)}, u32[]{:S(2)}) async-start(f32[8,16,24,128]{3,2,1,0:T(8,128)} %get-tuple-element.64), calls=%async_computation.3 | async-start | bytes 3145728 | tf_op jit(solution)/shard_map/all_to_all | solution.py:431
  95.8 8.2 %swap.1.own = f32[24,128,512]{2,1,0:T(8,128)} custom-call(f32[128,24,512]{2,1,0:T(8,128)} %estimate_ref.7), custom_call_target="tpu_custom_call" | custom-call | tf_op jit(solution)/shard_map/swap/pallas_call | solution.py:71
  104.0 4.4 %slice_select_fusion = (f32[7,128,512]{2,1,0:T(8,128)}, f32[7,128,512]{2,1,0:T(8,128)}) fusion(f32[24,128,512]{2,1,0:T(8,128)} %swap.1.own, pred[]{:T(512)S(6)} %eq.5), kind=kLoop, calls=%fused_computation | loop fusion | flops 917504 | bytes 7340033 | tf_op jit(solution)/shard_map/jit(_where)/select_n | solution.py:423
  108.4 2.3 collective-permute-start.1
  112.1 18.3 %all-to-all-done.3 = f32[8,16,24,128]{3,2,1,0:T(8,128)S(1)} async-done(((f32[8,16,24,128]{3,2,1,0:T(8,128)}), f32[8,16,24,128]{3,2,1,0:T(8,128)S(1)}, u32[]{:S(2)}, u32[]{:S(2)}) %all-to-all-start.3) | async-done | bytes 1572896 | tf_op jit(solution)/shard_map/all_to_all | solution.py:431
  130.4 7.5 %all-to-all-start = ((f32[8,16,24,128]{3,2,1,0:T(8,128)}), f32[8,16,24,128]{3,2,1,0:T(8,128)}, u32[]{:S(2)}, u32[]{:S(2)}) async-start(f32[8,16,24,128]{3,2,1,0:T(8,128)} %get-tuple-element.48), calls=%async_computation | async-start | bytes 3145728 | tf_op jit(solution)/shard_map/all_to_all | solution.py:431
  139.3 1.9 pad_add_fusion.scalars
  141.2 3.5 bands.1
  144.7 31.3 %collective-permute-done.1.outer = f32[7,128,512]{2,1,0:T(8,128)S(1)} collective-permute-done((f32[7,128,512]{2,1,0:T(8,128)}, f32[7,128,512]{2,1,0:T(8,128)S(1)}, u32[]{:S(2)}, u32[]{:S(2)}) %collective-permute-start.1) | collective-permute-done | bytes 1835040 | tf_op jit(solution)/shard_map/ppermute | solution.py:415
  179.7 21.7 %forward.1.blurred_ref = f32[24,128,512]{2,1,0:T(8,128)} custom-call(s32[4]{0:T(128)S(1)} %copy-done.5, f32[15]{0:T(128)S(1)} %bitcast.20, f32[24,128,512]{2,1,0:T(8,128)} %swap.1.own, f32[7,128,512]{2,1,0:T(8,128)} %collective-permute-done.inner, f32[7,128,512]{2,1,0:T(8,128)S(1)} %collective-permute-done.1.outer, bf16[256,256]{1,0:T(8,128)(2,1)S(1)} %copy-done.15, ...), custom_call_target="tpu_custom_call" | custom-call | flops 20000000000 | bytes 20000000 | tf_op jit(solution)/shard_map/forward/pallas_call | solution.py:138
  201.4 6.4 %ratio.7 = (f32[24,128,128]{2,1,0:T(8,128)}, f32[7,128,128]{2,1,0:T(8,128)}, f32[7,128,128]{2,1,0:T(8,128)}) custom-call(s32[4]{0:T(128)} %pad_add_fusion.scalars, f32[128,24,128]{2,1,0:T(8,128)} %bitcast.27, f32[24,128,512]{2,1,0:T(8,128)} %forward.1.blurred_ref), custom_call_target="tpu_custom_call" | custom-call | flops 1000000 | bytes 6000000 | tf_op jit(solution)/shard_map/ratio/pallas_call | solution.py:166
  207.8 3.0 collective-permute-start.9
  211.0 6.3 %ratio.6 = (f32[24,128,128]{2,1,0:T(8,128)}, f32[7,128,128]{2,1,0:T(8,128)}, f32[7,128,128]{2,1,0:T(8,128)}) custom-call(s32[4]{0:T(128)} %pad_add_fusion.scalars, f32[128,24,128]{2,1,0:T(8,128)} %bitcast.26, f32[24,128,512]{2,1,0:T(8,128)} %forward.1.blurred_ref), custom_call_target="tpu_custom_call" | custom-call | flops 1000000 | bytes 6000000 | tf_op jit(solution)/shard_map/ratio/pallas_call | solution.py:166
  217.3 2.5 collective-permute-start.7
  219.9 6.3 %ratio.5 = (f32[24,128,128]{2,1,0:T(8,128)}, f32[7,128,128]{2,1,0:T(8,128)}, f32[7,128,128]{2,1,0:T(8,128)}) custom-call(s32[4]{0:T(128)} %pad_add_fusion.scalars, f32[128,24,128]{2,1,0:T(8,128)} %bitcast.25, f32[24,128,512]{2,1,0:T(8,128)} %forward.1.blurred_ref), custom_call_target="tpu_custom_call" | custom-call | flops 1000000 | bytes 6000000 | tf_op jit(solution)/shard_map/ratio/pallas_call | solution.py:166
  226.7 6.4 %ratio.4 = (f32[24,128,128]{2,1,0:T(8,128)}, f32[7,128,128]{2,1,0:T(8,128)}, f32[7,128,128]{2,1,0:T(8,128)}) custom-call(s32[4]{0:T(128)} %pad_add_fusion.scalars, f32[128,24,128]{2,1,0:T(8,128)} %bitcast.6.measured_ref, f32[24,128,512]{2,1,0:T(8,128)} %forward.1.blurred_ref), custom_call_target="tpu_custom_call" | custom-call | flops 1000000 | bytes 6000000 | tf_op jit(solution)/shard_map/ratio/pallas_call | solution.py:166
  233.1 3.0 collective-permute-start.5
  237.1 5.1 %back.4 = (bf16[24,128,128]{2,1,0:T(8,128)(2,1)S(1)}, bf16[24,128,128]{2,1,0:T(8,128)(2,1)S(1)}) custom-call(s32[4]{0:T(128)S(1)} %copy-done.6, f32[15]{0:T(128)S(1)} %bitcast.21, f32[24,128,128]{2,1,0:T(8,128)S(1)} %copy-done.11, f32[7,128,128]{2,1,0:T(8,128)} %collective-permute-done.8.inner, f32[7,128,128]{2,1,0:T(8,128)} %collective-permute-done.9.outer, ...), custom_call_target="tpu_custom_call" | custom-call | flops 5000000000 | bytes 6000000 | tf_op jit(solution)/shard_map/back/pallas_call | solution.py:252
  242.3 2.6 collective-permute-start.3
  244.9 6.2 %back.5 = (bf16[24,128,128]{2,1,0:T(8,128)(2,1)S(1)}, bf16[24,128,128]{2,1,0:T(8,128)(2,1)S(1)}, f32[24,32,128]{2,1,0:T(8,128)S(1)}, f32[24,32,128]{2,1,0:T(8,12...) custom-call(s32[4]{0:T(128)S(1)} %copy-done.6, f32[15]{0:T(128)S(1)} %bitcast.22, ...), custom_call_target="tpu_custom_call" | custom-call | flops 5000000000 | bytes 6000000 | tf_op jit(solution)/shard_map/back/pallas_call | solution.py:252
  255.3 6.1 %back.6 = (bf16[24,128,128]{2,1,0:T(8,128)(2,1)S(1)}, bf16[24,128,128]{2,1,0:T(8,128)(2,1)S(1)}, f32[24,32,128]{2,1,0:T(8,128)S(1)}, f32[24,32,128]{2,1,0:T(8,12...) custom-call(s32[4]{0:T(128)S(1)} %copy-done.6, f32[15]{0:T(128)S(1)} %bitcast.23, ...), custom_call_target="tpu_custom_call" | custom-call | flops 5000000000 | bytes 6000000 | tf_op jit(solution)/shard_map/back/pallas_call | solution.py:252
  265.2 9.0 %back.7 = (bf16[24,128,128]{2,1,0:T(8,128)(2,1)}, bf16[24,128,128]{2,1,0:T(8,128)(2,1)}, f32[24,32,128]{2,1,0:T(8,128)S(1)}, f32[24,32,128]{2,1,0:T(8,128)}, f32...) custom-call(s32[4]{0:T(128)S(1)} %copy-done.6, ...), custom_call_target="tpu_custom_call" | custom-call | flops 5000000000 | bytes 6000000 | tf_op jit(solution)/shard_map/back/pallas_call | solution.py:252
  280.6 2.4 collective-permute-start.18
  283.1 3.1 merge.7.refs_0_
  286.2 3.3 collective-permute-done.23.c
  290.0 2.1 collective-permute-start.11
  292.1 5.5 %collective-permute-done.16.b = f32[24,32,128]{2,1,0:T(8,128)} collective-permute-done((f32[24,32,128]{2,1,0:T(8,128)}, f32[24,32,128]{2,1,0:T(8,128)}, u32[]{:S(2)}, u32[]{:S(2)}) %collective-permute-start.16) | collective-permute-done | bytes 393248 | tf_op jit(solution)/shard_map/ppermute | solution.py:397
  297.6 2.4 collective-permute-start.12
  300.1 6.3 %collective-permute-done.17.c = f32[24,32,128]{2,1,0:T(8,128)S(1)} collective-permute-done((f32[24,32,128]{2,1,0:T(8,128)}, f32[24,32,128]{2,1,0:T(8,128)S(1)}, u32[]{:S(2)}, u32[]{:S(2)}) %collective-permute-start.17) | collective-permute-done | bytes 393248 | tf_op jit(solution)/shard_map/ppermute | solution.py:397
  308.9 3.1 merge.6.refs_0_
  311.9 3.2 merge.5.refs_0_
  316.6 15.0 %collective-permute-done.11.c = f32[24,32,128]{2,1,0:T(8,128)} collective-permute-done((f32[24,32,128]{2,1,0:T(8,128)S(1)}, f32[24,32,128]{2,1,0:T(8,128)}, u32[]{:S(2)}, u32[]{:S(2)}) %collective-permute-start.11) | collective-permute-done | bytes 393248 | tf_op jit(solution)/shard_map/ppermute | solution.py:397
  332.5 1.7 collective-permute-start.26
  335.7 12.8 %collective-permute-done.32.refs_2_ = f32[32,24,128]{2,1,0:T(8,128)S(1)} collective-permute-done((f32[32,24,128]{2,1,0:T(8,128)}, f32[32,24,128]{2,1,0:T(8,128)S(1)}, u32[]{:S(2)}, u32[]{:S(2)}) %collective-permute-start.32) | collective-permute-done | bytes 393248 | tf_op jit(solution)/shard_map/ppermute | solution.py:397
  349.2 3.2 merge.4.refs_0_
  352.5 1.8 collective-permute-start.20
  355.8 9.5 %collective-permute-done.26.refs_2_ = f32[32,24,128]{2,1,0:T(8,128)} collective-permute-done((f32[32,24,128]{2,1,0:T(8,128)S(1)}, f32[32,24,128]{2,1,0:T(8,128)}, u32[]{:S(2)}, u32[]{:S(2)}) %collective-permute-start.26) | collective-permute-done | bytes 393248 | tf_op jit(solution)/shard_map/ppermute | solution.py:397
  366.1 1.7 collective-permute-start.14
  369.4 2.5 assemble.4.refs_4_
  372.0 2.5 assemble.5.refs_4_
  374.5 7.6 %collective-permute-done.20.refs_2_ = f32[32,24,128]{2,1,0:T(8,128)S(1)} collective-permute-done((f32[32,24,128]{2,1,0:T(8,128)S(1)}, f32[32,24,128]{2,1,0:T(8,128)S(1)}, u32[]{:S(2)}, u32[]{:S(2)}) %collective-permute-start.20) | collective-permute-done | bytes 393248 | tf_op jit(solution)/shard_map/ppermute | solution.py:397
  383.6 2.5 assemble.6.refs_4_
  386.2 4.2 %collective-permute-done.14.refs_2_ = f32[32,24,128]{2,1,0:T(8,128)S(1)} collective-permute-done((f32[32,24,128]{2,1,0:T(8,128)}, f32[32,24,128]{2,1,0:T(8,128)S(1)}, u32[]{:S(2)}, u32[]{:S(2)}) %collective-permute-start.14) | collective-permute-done | bytes 393248 | tf_op jit(solution)/shard_map/ppermute | solution.py:397
  391.9 2.5 assemble.7
  (130 shorter events, 37.0 us)
Async XLA Ops:
  89.0 41.4 %all-to-all-start.3 = ((f32[8,16,24,128]{3,2,1,0:T(8,128)}), f32[8,16,24,128]{3,2,1,0:T(8,128)S(1)}, u32[]{:S(2)}, u32[]{:S(2)}) async-start(f32[8,16,24,128]{3,2,1,0:T(8,128)} %get-tuple-element.64), calls=%async_computation.3 | async-start | bytes 3145728 | tf_op jit(solution)/shard_map/all_to_all | solution.py:431
  108.4 29.6 %copy-start.38 = (s32[1,4]{1,0:T(1,128)S(1)}, s32[1,4]{1,0:T(1,128)}, u32[]{:S(2)}) copy-start(s32[1,4]{1,0:T(1,128)} %param.13) | copy-start | bytes 52
  108.4 67.7 %copy-start.7 = (f32[1,15]{1,0:T(1,128)S(1)}, f32[1,15]{1,0:T(1,128)}, u32[]{:S(2)}) copy-start(f32[1,15]{1,0:T(1,128)} %profile_y.1) | copy-start | bytes 184
  108.4 67.7 %collective-permute-start.1 = (f32[7,128,512]{2,1,0:T(8,128)}, f32[7,128,512]{2,1,0:T(8,128)S(1)}, u32[]{:S(2)}, u32[]{:S(2)}) collective-permute-start(f32[7,128,512]{2,1,0:T(8,128)} %get-tuple-element.91), channel_id=1, source_target_pairs={{1,2},{3,4},{5,6},{2,1},{4,3},{6,5},{9,10},{11,12},{13,14},{10,9},... | collective-permute-start | bytes 5505032 | tf_op jit(solution)/shard_map/ppermute | solution.py:415
  110.7 65.3 %collective-permute-start = (f32[7,128,512]{2,1,0:T(8,128)}, f32[7,128,512]{2,1,0:T(8,128)}, u32[]{:S(2)}, u32[]{:S(2)}) collective-permute-start(f32[7,128,512]{2,1,0:T(8,128)} %get-tuple-element.92), channel_id=1, source_target_pairs={{0,1},{1,0},{2,3},{3,2},{4,5},{5,4},{6,7},{7,6},{8,9},{9,8},{10,11... | collective-permute-start | bytes 5505032 | tf_op jit(solution)/shard_map/ppermute | solution.py:415
  130.4 71.0 %copy-start.16 = (f32[8,16,24,128]{3,2,1,0:T(8,128)}, f32[8,16,24,128]{3,2,1,0:T(8,128)S(1)}, u32[]{:S(2)}) copy-start(f32[8,16,24,128]{3,2,1,0:T(8,128)S(1)} %all-to-all-done.3) | copy-start | bytes 4718596
  130.4 96.3 %all-to-all-start = ((f32[8,16,24,128]{3,2,1,0:T(8,128)}), f32[8,16,24,128]{3,2,1,0:T(8,128)}, u32[]{:S(2)}, u32[]{:S(2)}) async-start(f32[8,16,24,128]{3,2,1,0:T(8,128)} %get-tuple-element.48), calls=%async_computation | async-start | bytes 3145728 | tf_op jit(solution)/shard_map/all_to_all | solution.py:431
  201.4 9.5 %copy-start.20 = (bf16[4,256,256]{2,1,0:T(8,128)(2,1)S(1)}, bf16[4,256,256]{2,1,0:T(8,128)(2,1)}, u32[]{:S(2)}) copy-start(bf16[4,256,256]{2,1,0:T(8,128)(2,1)} %get-tuple-element.70) | copy-start | bytes 1572868
  207.8 25.2 %collective-permute-start.8 = (f32[7,128,128]{2,1,0:T(8,128)}, f32[7,128,128]{2,1,0:T(8,128)}, u32[]{:S(2)}, u32[]{:S(2)}) collective-permute-start(f32[7,128,128]{2,1,0:T(8,128)} %get-tuple-element.66), channel_id=1, source_target_pairs={{0,1},{1,0},{2,3},{3,2},{4,5},{5,4},{6,7},{7,6},{8,9},{9,8},{10,11... | collective-permute-start | bytes 1376264 | tf_op jit(solution)/shard_map/ppermute | solution.py:415
  207.8 28.2 %collective-permute-start.9 = (f32[7,128,128]{2,1,0:T(8,128)}, f32[7,128,128]{2,1,0:T(8,128)}, u32[]{:S(2)}, u32[]{:S(2)}) collective-permute-start(f32[7,128,128]{2,1,0:T(8,128)} %get-tuple-element.67), channel_id=1, source_target_pairs={{1,2},{3,4},{5,6},{2,1},{4,3},{6,5},{9,10},{11,12},{13,14},{10,9},... | collective-permute-start | bytes 1376264 | tf_op jit(solution)/shard_map/ppermute | solution.py:415
  217.3 24.9 %collective-permute-start.6 = (f32[7,128,128]{2,1,0:T(8,128)}, f32[7,128,128]{2,1,0:T(8,128)S(1)}, u32[]{:S(2)}, u32[]{:S(2)}) collective-permute-start(f32[7,128,128]{2,1,0:T(8,128)} %get-tuple-element.62), channel_id=1, source_target_pairs={{0,1},{1,0},{2,3},{3,2},{4,5},{5,4},{6,7},{7,6},{8,9},{9,8},{10,11... | collective-permute-start | bytes 1376264 | tf_op jit(solution)/shard_map/ppermute | solution.py:415
  217.3 27.5 %collective-permute-start.7 = (f32[7,128,128]{2,1,0:T(8,128)}, f32[7,128,128]{2,1,0:T(8,128)S(1)}, u32[]{:S(2)}, u32[]{:S(2)}) collective-permute-start(f32[7,128,128]{2,1,0:T(8,128)} %get-tuple-element.63), channel_id=1, source_target_pairs={{1,2},{3,4},{5,6},{2,1},{4,3},{6,5},{9,10},{11,12},{13,14},{10,9},... | collective-permute-start | bytes 1376264 | tf_op jit(solution)/shard_map/ppermute | solution.py:415
  226.2 27.0 %collective-permute-start.4 = (f32[7,128,128]{2,1,0:T(8,128)}, f32[7,128,128]{2,1,0:T(8,128)S(1)}, u32[]{:S(2)}, u32[]{:S(2)}) collective-permute-start(f32[7,128,128]{2,1,0:T(8,128)} %get-tuple-element.58), channel_id=1, source_target_pairs={{0,1},{1,0},{2,3},{3,2},{4,5},{5,4},{6,7},{7,6},{8,9},{9,8},{10,11... | collective-permute-start | bytes 1376264 | tf_op jit(solution)/shard_map/ppermute | solution.py:415
  233.1 21.7 %collective-permute-start.5 = (f32[7,128,128]{2,1,0:T(8,128)}, f32[7,128,128]{2,1,0:T(8,128)S(1)}, u32[]{:S(2)}, u32[]{:S(2)}) collective-permute-start(f32[7,128,128]{2,1,0:T(8,128)} %get-tuple-element.59), channel_id=1, source_target_pairs={{1,2},{3,4},{5,6},{2,1},{4,3},{6,5},{9,10},{11,12},{13,14},{10,9},... | collective-permute-start | bytes 1376264 | tf_op jit(solution)/shard_map/ppermute | solution.py:415
  236.1 26.1 %collective-permute-start.2 = (f32[7,128,128]{2,1,0:T(8,128)}, f32[7,128,128]{2,1,0:T(8,128)S(1)}, u32[]{:S(2)}, u32[]{:S(2)}) collective-permute-start(f32[7,128,128]{2,1,0:T(8,128)} %get-tuple-element.53), channel_id=1, source_target_pairs={{0,1},{1,0},{2,3},{3,2},{4,5},{5,4},{6,7},{7,6},{8,9},{9,8},{10,11... | collective-permute-start | bytes 1376264 | tf_op jit(solution)/shard_map/ppermute | solution.py:415
  242.3 21.4 %collective-permute-start.3 = (f32[7,128,128]{2,1,0:T(8,128)S(1)}, f32[7,128,128]{2,1,0:T(8,128)S(1)}, u32[]{:S(2)}, u32[]{:S(2)}) collective-permute-start(f32[7,128,128]{2,1,0:T(8,128)S(1)} %copy-done.37), channel_id=1, source_target_pairs={{1,2},{3,4},{5,6},{2,1},{4,3},{6,5},{9,10},{11,12},{13,14},{10,9},... | collective-permute-start | bytes 1376264 | tf_op jit(solution)/shard_map/ppermute | solution.py:415
  244.8 10.4 %copy-start.9 = (f32[24,128,128]{2,1,0:T(8,128)S(1)}, f32[24,128,128]{2,1,0:T(8,128)}, u32[]{:S(2)}) copy-start(f32[24,128,128]{2,1,0:T(8,128)} %get-tuple-element.57.own) | copy-start | bytes 4718596
  251.8 24.0 %collective-permute-start.28 = (f32[24,32,128]{2,1,0:T(8,128)S(1)}, f32[24,32,128]{2,1,0:T(8,128)S(1)}, u32[]{:S(2)}, u32[]{:S(2)}) collective-permute-start(f32[24,32,128]{2,1,0:T(8,128)S(1)} %get-tuple-element.88), channel_id=1, source_target_pairs={{0,8},{8,0},{16,24},{24,16},{1,9},{9,1},{17,25},{25,17},{2,10},{10... | collective-permute-start | bytes 1179656 | tf_op jit(solution)/shard_map/ppermute | solution.py:397
  253.2 23.0 %collective-permute-start.29 = (f32[24,32,128]{2,1,0:T(8,128)S(1)}, f32[24,32,128]{2,1,0:T(8,128)S(1)}, u32[]{:S(2)}, u32[]{:S(2)}) collective-permute-start(f32[24,32,128]{2,1,0:T(8,128)S(1)} %get-tuple-element.89), channel_id=1, source_target_pairs={{0,16},{8,24},{16,0},{24,8},{1,17},{9,25},{17,1},{25,9},{2,18},{10... | collective-permute-start | bytes 1179656 | tf_op jit(solution)/shard_map/ppermute | solution.py:397
  254.8 22.9 %collective-permute-start.30 = (f32[24,32,128]{2,1,0:T(8,128)S(1)}, f32[24,32,128]{2,1,0:T(8,128)S(1)}, u32[]{:S(2)}, u32[]{:S(2)}) collective-permute-start(f32[24,32,128]{2,1,0:T(8,128)S(1)} %get-tuple-element.90), channel_id=1, source_target_pairs={{0,24},{8,16},{16,8},{24,0},{1,25},{9,17},{17,9},{25,1},{2,26},{10... | collective-permute-start | bytes 1179656 | tf_op jit(solution)/shard_map/ppermute | solution.py:397
  255.3 9.9 %copy-start.8 = (f32[24,128,128]{2,1,0:T(8,128)S(1)}, f32[24,128,128]{2,1,0:T(8,128)}, u32[]{:S(2)}) copy-start(f32[24,128,128]{2,1,0:T(8,128)} %get-tuple-element.52.own) | copy-start | bytes 4718596
  262.2 18.5 %collective-permute-start.22 = (f32[24,32,128]{2,1,0:T(8,128)S(1)}, f32[24,32,128]{2,1,0:T(8,128)S(1)}, u32[]{:S(2)}, u32[]{:S(2)}) collective-permute-start(f32[24,32,128]{2,1,0:T(8,128)S(1)} %get-tuple-element.84), channel_id=1, source_target_pairs={{0,8},{8,0},{16,24},{24,16},{1,9},{9,1},{17,25},{25,17},{2,10},{10... | collective-permute-start | bytes 1179656 | tf_op jit(solution)/shard_map/ppermute | solution.py:397
  263.6 25.8 %collective-permute-start.23 = (f32[24,32,128]{2,1,0:T(8,128)S(1)}, f32[24,32,128]{2,1,0:T(8,128)}, u32[]{:S(2)}, u32[]{:S(2)}) collective-permute-start(f32[24,32,128]{2,1,0:T(8,128)S(1)} %get-tuple-element.85), channel_id=1, source_target_pairs={{0,16},{8,24},{16,0},{24,8},{1,17},{9,25},{17,1},{25,9},{2,18},{10... | collective-permute-start | bytes 1179656 | tf_op jit(solution)/shard_map/ppermute | solution.py:397
  275.7 14.3 %collective-permute-start.24 = (f32[24,32,128]{2,1,0:T(8,128)S(1)}, f32[24,32,128]{2,1,0:T(8,128)S(1)}, u32[]{:S(2)}, u32[]{:S(2)}) collective-permute-start(f32[24,32,128]{2,1,0:T(8,128)S(1)} %get-tuple-element.86), channel_id=1, source_target_pairs={{0,24},{8,16},{16,8},{24,0},{1,25},{9,17},{17,9},{25,1},{2,26},{10... | collective-permute-start | bytes 1179656 | tf_op jit(solution)/shard_map/ppermute | solution.py:397
  276.2 21.4 %collective-permute-start.16 = (f32[24,32,128]{2,1,0:T(8,128)}, f32[24,32,128]{2,1,0:T(8,128)}, u32[]{:S(2)}, u32[]{:S(2)}) collective-permute-start(f32[24,32,128]{2,1,0:T(8,128)} %get-tuple-element.80), channel_id=1, source_target_pairs={{0,8},{8,0},{16,24},{24,16},{1,9},{9,1},{17,25},{25,17},{2,10},{10... | collective-permute-start | bytes 1179656 | tf_op jit(solution)/shard_map/ppermute | solution.py:397
  277.7 28.7 %collective-permute-start.17 = (f32[24,32,128]{2,1,0:T(8,128)}, f32[24,32,128]{2,1,0:T(8,128)S(1)}, u32[]{:S(2)}, u32[]{:S(2)}) collective-permute-start(f32[24,32,128]{2,1,0:T(8,128)} %get-tuple-element.81), channel_id=1, source_target_pairs={{0,16},{8,24},{16,0},{24,8},{1,17},{9,25},{17,1},{25,9},{2,18},{10... | collective-permute-start | bytes 1179656 | tf_op jit(solution)/shard_map/ppermute | solution.py:397
  280.6 26.6 %collective-permute-start.18 = (f32[24,32,128]{2,1,0:T(8,128)S(1)}, f32[24,32,128]{2,1,0:T(8,128)}, u32[]{:S(2)}, u32[]{:S(2)}) collective-permute-start(f32[24,32,128]{2,1,0:T(8,128)S(1)} %get-tuple-element.82), channel_id=1, source_target_pairs={{0,24},{8,16},{16,8},{24,0},{1,25},{9,17},{17,9},{25,1},{2,26},{10... | collective-permute-start | bytes 1179656 | tf_op jit(solution)/shard_map/ppermute | solution.py:397
  289.4 25.7 %collective-permute-start.10 = (f32[24,32,128]{2,1,0:T(8,128)S(1)}, f32[24,32,128]{2,1,0:T(8,128)S(1)}, u32[]{:S(2)}, u32[]{:S(2)}) collective-permute-start(f32[24,32,128]{2,1,0:T(8,128)S(1)} %get-tuple-element.76), channel_id=1, source_target_pairs={{0,8},{8,0},{16,24},{24,16},{1,9},{9,1},{17,25},{25,17},{2,10},{10... | collective-permute-start | bytes 1179656 | tf_op jit(solution)/shard_map/ppermute | solution.py:397
  290.0 18.8 %copy-start.28 = (f32[24,32,128]{2,1,0:T(8,128)}, f32[24,32,128]{2,1,0:T(8,128)S(1)}, u32[]{:S(2)}) copy-start(f32[24,32,128]{2,1,0:T(8,128)S(1)} %collective-permute-done.24.d) | copy-start | bytes 1179652
  290.0 41.5 %collective-permute-start.11 = (f32[24,32,128]{2,1,0:T(8,128)S(1)}, f32[24,32,128]{2,1,0:T(8,128)}, u32[]{:S(2)}, u32[]{:S(2)}) collective-permute-start(f32[24,32,128]{2,1,0:T(8,128)S(1)} %get-tuple-element.77), channel_id=1, source_target_pairs={{0,16},{8,24},{16,0},{24,8},{1,17},{9,25},{17,1},{25,9},{2,18},{10... | collective-permute-start | bytes 1179656 | tf_op jit(solution)/shard_map/ppermute | solution.py:397
  297.6 34.9 %collective-permute-start.12 = (f32[24,32,128]{2,1,0:T(8,128)S(1)}, f32[24,32,128]{2,1,0:T(8,128)}, u32[]{:S(2)}, u32[]{:S(2)}) collective-permute-start(f32[24,32,128]{2,1,0:T(8,128)S(1)} %get-tuple-element.78), channel_id=1, source_target_pairs={{0,24},{8,16},{16,8},{24,0},{1,25},{9,17},{17,9},{25,1},{2,26},{10... | collective-permute-start | bytes 1179656 | tf_op jit(solution)/shard_map/ppermute | solution.py:397
  306.4 27.8 %collective-permute-start.33 = (f32[32,24,128]{2,1,0:T(8,128)}, f32[32,24,128]{2,1,0:T(8,128)S(1)}, u32[]{:S(2)}, u32[]{:S(2)}) collective-permute-start(f32[32,24,128]{2,1,0:T(8,128)} %merge.7.refs_0_), channel_id=1, source_target_pairs={{0,24},{8,16},{16,8},{24,0},{1,25},{9,17},{17,9},{25,1},{2,26},{10... | collective-permute-start | bytes 1179656 | tf_op jit(solution)/shard_map/ppermute | solution.py:397
  307.2 41.3 %collective-permute-start.32 = (f32[32,24,128]{2,1,0:T(8,128)}, f32[32,24,128]{2,1,0:T(8,128)S(1)}, u32[]{:S(2)}, u32[]{:S(2)}) collective-permute-start(f32[32,24,128]{2,1,0:T(8,128)} %merge.7.refs_0_), channel_id=1, source_target_pairs={{0,16},{8,24},{16,0},{24,8},{1,17},{9,25},{17,1},{25,9},{2,18},{10... | collective-permute-start | bytes 1179656 | tf_op jit(solution)/shard_map/ppermute | solution.py:397
  311.9 19.7 %copy-start.19 = (f32[32,24,128]{2,1,0:T(8,128)S(1)}, f32[32,24,128]{2,1,0:T(8,128)}, u32[]{:S(2)}) copy-start(f32[32,24,128]{2,1,0:T(8,128)} %merge.6.refs_0_) | copy-start | bytes 1179652
  315.1 34.1 %copy-start.27 = (f32[24,32,128]{2,1,0:T(8,128)}, f32[24,32,128]{2,1,0:T(8,128)S(1)}, u32[]{:S(2)}) copy-start(f32[24,32,128]{2,1,0:T(8,128)S(1)} %collective-permute-done.10.b) | copy-start | bytes 1179652
  315.1 37.3 %collective-permute-start.31 = (f32[32,24,128]{2,1,0:T(8,128)S(1)}, f32[32,24,128]{2,1,0:T(8,128)S(1)}, u32[]{:S(2)}, u32[]{:S(2)}) collective-permute-start(f32[32,24,128]{2,1,0:T(8,128)S(1)} %copy-done.17), channel_id=1, source_target_pairs={{0,8},{8,0},{16,24},{24,16},{1,9},{9,1},{17,25},{25,17},{2,10},{10... | collective-permute-start | bytes 1179656 | tf_op jit(solution)/shard_map/ppermute | solution.py:397
  331.6 22.6 %collective-permute-start.27 = (f32[32,24,128]{2,1,0:T(8,128)S(1)}, f32[32,24,128]{2,1,0:T(8,128)S(1)}, u32[]{:S(2)}, u32[]{:S(2)}) collective-permute-start(f32[32,24,128]{2,1,0:T(8,128)S(1)} %copy-done.19), channel_id=1, source_target_pairs={{0,24},{8,16},{16,8},{24,0},{1,25},{9,17},{17,9},{25,1},{2,26},{10... | collective-permute-start | bytes 1179656 | tf_op jit(solution)/shard_map/ppermute | solution.py:397
  332.5 32.7 %collective-permute-start.26 = (f32[32,24,128]{2,1,0:T(8,128)S(1)}, f32[32,24,128]{2,1,0:T(8,128)}, u32[]{:S(2)}, u32[]{:S(2)}) collective-permute-start(f32[32,24,128]{2,1,0:T(8,128)S(1)} %copy-done.19), channel_id=1, source_target_pairs={{0,16},{8,24},{16,0},{24,8},{1,17},{9,25},{17,1},{25,9},{2,18},{10... | collective-permute-start | bytes 1179656 | tf_op jit(solution)/shard_map/ppermute | solution.py:397
  334.2 18.2 %copy-start.24 = (f32[32,24,128]{2,1,0:T(8,128)}, f32[32,24,128]{2,1,0:T(8,128)S(1)}, u32[]{:S(2)}) copy-start(f32[32,24,128]{2,1,0:T(8,128)S(1)} %collective-permute-done.33.refs_3_) | copy-start | bytes 1179652
  334.2 31.9 %collective-permute-start.25 = (f32[32,24,128]{2,1,0:T(8,128)S(1)}, f32[32,24,128]{2,1,0:T(8,128)}, u32[]{:S(2)}, u32[]{:S(2)}) collective-permute-start(f32[32,24,128]{2,1,0:T(8,128)S(1)} %copy-done.19), channel_id=1, source_target_pairs={{0,8},{8,0},{16,24},{24,16},{1,9},{9,1},{17,25},{25,17},{2,10},{10... | collective-permute-start | bytes 1179656 | tf_op jit(solution)/shard_map/ppermute | solution.py:397
  348.5 19.3 %collective-permute-start.21 = (f32[32,24,128]{2,1,0:T(8,128)}, f32[32,24,128]{2,1,0:T(8,128)}, u32[]{:S(2)}, u32[]{:S(2)}) collective-permute-start(f32[32,24,128]{2,1,0:T(8,128)} %merge.5.refs_0_), channel_id=1, source_target_pairs={{0,24},{8,16},{16,8},{24,0},{1,25},{9,17},{17,9},{25,1},{2,26},{10... | collective-permute-start | bytes 1179656 | tf_op jit(solution)/shard_map/ppermute | solution.py:397
  352.4 17.0 %copy-start.29 = (f32[32,24,128]{2,1,0:T(8,128)}, f32[32,24,128]{2,1,0:T(8,128)S(1)}, u32[]{:S(2)}) copy-start(f32[32,24,128]{2,1,0:T(8,128)S(1)} %collective-permute-done.31.refs_1_) | copy-start | bytes 1179652
  352.5 29.7 %collective-permute-start.20 = (f32[32,24,128]{2,1,0:T(8,128)S(1)}, f32[32,24,128]{2,1,0:T(8,128)S(1)}, u32[]{:S(2)}, u32[]{:S(2)}) collective-permute-start(f32[32,24,128]{2,1,0:T(8,128)S(1)} %copy-done.18), channel_id=1, source_target_pairs={{0,16},{8,24},{16,0},{24,8},{1,17},{9,25},{17,1},{25,9},{2,18},{10... | collective-permute-start | bytes 1179656 | tf_op jit(solution)/shard_map/ppermute | solution.py:397
  354.2 17.7 %copy-start.30 = (f32[32,24,128]{2,1,0:T(8,128)}, f32[32,24,128]{2,1,0:T(8,128)S(1)}, u32[]{:S(2)}) copy-start(f32[32,24,128]{2,1,0:T(8,128)S(1)} %collective-permute-done.27.refs_3_) | copy-start | bytes 1179652
  354.2 27.9 %collective-permute-start.19 = (f32[32,24,128]{2,1,0:T(8,128)S(1)}, f32[32,24,128]{2,1,0:T(8,128)S(1)}, u32[]{:S(2)}, u32[]{:S(2)}) collective-permute-start(f32[32,24,128]{2,1,0:T(8,128)S(1)} %copy-done.18), channel_id=1, source_target_pairs={{0,8},{8,0},{16,24},{24,16},{1,9},{9,1},{17,25},{25,17},{2,10},{10... | collective-permute-start | bytes 1179656 | tf_op jit(solution)/shard_map/ppermute | solution.py:397
  365.3 20.9 %collective-permute-start.15 = (f32[32,24,128]{2,1,0:T(8,128)}, f32[32,24,128]{2,1,0:T(8,128)S(1)}, u32[]{:S(2)}, u32[]{:S(2)}) collective-permute-start(f32[32,24,128]{2,1,0:T(8,128)} %merge.4.refs_0_), channel_id=1, source_target_pairs={{0,24},{8,16},{16,8},{24,0},{1,25},{9,17},{17,9},{25,1},{2,26},{10... | collective-permute-start | bytes 1179656 | tf_op jit(solution)/shard_map/ppermute | solution.py:397
  366.1 24.3 %collective-permute-start.14 = (f32[32,24,128]{2,1,0:T(8,128)}, f32[32,24,128]{2,1,0:T(8,128)S(1)}, u32[]{:S(2)}, u32[]{:S(2)}) collective-permute-start(f32[32,24,128]{2,1,0:T(8,128)} %merge.4.refs_0_), channel_id=1, source_target_pairs={{0,16},{8,24},{16,0},{24,8},{1,17},{9,25},{17,1},{25,9},{2,18},{10... | collective-permute-start | bytes 1179656 | tf_op jit(solution)/shard_map/ppermute | solution.py:397
  367.9 22.5 %collective-permute-start.13 = (f32[32,24,128]{2,1,0:T(8,128)}, f32[32,24,128]{2,1,0:T(8,128)S(1)}, u32[]{:S(2)}, u32[]{:S(2)}) collective-permute-start(f32[32,24,128]{2,1,0:T(8,128)} %merge.4.refs_0_), channel_id=1, source_target_pairs={{0,8},{8,0},{16,24},{24,16},{1,9},{9,1},{17,25},{25,17},{2,10},{10... | collective-permute-start | bytes 1179656 | tf_op jit(solution)/shard_map/ppermute | solution.py:397
  (27 other events, 87.3 us)

commit v2 on v1

v2 whole, which is shorter than its diff:
```python
import functools

import jax
import jax.numpy as jnp
from jax import lax
from jax.experimental import pallas as pl
from jax.experimental.pallas import tpu as pltpu
from jax.sharding import PartitionSpec as P

LANES = 128
SLOT = 8
VMEM_MIB = 56
F32 = jnp.float32
BF16 = jnp.bfloat16
SMEM = pl.BlockSpec(memory_space=pltpu.SMEM)
VMEM = pl.BlockSpec(memory_space=pltpu.VMEM)
ANY = pl.BlockSpec(memory_space=pl.ANY)


MICROS = dict(prep=9, edge_rows=5, swap=8, swap_edges=6, gate=1, forward=30, ratio=5, back=60, bands=4, merge=30, assemble=10)


def cost(name):
    micros = MICROS[name]
    return pl.CostEstimate(flops=int(micros * 1.1e9), bytes_accessed=int(micros * 3.6e6), transcendentals=0)


def sds(shape, dtype=F32):
    return jax.ShapeDtypeStruct(shape, dtype)


def params():
    return pltpu.CompilerParams(vmem_limit_bytes=VMEM_MIB << 20)


def split(value):
    high = value.astype(BF16)
    return high, (value - high.astype(F32)).astype(BF16)


def dot(a, b):
    return jnp.dot(a, b, preferred_element_type=F32)


def pack(rows):
    lane = lax.broadcasted_iota(jnp.int32, rows[0].shape, 1)
    total = jnp.zeros(rows[0].shape, F32)
    for slot, row in enumerate(rows):
        moved = pltpu.roll(row, (SLOT * slot + SLOT) % LANES, 1)
        total = jnp.where((lane >= SLOT * slot) & (lane < SLOT * slot + SLOT), moved, total)
    return total


def unpack(packed, slot):
    lane = lax.broadcasted_iota(jnp.int32, packed.shape, 1)
    moved = pltpu.roll(packed, (2 * LANES - SLOT - SLOT * slot) % LANES, 1)
    return jnp.where(lane >= LANES - SLOT, moved, 0.0)


def prep_kernel(lead, groups, offsets, stack_ref, after, *out_refs):
    *out_refs, token_ref = out_refs
    token_ref[...] = jnp.zeros(token_ref.shape, F32)
    planes, rows, cells = stack_ref.shape
    offset = offsets[0]
    lane = lax.broadcasted_iota(jnp.int32, (1, 1, cells), 2)
    column = lane + lead
    column = jnp.where(column >= cells, column - cells, column)
    source = column + offset
    inside = (source >= 0) & (source < cells)
    shift = lax.rem(2 * cells - lead - offset, cells)
    rolled = pltpu.roll(stack_ref[...].reshape(planes * rows, cells), shift, 1)
    rolled = jnp.where(inside, rolled.reshape(planes, rows, cells), 0.0)
    size = planes * rows
    for group, out_ref in zip(groups, out_refs):
        for number, chunk in enumerate(group):
            values = rolled[:, :, chunk * LANES : (chunk + 1) * LANES]
            out_ref[0, number * size : (number + 1) * size] = values.reshape(size, LANES)
    tail = rolled[:, :, cells - LANES :]
    per = LANES // SLOT
    for number in range(pl.cdiv(rows, per)):
        at = len(groups[0]) * size + number * planes
        members = range(number * per, min((number + 1) * per, rows))
        out_refs[0][0, at : at + planes] = pack([tail[:, r, :] for r in members])


def prep(offsets, stack, tiles, lead, groups, after):
    planes, all_rows, cells = stack.shape
    rows = all_rows // tiles
    sizes = [len(group) * planes * rows for group in groups]
    sizes[0] += planes * pl.cdiv(rows, LANES // SLOT)
    return pl.pallas_call(
        functools.partial(prep_kernel, lead, groups),
        grid=(tiles,),
        in_specs=[SMEM, pl.BlockSpec((planes, rows, cells), lambda i: (0, i, 0)), ANY],
        out_specs=[pl.BlockSpec((1, size, LANES), lambda i: (i, 0, 0)) for size in sizes]
        + [pl.BlockSpec((8, LANES), lambda i: (0, 0))],
        out_shape=[sds((tiles, size, LANES)) for size in sizes] + [sds((8, LANES))],
        compiler_params=params(),
        cost_estimate=cost("prep"),
        name="prep",
    )(offsets, stack, after)


def copy_kernel(scalars, first_ref, second_ref, inner_ref, outer_ref):
    inner_ref[...] = first_ref[...]

    @pl.when(pl.program_id(0) == 0)
    def _():
        outer_ref[...] = second_ref[...]


def edge_rows(places, cells):
    planes, rows, width = cells.shape
    last = rows // 8 - 1
    step = planes // 4
    return pl.pallas_call(
        copy_kernel,
        grid_spec=pltpu.PrefetchScalarGridSpec(
            num_scalar_prefetch=1,
            grid=(planes // step,),
            in_specs=[
                pl.BlockSpec((step, 8, width), lambda i, s: (i, s[0] * last, 0)),
                pl.BlockSpec((step, 8, width), lambda i, s: (s[1], (1 - s[0]) * last, 0)),
            ],
            out_specs=[
                pl.BlockSpec((step, 8, width), lambda i, s: (i, 0, 0)),
                pl.BlockSpec((step, 8, width), lambda i, s: (0, 0, 0)),
            ],
        ),
        out_shape=[sds((planes, 8, width)), sds((step, 8, width))],
        compiler_params=params(),
        cost_estimate=cost("edge_rows"),
        name="edge_rows",
    )(places, cells, cells)


def swap_kernel(in_ref, after, out_ref):
    out_ref[...] = jnp.swapaxes(in_ref[...], 0, 1)


def swap(cells, after):
    planes, rows, width = cells.shape
    return pl.pallas_call(
        swap_kernel,
        grid=(planes // 16,),
        in_specs=[pl.BlockSpec((16, rows, width), lambda i: (i, 0, 0)), ANY],
        out_specs=pl.BlockSpec((rows, 16, width), lambda i: (0, i, 0)),
        out_shape=sds((rows, planes, width)),
        compiler_params=params(),
        cost_estimate=cost("swap"),
        name="swap",
    )(cells, after)


def swap_edges_kernel(half, scalars, inner_ref, a, b, c, d, after, inner_out, outer_out):
    even = scalars[0]
    inner = jnp.swapaxes(inner_ref[...], 0, 1)
    skip = inner.shape[0] - half
    inner_out[...] = jnp.where(even == 1, inner[:half], inner[skip:])
    for k, piece in enumerate((a, b, c, d)):

        @pl.when(pl.program_id(0) == k)
        def _():
            outer = jnp.swapaxes(piece[...], 0, 1)
            outer_out[...] = jnp.where(even == 1, outer[skip:], outer[:half])


def swap_edges(places, inner, pieces, half, after):
    planes, rows, width = inner.shape
    step = planes // 4
    return pl.pallas_call(
        functools.partial(swap_edges_kernel, half),
        grid_spec=pltpu.PrefetchScalarGridSpec(
            num_scalar_prefetch=1,
            grid=(4,),
            in_specs=[pl.BlockSpec((step, rows, width), lambda i, s: (s[1] ^ i, 0, 0))]
            + [pl.BlockSpec((step, rows, width), lambda i, s: (0, 0, 0))] * 4
            + [ANY],
            out_specs=[pl.BlockSpec((half, step, width), lambda i, s: (0, s[1] ^ i, 0))] * 2,
        ),
        out_shape=[sds((half, planes, width))] * 2,
        compiler_params=params(),
        cost_estimate=cost("swap_edges"),
        name="swap_edges",
    )(places, inner, *pieces, after)


def gate_kernel(*refs):
    pass


def gate(arrays, after):
    count = len(arrays)
    return pl.pallas_call(
        gate_kernel,
        in_specs=[ANY] * (count + len(after)),
        out_specs=[ANY] * count,
        out_shape=[sds(array.shape) for array in arrays],
        input_output_aliases={i: i for i in range(count)},
        compiler_params=params(),
        cost_estimate=cost("gate"),
        name="gate",
    )(*arrays, *after)


def place_rows(even, own, inner, outer, edges_at, buffer, sems, half):
    rows, planes, _ = own.shape
    blocks = sems.shape[1]
    step = planes // blocks
    inner_at = jnp.where(even == 1, half + rows, 0)
    outer_at = jnp.where(even == 1, 0, half + rows)
    copies = []
    for block in range(blocks):
        at = pl.ds(block * step, step)
        edge = pl.ds(edges_at, half)
        copies.append(
            [
                pltpu.make_async_copy(own.at[:, at], buffer.at[pl.ds(half, rows), at], sems.at[0, block]),
                pltpu.make_async_copy(inner.at[edge, at], buffer.at[pl.ds(inner_at, half), at], sems.at[1, block]),
                pltpu.make_async_copy(outer.at[edge, at], buffer.at[pl.ds(outer_at, half), at], sems.at[2, block]),
            ]
        )
    return copies


def start_all(copies):
    for copy in copies:
        copy.start()


def wait_all(copies):
    for copy in copies:
        copy.wait()


def blur_y(buffer, weights, taps, rows, planes_at, lanes_at):
    at = (pl.ds(planes_at, 16), pl.ds(lanes_at, LANES))
    cells = [buffer[(r, *at)] for r in range(rows + taps - 1)]
    for r in range(rows):
        total = weights[0] * cells[r]
        for tap in range(1, taps):
            total = total + weights[tap] * cells[r + tap]
        yield r, split(total)


def forward_kernel(taps, scalars, weights, own, inner, outer, along_z, high_x, low_x, after, out_ref, buffer, halves, sems):
    rows, planes, cells = own.shape
    half = (taps - 1) // 2
    blocks = place_rows(scalars[0], own, inner, outer, 0, buffer, sems, half)
    for copies in blocks:
        start_all(copies)
    step = planes // len(blocks)
    for block, copies in enumerate(blocks):
        wait_all(copies)

        def step_y(index, carry):
            planes_at = pl.multiple_of(block * step + (index // (cells // LANES)) * 16, 16)
            lanes_at = pl.multiple_of((index % (cells // LANES)) * LANES, LANES)
            for r, (high, low) in blur_y(buffer, weights, taps, rows, planes_at, lanes_at):
                halves[r, pl.ds(planes_at, 16), pl.ds(lanes_at, LANES)] = high
                halves[r, pl.ds(planes + planes_at, 16), pl.ds(lanes_at, LANES)] = low
            return carry

        lax.fori_loop(0, (step // 16) * (cells // LANES), step_y, 0)
    group = 4

    def step_zx(index, carry):
        parts = []
        for g in range(group):
            both = dot(along_z[...], halves[index * group + g])
            parts.append(both[:planes] + both[planes:])
        high, low = split(jnp.concatenate(parts, axis=0))
        result = dot(high, high_x[...]) + dot(low, high_x[...]) + dot(high, low_x[...])
        out_ref[pl.ds(index * group, group)] = result.reshape(group, planes, cells)
        return carry

    lax.fori_loop(0, rows // group, step_zx, 0)


def forward(even, weights, own, inner, outer, along_z, high_x, low_x, after):
    rows, planes, cells = own.shape
    taps = weights.shape[0]
    return pl.pallas_call(
        functools.partial(forward_kernel, taps),
        in_specs=[SMEM, SMEM, ANY, ANY, ANY, VMEM, VMEM, VMEM, ANY],
        out_specs=VMEM,
        out_shape=sds((rows, planes, cells)),
        scratch_shapes=[
            pltpu.VMEM((rows + taps - 1, planes, cells), F32),
            pltpu.VMEM((rows, 2 * planes, cells), BF16),
            pltpu.SemaphoreType.DMA((3, 4)),
        ],
        compiler_params=params(),
        cost_estimate=cost("forward"),
        name="forward",
    )(even, weights, own, inner, outer, along_z, high_x, low_x, after)


def edges_of(cells, half):
    return cells[:half], cells[cells.shape[0] - half :]


def ratio_kernel(half, chunks, first, scalars, moved_ref, *refs):
    count = len(chunks)
    blurred_refs, refs = refs[:count], refs[count:]
    if first:
        tail_ref, _, *refs = refs
        tail_out, packed = refs[count + 2 :]
    else:
        _, *refs = refs
    out_refs = refs[:count]
    inner_ref, outer_ref = refs[count : count + 2]
    rows, planes, _ = out_refs[0].shape
    tiles = moved_ref.shape[0]
    slab = planes // tiles
    size = slab * rows
    even = scalars[0]
    step = max(16, slab)
    for number, (blurred_ref, out_ref) in enumerate(zip(blurred_refs, out_refs)):
        edge = slice(number * half, (number + 1) * half)
        for at in range(0, planes, step):
            cells = [
                moved_ref[i, number * size : (number + 1) * size].reshape(slab, rows, LANES)
                for i in range(at // slab, (at + step) // slab)
            ]
            cells = cells[0] if len(cells) == 1 else jnp.concatenate(cells, axis=0)
            cells = jnp.swapaxes(cells, 0, 1) / blurred_ref[:, at : at + step]
            out_ref[:, at : at + step] = cells
            low, high = cells[:half], cells[rows - half :]
            inner_ref[edge, at : at + step] = jnp.where(even == 1, high, low)
            outer_ref[edge, at : at + step] = jnp.where(even == 1, low, high)
    if first:
        for number in range(packed.shape[0]):
            for source in range(tiles):
                at = count * size + number * slab
                packed[number, source * slab : (source + 1) * slab] = moved_ref[source, at : at + slab]
        per = LANES // SLOT
        values = []
        for r in range(rows):
            value = unpack(packed[r // per], r % per) / tail_ref[r]
            tail_out[r] = value
            if r < half or r >= rows - half:
                values.append(value)
        low, high = pack(values[:half]), pack(values[half:])
        inner_ref[count * half] = jnp.where(even == 1, high, low)
        outer_ref[count * half] = jnp.where(even == 1, low, high)


def ratio(scalars, moved, blurred, half, chunks, after):
    rows, planes, cells = blurred.shape
    first = 0 in chunks
    count = len(chunks)

    def column(block):
        return pl.BlockSpec((rows, planes, LANES), lambda i: (0, 0, block))

    edge = sds((half * count + (1 if first else 0), planes, LANES))
    whole = sds((rows, planes, LANES))
    outs = [whole] * count + [edge, edge] + ([whole] if first else [])
    columns = list(chunks) + ([cells // LANES - 1] if first else [])
    outs = pl.pallas_call(
        functools.partial(ratio_kernel, half, chunks, first),
        grid=(1,),
        in_specs=[SMEM, pl.BlockSpec(moved.shape, lambda i: (0, 0, 0))]
        + [column(block) for block in columns]
        + [ANY],
        out_specs=[pl.BlockSpec(out.shape, lambda i: (0, 0, 0)) for out in outs],
        out_shape=outs,
        scratch_shapes=[pltpu.VMEM((pl.cdiv(rows, LANES // SLOT), planes, LANES), F32)] if first else [],
        compiler_params=params(),
        cost_estimate=cost("ratio"),
        name="ratio",
    )(scalars, moved, *[blurred] * len(columns), after)
    return outs[:count], outs[count], outs[count + 1], outs[count + 2 :]


def back_kernel(taps, count, first, scalars, weights, inner, outer, along_z, along_x, *refs):
    owns, refs = refs[:count], refs[count:]
    tail, refs = (refs[0], refs[1:]) if first else (None, refs)
    before, refs = (None, refs) if first else (refs[:2], refs[2:])
    _, *refs = refs
    high_out, low_out, *quarters = refs[:6]
    buffers, halves, yz_high, yz_low, totals, sems, out_sems, spare, spare_sems = refs[6:]
    rows, planes, _ = owns[0].shape
    half = (taps - 1) // 2
    even = scalars[0]
    group = 4

    def blur_rows(buffer, planes_from, planes_count):
        def step_y(index, carry):
            planes_at = pl.multiple_of(planes_from + index * 16, 16)
            for r, (high, low) in blur_y(buffer, weights, taps, rows, planes_at, 0):
                lanes = slice((r % 2) * LANES, (r % 2 + 1) * LANES)
                halves[r // 2, pl.ds(planes_at, 16), lanes] = high
                halves[r // 2, pl.ds(planes + planes_at, 16), lanes] = low
            return carry

        lax.fori_loop(0, planes_count // 16, step_y, 0)

    def blur_planes(slot, number):
        def step_zx(index, carry):
            parts = []
            for g in range(group // 2):
                both = dot(along_z[...], halves[index * (group // 2) + g])
                both = both[:planes] + both[planes:]
                parts += [both[:, :LANES], both[:, LANES:]]
            mine = split(jnp.concatenate(parts, axis=0))
            at = pl.ds(index * group, group)
            for value, keep, last in zip(mine, (yz_high, yz_low), (high_out, low_out)):
                value = value.reshape(group, planes, LANES)
                if number == count - 1:
                    last[at] = value
                else:
                    keep[slot, at] = value
            if number >= 0:
                others = [before[0][at], before[1][at]] if slot is None else [yz_high[slot ^ 1, at], yz_low[slot ^ 1, at]]
                result = 0.0
                for own, other in zip(mine, others):
                    pair = jnp.concatenate([other.reshape(-1, LANES), own], axis=1)
                    result = result + dot(pair, along_x[number])
                result = result[:, :LANES] + result[:, LANES:]
                totals[pl.ds(number * rows + index * group, group)] = result.reshape(group, planes, LANES)
            return carry

        lax.fori_loop(0, rows // group, step_zx, 0)

    loads = [
        place_rows(even, own, inner, outer, number * half, buffers.at[number], sems.at[number], half)
        for number, own in enumerate(owns)
    ]
    if first:
        inner_at = jnp.where(even == 1, half + rows, 0)
        outer_at = jnp.where(even == 1, 0, half + rows)
        tail_loads = [
            pltpu.make_async_copy(tail, buffers.at[count, pl.ds(half, rows)], spare_sems.at[0]),
            pltpu.make_async_copy(inner.at[count * half], spare.at[0], spare_sems.at[1]),
            pltpu.make_async_copy(outer.at[count * half], spare.at[1], spare_sems.at[2]),
        ]
        start_all(tail_loads)
    for load in loads:
        for copies in load:
            start_all(copies)
    if first:
        wait_all(tail_loads)
        for number, at in enumerate((inner_at, outer_at)):
            for r in range(half):
                buffers[count, at + r] = unpack(spare[number], r)
        blur_rows(buffers.at[count], 0, planes)
        blur_planes(0, -1)
    size = planes // 4
    stores = []
    for number, load in enumerate(loads):
        step = planes // len(load)
        for block, copies in enumerate(load):
            wait_all(copies)
            blur_rows(buffers.at[number], block * step, step)
        blur_planes((number + 1) % 2 if first else None, number)
        for k, quarter in enumerate(quarters):
            start = pl.multiple_of((scalars[1] ^ k) * size, size)
            at = pl.ds(number * rows, rows)
            stores.append(
                pltpu.make_async_copy(totals.at[at, pl.ds(start, size)], quarter.at[at], out_sems.at[number, k])
            )
        start_all(stores[-4:])
    wait_all(stores)


def back(scalars, weights, owns, tail, inner, outer, along_z, along_x, before, chunks, after):
    rows, planes, _ = owns[0].shape
    taps = weights.shape[0]
    count = len(chunks)
    first = before is None
    square = pl.BlockSpec((count, 2 * LANES, 2 * LANES), lambda i: (chunks[0] // count, 0, 0))
    outs = pl.pallas_call(
        functools.partial(back_kernel, taps, count, first),
        grid=(1,),
        in_specs=[SMEM, SMEM, ANY, ANY, VMEM, square]
        + [ANY] * count
        + ([ANY] if first else [VMEM, VMEM])
        + [ANY],
        out_specs=[VMEM] * 2 + [ANY] * 4,
        out_shape=[sds((rows, planes, LANES), BF16)] * 2 + [sds((count * rows, planes // 4, LANES))] * 4,
        scratch_shapes=[
            pltpu.VMEM((count + (1 if first else 0), rows + taps - 1, planes, LANES), F32),
            pltpu.VMEM((rows // 2, 2 * planes, 2 * LANES), BF16),
            pltpu.VMEM((2, rows, planes, LANES), BF16),
            pltpu.VMEM((2, rows, planes, LANES), BF16),
            pltpu.VMEM((count * rows, planes, LANES), F32),
            pltpu.SemaphoreType.DMA((count, 3, 4)),
            pltpu.SemaphoreType.DMA((count, 4)),
            pltpu.VMEM((2, planes, LANES), F32),
            pltpu.SemaphoreType.DMA((3,)),
        ],
        compiler_params=params(),
        cost_estimate=cost("back"),
        name="back",
    )(
        scalars, weights, inner, outer, along_z, along_x, *owns, *(tail if first else before), after
    )
    return outs[:2], outs[2:]


def merge_kernel(count, scalars, estimate_ref, a, b, c, d, after, out_ref):
    step, rows, _ = estimate_ref.shape
    total = (a[...] + b[...]) + (c[...] + d[...])
    views = scalars[2].astype(F32)
    for number in range(count):
        lanes = slice(number * LANES, (number + 1) * LANES)
        mine = jnp.swapaxes(total[number * rows : (number + 1) * rows], 0, 1)
        out_ref[:, :, lanes] = estimate_ref[:, :, lanes] * mine / views


def merge(scalars, estimate, parts, chunks, after):
    _, size, _ = parts[0].shape
    rows = estimate.shape[1]
    count = len(chunks)
    step = 16
    steps = size // step
    piece = pl.BlockSpec((count * rows, step, LANES), lambda i, s: (0, i, 0))
    block = chunks[0] // count
    return pl.pallas_call(
        functools.partial(merge_kernel, count),
        grid_spec=pltpu.PrefetchScalarGridSpec(
            num_scalar_prefetch=1,
            grid=(steps,),
            in_specs=[
                pl.BlockSpec((step, rows, count * LANES), lambda i, s: (s[1] * steps + i, 0, block))
            ]
            + [piece] * 4
            + [ANY],
            out_specs=pl.BlockSpec((step, rows, count * LANES), lambda i, s: (i, 0, 0)),
        ),
        out_shape=sds((size, rows, count * LANES)),
        compiler_params=params(),
        cost_estimate=cost("merge"),
        name="merge",
    )(scalars, estimate, *parts, after)


def assemble_kernel(count, cells_at, scalars, *refs):
    pieces, out_ref, sems = refs[:count], refs[-2], refs[-1]
    size, _, width = pieces[0].shape
    copies = []
    for k, piece in enumerate(pieces):
        start = 0 if count == 1 else (scalars[1] ^ k) * size
        copies.append(
            pltpu.make_async_copy(
                piece, out_ref.at[pl.ds(start, size), :, pl.ds(cells_at, width)], sems.at[k]
            )
        )
    start_all(copies)
    wait_all(copies)


def assemble(scalars, pieces, shape, cells_at, result, after):
    earlier = [] if result is None else [result]
    count = len(pieces)
    return pl.pallas_call(
        functools.partial(assemble_kernel, count, cells_at),
        in_specs=[SMEM] + [VMEM] * count + [ANY] * (len(earlier) + 1),
        out_specs=ANY,
        out_shape=sds(shape),
        scratch_shapes=[pltpu.SemaphoreType.DMA((count,))],
        input_output_aliases={} if result is None else {count + 1: 0},
        compiler_params=params(),
        cost_estimate=cost("assemble"),
        name="assemble",
    )(scalars, *pieces, *earlier, after)


def taps_at(distance, profile):
    result = jnp.zeros(distance.shape, F32)
    for tap in range(profile.shape[1]):
        result = jnp.where(distance == tap, profile[0, tap], result)
    return result


def total_of(profile):
    total = profile[0, 0]
    for tap in range(1, profile.shape[1]):
        total = total + profile[0, tap]
    return total


def bands_kernel(scalars, profile_z, profile_y, profile_x, after, forward_z, back_z, high_x, low_x, back_x):
    planes = forward_z.shape[0] // 2
    cells = high_x.shape[0]
    half_z = (profile_z.shape[1] - 1) // 2
    lead = (profile_x.shape[1] - 1) // 2
    total_z, total_y, total_x = total_of(profile_z), total_of(profile_y), total_of(profile_x)
    row = lax.broadcasted_iota(jnp.int32, (planes, planes), 0)
    column = lax.broadcasted_iota(jnp.int32, (planes, planes), 1)
    for out, distance in ((forward_z, column - row), (back_z, row - column)):
        high, low = split(taps_at(distance + half_z, profile_z) / total_z / total_y)
        for side in (slice(0, planes), slice(planes, 2 * planes)):
            out[:planes, side] = high
            out[planes:, side] = low

    step = 32

    def step_x(index, carry):
        at = pl.multiple_of(index * step, step)
        row = lax.broadcasted_iota(jnp.int32, (step, cells), 0) + at
        column = lax.broadcasted_iota(jnp.int32, (step, cells), 1) + lead
        column = jnp.where(column >= cells, column - cells, column)
        high, low = split(taps_at(row - column + lead, profile_x) / total_x)
        high_x[pl.ds(at, step), :] = high
        low_x[pl.ds(at, step), :] = low
        return carry

    lax.fori_loop(0, cells // step, step_x, 0)
    row = lax.broadcasted_iota(jnp.int32, (2 * LANES, LANES), 0)
    column = lax.broadcasted_iota(jnp.int32, (2 * LANES, LANES), 1)
    matrix = taps_at(column + LANES - row, profile_x) / total_x * scalars[3].astype(F32)
    for block in range(back_x.shape[0]):
        source = row + ((block - 1) * LANES + lead)
        high, low = split(jnp.where((source >= 0) & (source < cells), matrix, 0.0))
        back_x[block, :, :LANES] = high
        back_x[block, :, LANES:] = low


def bands(scalars, profile_z, profile_y, profile_x, planes, cells, after):
    return pl.pallas_call(
        bands_kernel,
        in_specs=[SMEM] * 4 + [ANY],
        out_specs=[VMEM] * 5,
        out_shape=[
            sds((2 * planes, 2 * planes), BF16),
            sds((2 * planes, 2 * planes), BF16),
            sds((cells, cells), BF16),
            sds((cells, cells), BF16),
            sds((cells // LANES, 2 * LANES, 2 * LANES), BF16),
        ],
        compiler_params=params(),
        cost_estimate=cost("bands"),
        name="bands",
    )(scalars, profile_z, profile_y, profile_x, after)


def swap_views(cells, mask):
    return lax.ppermute(cells, "view", [(i, i ^ mask) for i in range(4)])


def on_device(estimate, view_stacks, profile_z, profile_y, profile_x, offsets, coverage):
    planes, rows, cells = estimate.shape
    half = (profile_y.shape[1] - 1) // 2
    lead = (profile_x.shape[1] - 1) // 2
    tiles = lax.axis_size("tile")
    tile = lax.axis_index("tile")
    view = lax.axis_index("view")
    chunks = cells // LANES
    even = (tile + 1) % 2
    groups = [tuple(range(chunks - 2))] + [(chunk,) for chunk in range(chunks - 2, chunks)]
    covered = lax.dynamic_index_in_dim(coverage[0], view, 0, keepdims=False)
    scalars = jnp.stack([even, view, jnp.sum(coverage[0]), covered]).astype(jnp.int32)
    inner_pairs = [(i, i ^ 1) for i in range(tiles)]
    outer_pairs = [(i, i + 1) for i in range(1, tiles - 1, 2)] + [(i + 1, i) for i in range(1, tiles - 1, 2)]

    def exchange(inner, outer):
        return lax.ppermute(inner, "tile", inner_pairs), lax.ppermute(outer, "tile", outer_pairs)

    def move(index, after):
        cells = registered[index] if after is None else gate([registered[index]], after)[0]
        return lax.all_to_all(cells, "tile", split_axis=0, concat_axis=0)

    def share(index, after):
        new = merge(scalars, estimate, parts[index], groups[index], after)
        if index < final:
            pieces[index] = [lax.all_gather(new, "view", axis=0, tiled=True)]
        else:
            pieces[index] = [new] + [swap_views(new, k) for k in (1, 2, 3)]
        return new

    def finish(index, after):
        return assemble(scalars, pieces[index], estimate.shape, groups[index][0] * LANES, result, after)

    final = len(groups) - 1
    places = jnp.stack([even, view]).astype(jnp.int32)
    rows_sent = edge_rows(places, estimate)
    inner, outer = exchange(*rows_sent)
    outers = [outer] + [swap_views(outer, k) for k in (1, 2, 3)]
    *registered, token = prep(offsets, view_stacks[0], tiles, lead, groups, rows_sent[0])
    moved = move(0, (outer,))
    transposed = swap(estimate, token)
    forward_z, back_z, high_x, low_x, back_x = bands(
        scalars, profile_z, profile_y, profile_x, planes, cells, transposed
    )
    inner, outer = swap_edges(places, inner, outers, half, back_z)
    blurred = forward(
        scalars, profile_y[0], transposed, inner, outer, forward_z, high_x, low_x, back_z
    )
    flipped = profile_y[0, ::-1]
    last, result, before = blurred, None, None
    parts, pieces = {}, {}
    for index, group in enumerate(groups):
        quotients, inner, outer, tail = ratio(scalars, moved, blurred, half, group, last)
        last = quotients[0]
        inner, outer = exchange(inner, outer)
        if index < final:
            moved = move(index + 1, (inner,))
        if index >= 1:
            last = share(index - 1, last)
        before, sums = back(
            scalars, flipped, quotients, tail, inner, outer, back_z, back_x, before, group, last
        )
        last = before[0]
        parts[index] = [sums[0]] + [swap_views(sums[k], k) for k in (1, 2, 3)]
        if index >= 2:
            result = finish(index - 2, last)
            last = result
    last = share(final, last)
    result = finish(final - 1, last)
    result = finish(final, last)
    return result


def solution(mesh):
    return jax.shard_map(
        on_device,
        mesh=mesh,
        in_specs=(
            P(None, "tile", None),
            P("view", "tile", None, None),
            P("view", None),
            P("view", None),
            P("view", None),
            P("view"),
            P("tile", None),
        ),
        out_specs=P(None, "tile", None),
        check_vma=False,
    )
```

time: 398 us -> 324 us (0.81)
  blocking collectives: 80.6 us -> 0 us
  starting transfers between devices: 62.9 us -> 49.3 us
  between operations: 1.02 us -> 14.3 us
  Pallas kernels: 113 us -> 124 us
    all_to_all x2 -> x0, blocking collectives: 80.6 us -> none  [on_device(): lax.all_to_all(registered[chunk], 'tile', split_axis=0, concat_axis=0)]
    ppermute x5 -> x4, waiting for transfers between devices: 31.3 us -> 13.7 us  [exchange(): lax.ppermute(outer, 'tile', outer_pairs)]
    ppermute x24 -> x15, starting transfers between devices: 33.1 us -> 17.6 us  [swap_views(): return lax.ppermute(cells, 'view', [(i, i ^ mask) for i in range(4)])]
    all_to_all x2 -> x3, waiting for transfers between devices: 18.3 us -> 31.6 us  [move(): return lax.all_to_all(cells, 'tile', split_axis=0, concat_axis=0)]
    pallas_call x18 -> x19, Pallas kernels: 83 us -> 95.4 us  [the longest x3 39.5 us: back(): pl.pallas_call(functools.partial(back_kernel, taps, count, first), grid=(...]
    ppermute x24 -> x15, waiting for transfers between devices: 66.3 us -> 72.2 us  [swap_views(): return lax.ppermute(cells, 'view', [(i, i ^ mask) for i in range(4)])]
    select_n x1 -> x0, other arithmetic: 4.41 us -> none  [on_device(): jnp.where(is_even, first, last)]
    all_to_all x2 -> x3, starting transfers between devices: 14.4 us -> 17.3 us  [move(): return lax.all_to_all(cells, 'tile', split_axis=0, concat_axis=0)]
  transfers between devices with their start and end apart: 36 -> 28, of which waited for: 12 -> 16; matrix products, arithmetic and copies ran while one was open for 2% -> 1% of each run, Pallas kernels for 27% -> 34%
where the time goes in v2:
time: 324 us; the launch traced here: 323 us
  Pallas kernels  124 us (38%)
  waiting for transfers between devices  118 us (36%)
  starting transfers between devices  49.3 us (15%)
  between operations  14.3 us (4%)
  local copies, waits for them, and re-layouts  13.7 us (4%)
    ppermute x15, waiting for transfers between devices, swap_views(): return lax.ppermute(cells, 'view', [(i, i ^ mask) for i in range(4)])  72.2 us
    pallas_call x3, Pallas kernels, back(): pl.pallas_call(functools.partial(back_kernel, taps, count, first), grid=(...  39.5 us
    all_to_all x3, waiting for transfers between devices, move(): return lax.all_to_all(cells, 'tile', split_axis=0, concat_axis=0)  31.6 us
    pallas_call x1, Pallas kernels, forward(): pl.pallas_call(functools.partial(forward_kernel, taps), in_specs=[SMEM, S...  20.8 us
    ppermute x15, starting transfers between devices, swap_views(): return lax.ppermute(cells, 'view', [(i, i ^ mask) for i in range(4)])  17.6 us
    all_to_all x3, starting transfers between devices, move(): return lax.all_to_all(cells, 'tile', split_axis=0, concat_axis=0)  17.3 us
    pallas_call x3, Pallas kernels, ratio(): pl.pallas_call(functools.partial(ratio_kernel, half, chunks, first), grid...  14.3 us
    ppermute x4, waiting for transfers between devices, exchange(): lax.ppermute(outer, 'tile', outer_pairs)  13.7 us
  transfers between devices with their start and end apart: 28, of which 16 were waited for; matrix products, arithmetic and copies ran while one was open for 1% of the time, Pallas kernels for 34%

profile of v2, /device:TPU:16, one launch (start us, length us, event | category | flops | bytes accessed | tf_op | source)
XLA Modules:
  0.0 322.5 jit_solution(9686360762323858879)
XLA Ops:
  7.1 4.9 %edge_rows.1 = (f32[128,8,512]{2,1,0:T(8,128)}, f32[32,8,512]{2,1,0:T(8,128)}) custom-call(s32[2]{0:T(128)} %pad_add_fusion.1.scalars, f32[128,24,512]{2,1,0:T(8,128)} %estimate_ref.5, f32[128,24,512]{2,1,0:T(8,128)} %estimate_ref.5), custom_call_target="tpu_custom_call" | custom-call | flops 5500000256 | bytes 18000000 | tf_op jit(solution)/shard_map/edge_rows/pallas_call | solution.py:116
  12.0 1.9 collective-permute-start
  13.9 1.7 collective-permute-start.1
  16.3 8.8 %prep.1 = (f32[8,800,128]{2,1,0:T(8,128)}, f32[8,384,128]{2,1,0:T(8,128)}, f32[8,384,128]{2,1,0:T(8,128)}, f32[8,128]{1,0:T(8,128)}) custom-call(s32[1]{0:T(128)S(6)} %copy.18.offsets, f32[16,192,512]{2,1,0:T(8,128)} %bitcast.7, f32[128,8,512]{2,1,0:T(8,128)} %get-tuple-element.46.after), custom_call_target="tpu_custom_call" | custom-call | flops 9900000256 | bytes 32400000 | tf_op jit(solution)/shard_map/prep/pallas_call | solution.py:91
  25.9 4.3 %all-to-all-start = ((f32[8,800,128]{2,1,0:T(8,128)}), f32[8,800,128]{2,1,0:T(8,128)S(1)}, u32[]{:S(2)}, u32[]{:S(2)}) async-start(f32[8,800,128]{2,1,0:T(8,128)} %gate.3), calls=%async_computation | async-start | bytes 6553600 | tf_op jit(solution)/shard_map/all_to_all | solution.py:664
  31.5 8.2 %swap.1.after.own = f32[24,128,512]{2,1,0:T(8,128)} custom-call(f32[128,24,512]{2,1,0:T(8,128)} %estimate_ref.5, f32[8,128]{1,0:T(8,128)} %get-tuple-element.51.after), custom_call_target="tpu_custom_call" | custom-call | flops 8800000000 | bytes 28800000 | tf_op jit(solution)/shard_map/swap/pallas_call | solution.py:143
  39.8 2.4 collective-permute-start.4
  43.2 1.9 pad_add_fusion.scalars
  45.1 3.6 %bands.1 = (bf16[256,256]{1,0:T(8,128)(2,1)}, bf16[256,256]{1,0:T(8,128)(2,1)}, bf16[512,512]{1,0:T(8,128)(2,1)}, bf16[512,512]{1,0:T(8,128)(2,1)}, bf16[4,256,256]{2,1,0:T(8,128)(2,1)}) custom-call(s32[4]{0:T(128)} %pad_add_fusion.scalars, f32[1,31]{1,0:T(1,128)} %profile_z.1, f32[1,15]{1,0:T(1,128)} %profile_y.1, f32[1,15]{1,0:T(1,128)} %profile_x.1, ...), custom_call_target="tpu_custom_call" | custom-call | flops 4400000000 | bytes 14400000 | tf_op jit(solution)/shard_map/bands/pallas_call | solution.py:623
  48.7 6.8 %collective-permute-done.4.d = f32[32,8,512]{2,1,0:T(8,128)S(1)} collective-permute-done((f32[32,8,512]{2,1,0:T(8,128)S(1)}, f32[32,8,512]{2,1,0:T(8,128)S(1)}, u32[]{:S(2)}, u32[]{:S(2)}) %collective-permute-start.4) | collective-permute-done | bytes 524320 | tf_op jit(solution)/shard_map/ppermute | solution.py:641
  55.5 10.4 %collective-permute-done.3.c = f32[32,8,512]{2,1,0:T(8,128)S(1)} collective-permute-done((f32[32,8,512]{2,1,0:T(8,128)S(1)}, f32[32,8,512]{2,1,0:T(8,128)S(1)}, u32[]{:S(2)}, u32[]{:S(2)}) %collective-permute-start.3) | collective-permute-done | bytes 524320 | tf_op jit(solution)/shard_map/ppermute | solution.py:641
  66.9 6.0 %swap_edges.1 = (f32[7,128,512]{2,1,0:T(8,128)}, f32[7,128,512]{2,1,0:T(8,128)}) custom-call(s32[2]{0:T(128)} %pad_add_fusion.1.scalars, f32[128,8,512]{2,1,0:T(8,128)} %collective-permute-done.1.inner_ref, f32[32,8,512]{2,1,0:T(8,128)} %copy-done.4, f32[32,8,512]{2,1,0:T(8,128)} %copy-done.11, f32[32,8,512]{2,1,0:T(8,128)} %copy-done.10, ...), custom_call_target="tpu_custom_call" | custom-call | flops 6600000000 | bytes 21600000 | tf_op jit(solution)/shard_map/swap_edges/pallas_call | solution.py:171
  72.9 20.8 %forward.1.refs_0_.refs_1_.refs_2_.refs_3_ = f32[24,128,512]{2,1,0:T(8,128)} custom-call(s32[4]{0:T(128)} %pad_add_fusion.scalars, f32[15]{0:T(128)} %bitcast.8, f32[24,128,512]{2,1,0:T(8,128)} %swap.1.after.own, f32[7,128,512]{2,1,0:T(8,128)} %get-tuple-element.53.inner, f32[7,128,512]{2,1,0:T(8,128)} %get-tuple-element.54.outer, ...), custom_call_target="tpu_custom_call" | custom-call | flops 32999999488 | bytes 108000000 | tf_op jit(solution)/shard_map/forward/pallas_call | solution.py:283
  93.7 7.6 %all-to-all-done.moved_ref = f32[8,800,128]{2,1,0:T(8,128)S(1)} async-done(((f32[8,800,128]{2,1,0:T(8,128)}), f32[8,800,128]{2,1,0:T(8,128)S(1)}, u32[]{:S(2)}, u32[]{:S(2)}) %all-to-all-start) | async-done | bytes 3276832 | tf_op jit(solution)/shard_map/all_to_all | solution.py:664
  101.3 1.7 copy-done
  103.0 7.1 %ratio.3 = (f32[24,128,128]{2,1,0:T(8,128)}, f32[24,128,128]{2,1,0:T(8,128)}, f32[15,128,128]{2,1,0:T(8,128)}, f32[15,128,128]{2,1,0:T(8,128)}, f32[24,128,128]{2,1,0:T(8,128)}) custom-call(s32[4]{0:T(128)} %pad_add_fusion.scalars, f32[8,800,128]{2,1,0:T(8,128)} %copy-done, f32[24,128,512]{2,1,0:T(8,128)} %forward.1.refs_0_.refs_1_.refs_2_.refs_3_, ...), custom_call_target="tpu_custom_call" | custom-call | flops 5500000256 | bytes 18000000 | tf_op jit(solution)/shard_map/ratio/pallas_call | solution.py:361
  110.1 2.4 collective-permute-start.6
  114.1 6.5 %all-to-all-start.1 = ((f32[8,384,128]{2,1,0:T(8,128)}), f32[8,384,128]{2,1,0:T(8,128)S(1)}, u32[]{:S(2)}, u32[]{:S(2)}) async-start(f32[8,384,128]{2,1,0:T(8,128)} %gate.4), calls=%async_computation.1 | async-start | bytes 3145728 | tf_op jit(solution)/shard_map/all_to_all | solution.py:664
  120.6 10.2 %collective-permute-done.6.outer = f32[15,128,128]{2,1,0:T(8,128)S(1)} collective-permute-done((f32[15,128,128]{2,1,0:T(8,128)}, f32[15,128,128]{2,1,0:T(8,128)S(1)}, u32[]{:S(2)}, u32[]{:S(2)}) %collective-permute-start.6) | collective-permute-done | bytes 983072 | tf_op jit(solution)/shard_map/ppermute | solution.py:660
  131.8 19.6 %back.3 = (bf16[24,128,128]{2,1,0:T(8,128)(2,1)}, bf16[24,128,128]{2,1,0:T(8,128)(2,1)}, f32[48,32,128]{2,1,0:T(8,128)}, f32[48,32,128]{2,1,0:T(8,128)}, f32[48,32,128]{2,1,0:T(8,128)}, /*index=5*/f32[48,32,128]{2,1,0:T(8,128)}) custom-call(s32[4]{0:T(128)} %pad_add_fusion.scalars, f32[15]{0:T(128)} %bitcast.9, f32[15,128,128]{2,1,0:T(8,128)} %copy-done.3, ...), custom_call_target="tpu_custom_call" | custom-call | flops 65999998976 | bytes 216000000 | tf_op jit(solution)/shard_map/back/pallas_call | solution.py:474
  151.4 1.6 collective-permute-start.9
  153.0 1.5 collective-permute-start.10
  155.0 3.1 all-to-all-done.1.moved_ref
  159.3 3.6 %ratio.4 = (f32[24,128,128]{2,1,0:T(8,128)}, f32[7,128,128]{2,1,0:T(8,128)}, f32[7,128,128]{2,1,0:T(8,128)}) custom-call(s32[4]{0:T(128)} %pad_add_fusion.scalars, f32[8,384,128]{2,1,0:T(8,128)} %copy-done.1, f32[24,128,512]{2,1,0:T(8,128)} %forward.1.refs_0_.refs_1_.refs_2_.refs_3_, bf16[24,128,128]{2,1,0:T(8,128)(2,1)} %get-tuple-element.64.refs_1_), custom_call_target="tpu_custom_call" | custom-call | flops 5500000256 | bytes 18000000 | tf_op jit(solution)/shard_map/ratio/pallas_call | solution.py:361
  162.8 6.0 %collective-permute-start.8 = (f32[7,128,128]{2,1,0:T(8,128)}, f32[7,128,128]{2,1,0:T(8,128)}, u32[]{:S(2)}, u32[]{:S(2)}) collective-permute-start(f32[7,128,128]{2,1,0:T(8,128)} %get-tuple-element.66), channel_id=1, source_target_pairs={{1,2},{3,4},{5,6},{2,1},{4,3},{6,5},{9,10},{11,12},{13,14},{10,9},... | collective-permute-start | bytes 1376264 | tf_op jit(solution)/shard_map/ppermute | solution.py:660
  168.9 1.7 collective-permute-done.9.b
  170.6 2.6 collective-permute-done.10.c
  173.2 15.4 %collective-permute-done.11.d = f32[48,32,128]{2,1,0:T(8,128)} collective-permute-done((f32[48,32,128]{2,1,0:T(8,128)}, f32[48,32,128]{2,1,0:T(8,128)}, u32[]{:S(2)}, u32[]{:S(2)}) %collective-permute-start.11) | collective-permute-done | bytes 786464 | tf_op jit(solution)/shard_map/ppermute | solution.py:641
  188.6 3.7 %merge.3.refs_3_ = f32[32,24,256]{2,1,0:T(8,128)} custom-call(s32[4]{0:T(128)} %pad_add_fusion.scalars, f32[128,24,512]{2,1,0:T(8,128)} %estimate_ref.5, f32[48,32,128]{2,1,0:T(8,128)} %get-tuple-element.69.a, f32[48,32,128]{2,1,0:T(8,128)} %copy-done.7, f32[48,32,128]{2,1,0:T(8,128)} %copy-done.8, f32[48,32,128]{2,1,0:T(8,128)} %collective-permute-done.11.d, ...), custom_call_target="tpu_custom_call" | custom-call | flops 32999999488 | bytes 108000000 | tf_op jit(solution)/shard_map/merge/pallas_call | solution.py:521
  193.1 6.4 %all-to-all-start.2 = ((f32[8,384,128]{2,1,0:T(8,128)}), f32[8,384,128]{2,1,0:T(8,128)S(1)}, u32[]{:S(2)}, u32[]{:S(2)}) async-start(f32[8,384,128]{2,1,0:T(8,128)} %gate.5), calls=%async_computation.2 | async-start | bytes 3145728 | tf_op jit(solution)/shard_map/all_to_all | solution.py:664
  199.5 10.1 %back.4 = (bf16[24,128,128]{2,1,0:T(8,128)(2,1)}, bf16[24,128,128]{2,1,0:T(8,128)(2,1)}, f32[24,32,128]{2,1,0:T(8,128)}, f32[24,32,128]{2,1,0:T(8,128)}, f32[24,32,128]{2,1,0:T(8,128)}, /*index=5*/f32[24,32,128]{2,1,0:T(8,128)}) custom-call(s32[4]{0:T(128)} %pad_add_fusion.scalars, f32[15]{0:T(128)} %bitcast.10, f32[7,128,128]{2,1,0:T(8,128)} %copy-done.12, ...), custom_call_target="tpu_custom_call" | custom-call | flops 65999998976 | bytes 216000000 | tf_op jit(solution)/shard_map/back/pallas_call | solution.py:474
  209.6 1.9 collective-permute-start.15
  211.5 1.6 collective-permute-start.16
  213.1 20.9 %all-to-all-done.2.moved_ref = f32[8,384,128]{2,1,0:T(8,128)S(1)} async-done(((f32[8,384,128]{2,1,0:T(8,128)}), f32[8,384,128]{2,1,0:T(8,128)S(1)}, u32[]{:S(2)}, u32[]{:S(2)}) %all-to-all-start.2) | async-done | bytes 1572896 | tf_op jit(solution)/shard_map/all_to_all | solution.py:664
  235.2 3.6 %ratio.5 = (f32[24,128,128]{2,1,0:T(8,128)}, f32[7,128,128]{2,1,0:T(8,128)}, f32[7,128,128]{2,1,0:T(8,128)}) custom-call(s32[4]{0:T(128)} %pad_add_fusion.scalars, f32[8,384,128]{2,1,0:T(8,128)} %copy-done.2, f32[24,128,512]{2,1,0:T(8,128)} %forward.1.refs_0_.refs_1_.refs_2_.refs_3_, bf16[24,128,128]{2,1,0:T(8,128)(2,1)} %get-tuple-element.73.refs_1_), custom_call_target="tpu_custom_call" | custom-call | flops 5500000256 | bytes 18000000 | tf_op jit(solution)/shard_map/ratio/pallas_call | solution.py:361
  238.8 2.4 collective-permute-start.13
  242.2 3.0 merge.4.refs_3_
  245.3 3.5 %collective-permute-done.13.outer = f32[7,128,128]{2,1,0:T(8,128)S(1)} collective-permute-done((f32[7,128,128]{2,1,0:T(8,128)}, f32[7,128,128]{2,1,0:T(8,128)S(1)}, u32[]{:S(2)}, u32[]{:S(2)}) %collective-permute-start.13) | collective-permute-done | bytes 458784 | tf_op jit(solution)/shard_map/ppermute | solution.py:660
  249.5 9.8 %back.5 = (bf16[24,128,128]{2,1,0:T(8,128)(2,1)}, bf16[24,128,128]{2,1,0:T(8,128)(2,1)}, f32[24,32,128]{2,1,0:T(8,128)}, f32[24,32,128]{2,1,0:T(8,128)}, f32[24,32,128]{2,1,0:T(8,128)}, /*index=5*/f32[24,32,128]{2,1,0:T(8,128)}) custom-call(s32[4]{0:T(128)} %pad_add_fusion.scalars, f32[15]{0:T(128)} %bitcast.11, f32[7,128,128]{2,1,0:T(8,128)} %copy-done.13, ...), custom_call_target="tpu_custom_call" | custom-call | flops 65999998976 | bytes 216000000 | tf_op jit(solution)/shard_map/back/pallas_call | solution.py:474
  259.6 1.9 collective-permute-start.18
  262.9 3.6 %assemble.3.after.refs_1_ = f32[128,24,512]{2,1,0:T(8,128)} custom-call(s32[4]{0:T(128)} %pad_add_fusion.scalars, f32[128,24,256]{2,1,0:T(8,128)} %all-gather.3.cloned.1.call-done.refs_0_, bf16[24,128,128]{2,1,0:T(8,128)(2,1)} %get-tuple-element.86.refs_1_), custom_call_target="tpu_custom_call" | custom-call | flops 11000000512 | bytes 36000000 | tf_op jit(solution)/shard_map/assemble/pallas_call | solution.py:558
  266.5 6.1 %collective-permute-done.17.b = f32[24,32,128]{2,1,0:T(8,128)S(1)} collective-permute-done((f32[24,32,128]{2,1,0:T(8,128)}, f32[24,32,128]{2,1,0:T(8,128)S(1)}, u32[]{:S(2)}, u32[]{:S(2)}) %collective-permute-start.17) | collective-permute-done | bytes 393248 | tf_op jit(solution)/shard_map/ppermute | solution.py:641
  272.7 15.3 %collective-permute-done.19.d = f32[24,32,128]{2,1,0:T(8,128)S(1)} collective-permute-done((f32[24,32,128]{2,1,0:T(8,128)}, f32[24,32,128]{2,1,0:T(8,128)S(1)}, u32[]{:S(2)}, u32[]{:S(2)}) %collective-permute-start.19) | collective-permute-done | bytes 393248 | tf_op jit(solution)/shard_map/ppermute | solution.py:641
  288.7 3.1 merge.5.refs_2_.refs_0_.refs_5_
  295.3 2.6 assemble.4.refs_4_
  297.9 7.1 %collective-permute-done.22.refs_3_ = f32[32,24,128]{2,1,0:T(8,128)S(1)} collective-permute-done((f32[32,24,128]{2,1,0:T(8,128)}, f32[32,24,128]{2,1,0:T(8,128)S(1)}, u32[]{:S(2)}, u32[]{:S(2)}) %collective-permute-start.22) | collective-permute-done | bytes 393248 | tf_op jit(solution)/shard_map/ppermute | solution.py:641
  304.9 6.7 %collective-permute-done.21.refs_2_ = f32[32,24,128]{2,1,0:T(8,128)S(1)} collective-permute-done((f32[32,24,128]{2,1,0:T(8,128)}, f32[32,24,128]{2,1,0:T(8,128)S(1)}, u32[]{:S(2)}, u32[]{:S(2)}) %collective-permute-start.21) | collective-permute-done | bytes 393248 | tf_op jit(solution)/shard_map/ppermute | solution.py:641
  313.2 2.5 assemble.5
  (88 shorter events, 20.2 us)
Async XLA Ops:
  12.0 13.1 %collective-permute-start = (f32[32,8,512]{2,1,0:T(8,128)}, f32[32,8,512]{2,1,0:T(8,128)S(1)}, u32[]{:S(2)}, u32[]{:S(2)}) collective-permute-start(f32[32,8,512]{2,1,0:T(8,128)} %get-tuple-element.50), channel_id=1, source_target_pairs={{1,2},{3,4},{5,6},{2,1},{4,3},{6,5},{9,10},{11,12},{13,14},{10,9},... | collective-permute-start | bytes 1572872 | tf_op jit(solution)/shard_map/ppermute | solution.py:660
  13.9 52.0 %collective-permute-start.1 = (f32[128,8,512]{2,1,0:T(8,128)}, f32[128,8,512]{2,1,0:T(8,128)}, u32[]{:S(2)}, u32[]{:S(2)}) collective-permute-start(f32[128,8,512]{2,1,0:T(8,128)} %get-tuple-element.46.after), channel_id=1, source_target_pairs={{0,1},{1,0},{2,3},{3,2},{4,5},{5,4},{6,7},{7,6},{8,9},{9,8},{10,11... | collective-permute-start | bytes 6291464 | tf_op jit(solution)/shard_map/ppermute | solution.py:660
  25.1 0.8 copy-start.4
  25.9 4.3 %copy-start.24 = (s32[1,4]{1,0:T(1,128)S(1)}, s32[1,4]{1,0:T(1,128)}, u32[]{:S(2)}) copy-start(s32[1,4]{1,0:T(1,128)} %param.13) | copy-start | bytes 52
  25.9 75.4 %all-to-all-start = ((f32[8,800,128]{2,1,0:T(8,128)}), f32[8,800,128]{2,1,0:T(8,128)S(1)}, u32[]{:S(2)}, u32[]{:S(2)}) async-start(f32[8,800,128]{2,1,0:T(8,128)} %gate.3), calls=%async_computation | async-start | bytes 6553600 | tf_op jit(solution)/shard_map/all_to_all | solution.py:664
  31.5 8.2 %copy-start.5 = (f32[32,8,512]{2,1,0:T(8,128)S(1)}, f32[32,8,512]{2,1,0:T(8,128)}, u32[]{:S(2)}) copy-start(f32[32,8,512]{2,1,0:T(8,128)} %copy-done.4) | copy-start | bytes 1572868
  39.8 15.7 %collective-permute-start.4 = (f32[32,8,512]{2,1,0:T(8,128)S(1)}, f32[32,8,512]{2,1,0:T(8,128)S(1)}, u32[]{:S(2)}, u32[]{:S(2)}) collective-permute-start(f32[32,8,512]{2,1,0:T(8,128)S(1)} %copy-done.5), channel_id=1, source_target_pairs={{0,24},{8,16},{16,8},{24,0},{1,25},{9,17},{17,9},{25,1},{2,26},{10... | collective-permute-start | bytes 1572872 | tf_op jit(solution)/shard_map/ppermute | solution.py:641
  42.2 23.7 %collective-permute-start.3 = (f32[32,8,512]{2,1,0:T(8,128)S(1)}, f32[32,8,512]{2,1,0:T(8,128)S(1)}, u32[]{:S(2)}, u32[]{:S(2)}) collective-permute-start(f32[32,8,512]{2,1,0:T(8,128)S(1)} %copy-done.5), channel_id=1, source_target_pairs={{0,16},{8,24},{16,0},{24,8},{1,17},{9,25},{17,1},{25,9},{2,18},{10... | collective-permute-start | bytes 1572872 | tf_op jit(solution)/shard_map/ppermute | solution.py:641
  42.7 23.3 %collective-permute-start.2 = (f32[32,8,512]{2,1,0:T(8,128)S(1)}, f32[32,8,512]{2,1,0:T(8,128)S(1)}, u32[]{:S(2)}, u32[]{:S(2)}) collective-permute-start(f32[32,8,512]{2,1,0:T(8,128)S(1)} %copy-done.5), channel_id=1, source_target_pairs={{0,8},{8,0},{16,24},{24,16},{1,9},{9,1},{17,25},{25,17},{2,10},{10... | collective-permute-start | bytes 1572872 | tf_op jit(solution)/shard_map/ppermute | solution.py:641
  55.5 10.5 %copy-start.9 = (f32[32,8,512]{2,1,0:T(8,128)}, f32[32,8,512]{2,1,0:T(8,128)S(1)}, u32[]{:S(2)}) copy-start(f32[32,8,512]{2,1,0:T(8,128)S(1)} %collective-permute-done.4.d) | copy-start | bytes 1572868
  65.9 0.8 copy-start.10
  66.0 0.9 copy-start.11
  93.7 18.8 %copy-start.25 = (f32[1,15]{1,0:T(1,128)S(1)}, f32[1,15]{1,0:T(1,128)}, u32[]{:S(2)}) copy-start(f32[1,15]{1,0:T(1,128)} %profile_y.1) | copy-start | bytes 184
  101.3 1.7 copy-start
  110.1 3.0 collective-permute-start.5
  110.1 20.7 %collective-permute-start.6 = (f32[15,128,128]{2,1,0:T(8,128)}, f32[15,128,128]{2,1,0:T(8,128)S(1)}, u32[]{:S(2)}, u32[]{:S(2)}) collective-permute-start(f32[15,128,128]{2,1,0:T(8,128)} %get-tuple-element.59), channel_id=1, source_target_pairs={{1,2},{3,4},{5,6},{2,1},{4,3},{6,5},{9,10},{11,12},{13,14},{10,9},... | collective-permute-start | bytes 2949128 | tf_op jit(solution)/shard_map/ppermute | solution.py:660
  113.1 0.9 copy-start.3
  114.1 44.0 %all-to-all-start.1 = ((f32[8,384,128]{2,1,0:T(8,128)}), f32[8,384,128]{2,1,0:T(8,128)S(1)}, u32[]{:S(2)}, u32[]{:S(2)}) async-start(f32[8,384,128]{2,1,0:T(8,128)} %gate.4), calls=%async_computation.1 | async-start | bytes 3145728 | tf_op jit(solution)/shard_map/all_to_all | solution.py:664
  120.6 142.3 %all-gather.3.cloned.1.call-start = ((), (), s32[]{:S(2)}) async-start(), calls=%async_computation.3 | async-start | bytes 3932160 | tf_op jit(solution)/shard_map/all_gather | solution.py:669
  130.8 1.0 copy-start.6
  151.4 19.1 %collective-permute-start.9 = (f32[48,32,128]{2,1,0:T(8,128)}, f32[48,32,128]{2,1,0:T(8,128)S(1)}, u32[]{:S(2)}, u32[]{:S(2)}) collective-permute-start(f32[48,32,128]{2,1,0:T(8,128)} %get-tuple-element.70), channel_id=1, source_target_pairs={{0,8},{8,0},{16,24},{24,16},{1,9},{9,1},{17,25},{25,17},{2,10},{10... | collective-permute-start | bytes 2359304 | tf_op jit(solution)/shard_map/ppermute | solution.py:641
  153.0 20.2 %collective-permute-start.10 = (f32[48,32,128]{2,1,0:T(8,128)}, f32[48,32,128]{2,1,0:T(8,128)S(1)}, u32[]{:S(2)}, u32[]{:S(2)}) collective-permute-start(f32[48,32,128]{2,1,0:T(8,128)} %get-tuple-element.71), channel_id=1, source_target_pairs={{0,16},{8,24},{16,0},{24,8},{1,17},{9,25},{17,1},{25,9},{2,18},{10... | collective-permute-start | bytes 2359304 | tf_op jit(solution)/shard_map/ppermute | solution.py:641
  154.5 34.1 %collective-permute-start.11 = (f32[48,32,128]{2,1,0:T(8,128)}, f32[48,32,128]{2,1,0:T(8,128)}, u32[]{:S(2)}, u32[]{:S(2)}) collective-permute-start(f32[48,32,128]{2,1,0:T(8,128)} %get-tuple-element.72), channel_id=1, source_target_pairs={{0,24},{8,16},{16,8},{24,0},{1,25},{9,17},{17,9},{25,1},{2,26},{10... | collective-permute-start | bytes 2359304 | tf_op jit(solution)/shard_map/ppermute | solution.py:641
  158.1 1.1 copy-start.1
  162.8 29.5 %collective-permute-start.7 = (f32[7,128,128]{2,1,0:T(8,128)}, f32[7,128,128]{2,1,0:T(8,128)S(1)}, u32[]{:S(2)}, u32[]{:S(2)}) collective-permute-start(f32[7,128,128]{2,1,0:T(8,128)} %get-tuple-element.65), channel_id=1, source_target_pairs={{0,1},{1,0},{2,3},{3,2},{4,5},{5,4},{6,7},{7,6},{8,9},{9,8},{10,11... | collective-permute-start | bytes 1376264 | tf_op jit(solution)/shard_map/ppermute | solution.py:660
  162.8 36.7 %collective-permute-start.8 = (f32[7,128,128]{2,1,0:T(8,128)}, f32[7,128,128]{2,1,0:T(8,128)}, u32[]{:S(2)}, u32[]{:S(2)}) collective-permute-start(f32[7,128,128]{2,1,0:T(8,128)} %get-tuple-element.66), channel_id=1, source_target_pairs={{1,2},{3,4},{5,6},{2,1},{4,3},{6,5},{9,10},{11,12},{13,14},{10,9},... | collective-permute-start | bytes 1376264 | tf_op jit(solution)/shard_map/ppermute | solution.py:660
  170.6 18.0 %copy-start.7 = (f32[48,32,128]{2,1,0:T(8,128)}, f32[48,32,128]{2,1,0:T(8,128)S(1)}, u32[]{:S(2)}) copy-start(f32[48,32,128]{2,1,0:T(8,128)S(1)} %collective-permute-done.9.b) | copy-start | bytes 2359300
  173.2 15.4 %copy-start.8 = (f32[48,32,128]{2,1,0:T(8,128)}, f32[48,32,128]{2,1,0:T(8,128)S(1)}, u32[]{:S(2)}) copy-start(f32[48,32,128]{2,1,0:T(8,128)S(1)} %collective-permute-done.10.c) | copy-start | bytes 2359300
  193.1 41.0 %all-to-all-start.2 = ((f32[8,384,128]{2,1,0:T(8,128)}), f32[8,384,128]{2,1,0:T(8,128)S(1)}, u32[]{:S(2)}, u32[]{:S(2)}) async-start(f32[8,384,128]{2,1,0:T(8,128)} %gate.5), calls=%async_computation.2 | async-start | bytes 3145728 | tf_op jit(solution)/shard_map/all_to_all | solution.py:664
  199.5 95.8 %all-gather.5.cloned.1.call-start = ((), (), s32[]{:S(2)}) async-start(), calls=%async_computation.4 | async-start | bytes 1966080 | tf_op jit(solution)/shard_map/all_gather | solution.py:669
  209.6 31.6 %collective-permute-start.14 = (f32[24,32,128]{2,1,0:T(8,128)}, f32[24,32,128]{2,1,0:T(8,128)S(1)}, u32[]{:S(2)}, u32[]{:S(2)}) collective-permute-start(f32[24,32,128]{2,1,0:T(8,128)} %get-tuple-element.79), channel_id=1, source_target_pairs={{0,8},{8,0},{16,24},{24,16},{1,9},{9,1},{17,25},{25,17},{2,10},{10... | collective-permute-start | bytes 1179656 | tf_op jit(solution)/shard_map/ppermute | solution.py:641
  209.6 31.5 %collective-permute-start.15 = (f32[24,32,128]{2,1,0:T(8,128)}, f32[24,32,128]{2,1,0:T(8,128)S(1)}, u32[]{:S(2)}, u32[]{:S(2)}) collective-permute-start(f32[24,32,128]{2,1,0:T(8,128)} %get-tuple-element.80), channel_id=1, source_target_pairs={{0,16},{8,24},{16,0},{24,8},{1,17},{9,25},{17,1},{25,9},{2,18},{10... | collective-permute-start | bytes 1179656 | tf_op jit(solution)/shard_map/ppermute | solution.py:641
  211.5 29.7 %collective-permute-start.16 = (f32[24,32,128]{2,1,0:T(8,128)}, f32[24,32,128]{2,1,0:T(8,128)S(1)}, u32[]{:S(2)}, u32[]{:S(2)}) collective-permute-start(f32[24,32,128]{2,1,0:T(8,128)} %get-tuple-element.81), channel_id=1, source_target_pairs={{0,24},{8,16},{16,8},{24,0},{1,25},{9,17},{17,9},{25,1},{2,26},{10... | collective-permute-start | bytes 1179656 | tf_op jit(solution)/shard_map/ppermute | solution.py:641
  234.1 1.1 copy-start.2
  238.8 6.5 %collective-permute-start.12 = (f32[7,128,128]{2,1,0:T(8,128)}, f32[7,128,128]{2,1,0:T(8,128)S(1)}, u32[]{:S(2)}, u32[]{:S(2)}) collective-permute-start(f32[7,128,128]{2,1,0:T(8,128)} %get-tuple-element.74), channel_id=1, source_target_pairs={{0,1},{1,0},{2,3},{3,2},{4,5},{5,4},{6,7},{7,6},{8,9},{9,8},{10,11... | collective-permute-start | bytes 1376264 | tf_op jit(solution)/shard_map/ppermute | solution.py:660
  238.8 10.0 %collective-permute-start.13 = (f32[7,128,128]{2,1,0:T(8,128)}, f32[7,128,128]{2,1,0:T(8,128)S(1)}, u32[]{:S(2)}, u32[]{:S(2)}) collective-permute-start(f32[7,128,128]{2,1,0:T(8,128)} %get-tuple-element.75), channel_id=1, source_target_pairs={{1,2},{3,4},{5,6},{2,1},{4,3},{6,5},{9,10},{11,12},{13,14},{10,9},... | collective-permute-start | bytes 1376264 | tf_op jit(solution)/shard_map/ppermute | solution.py:660
  241.2 0.9 copy-start.16
  241.2 1.0 copy-start.17
  245.3 3.5 %copy-start.13 = (f32[7,128,128]{2,1,0:T(8,128)}, f32[7,128,128]{2,1,0:T(8,128)S(1)}, u32[]{:S(2)}) copy-start(f32[7,128,128]{2,1,0:T(8,128)S(1)} %collective-permute-done.12.inner) | copy-start | bytes 1376260
  259.4 13.2 %collective-permute-start.17 = (f32[24,32,128]{2,1,0:T(8,128)}, f32[24,32,128]{2,1,0:T(8,128)S(1)}, u32[]{:S(2)}, u32[]{:S(2)}) collective-permute-start(f32[24,32,128]{2,1,0:T(8,128)} %get-tuple-element.83), channel_id=1, source_target_pairs={{0,8},{8,0},{16,24},{24,16},{1,9},{9,1},{17,25},{25,17},{2,10},{10... | collective-permute-start | bytes 1179656 | tf_op jit(solution)/shard_map/ppermute | solution.py:641
  259.6 13.1 %collective-permute-start.18 = (f32[24,32,128]{2,1,0:T(8,128)}, f32[24,32,128]{2,1,0:T(8,128)S(1)}, u32[]{:S(2)}, u32[]{:S(2)}) collective-permute-start(f32[24,32,128]{2,1,0:T(8,128)} %get-tuple-element.84), channel_id=1, source_target_pairs={{0,16},{8,24},{16,0},{24,8},{1,17},{9,25},{17,1},{25,9},{2,18},{10... | collective-permute-start | bytes 1179656 | tf_op jit(solution)/shard_map/ppermute | solution.py:641
  261.5 26.5 %collective-permute-start.19 = (f32[24,32,128]{2,1,0:T(8,128)}, f32[24,32,128]{2,1,0:T(8,128)S(1)}, u32[]{:S(2)}, u32[]{:S(2)}) collective-permute-start(f32[24,32,128]{2,1,0:T(8,128)} %get-tuple-element.85), channel_id=1, source_target_pairs={{0,24},{8,16},{16,8},{24,0},{1,25},{9,17},{17,9},{25,1},{2,26},{10... | collective-permute-start | bytes 1179656 | tf_op jit(solution)/shard_map/ppermute | solution.py:641
  272.6 15.4 %copy-start.18 = (f32[24,32,128]{2,1,0:T(8,128)}, f32[24,32,128]{2,1,0:T(8,128)S(1)}, u32[]{:S(2)}) copy-start(f32[24,32,128]{2,1,0:T(8,128)S(1)} %collective-permute-done.17.b) | copy-start | bytes 1179652
  272.7 15.3 %copy-start.19 = (f32[24,32,128]{2,1,0:T(8,128)}, f32[24,32,128]{2,1,0:T(8,128)S(1)}, u32[]{:S(2)}) copy-start(f32[24,32,128]{2,1,0:T(8,128)S(1)} %collective-permute-done.18.c) | copy-start | bytes 1179652
  291.8 13.1 %collective-permute-start.22 = (f32[32,24,128]{2,1,0:T(8,128)}, f32[32,24,128]{2,1,0:T(8,128)S(1)}, u32[]{:S(2)}, u32[]{:S(2)}) collective-permute-start(f32[32,24,128]{2,1,0:T(8,128)} %merge.5.refs_2_.refs_0_.refs_5_), channel_id=1, source_target_pairs={{0,24},{8,16},{16,8},{24,0},{1,25},{9,17},{17,9},{25,1},{2,26},{10... | collective-permute-start | bytes 1179656 | tf_op jit(solution)/shard_map/ppermute | solution.py:641
  292.4 19.3 %collective-permute-start.21 = (f32[32,24,128]{2,1,0:T(8,128)}, f32[32,24,128]{2,1,0:T(8,128)S(1)}, u32[]{:S(2)}, u32[]{:S(2)}) collective-permute-start(f32[32,24,128]{2,1,0:T(8,128)} %merge.5.refs_2_.refs_0_.refs_5_), channel_id=1, source_target_pairs={{0,16},{8,24},{16,0},{24,8},{1,17},{9,25},{17,1},{25,9},{2,18},{10... | collective-permute-start | bytes 1179656 | tf_op jit(solution)/shard_map/ppermute | solution.py:641
  293.9 17.8 %collective-permute-start.20 = (f32[32,24,128]{2,1,0:T(8,128)}, f32[32,24,128]{2,1,0:T(8,128)S(1)}, u32[]{:S(2)}, u32[]{:S(2)}) collective-permute-start(f32[32,24,128]{2,1,0:T(8,128)} %merge.5.refs_2_.refs_0_.refs_5_), channel_id=1, source_target_pairs={{0,8},{8,0},{16,24},{24,16},{1,9},{9,1},{17,25},{25,17},{2,10},{10... | collective-permute-start | bytes 1179656 | tf_op jit(solution)/shard_map/ppermute | solution.py:641
  304.9 6.7 %copy-start.20 = (f32[32,24,128]{2,1,0:T(8,128)}, f32[32,24,128]{2,1,0:T(8,128)S(1)}, u32[]{:S(2)}) copy-start(f32[32,24,128]{2,1,0:T(8,128)S(1)} %collective-permute-done.22.refs_3_) | copy-start | bytes 1179652
  (6 other events, 4.5 us)
Sparse Core Ops, SparseCore 0:
  192.4 54.5 all-gather.2
  248.9 41.6 all-gather.4

commit v3 on v2

--- a/solution.py
+++ b/solution.py
@@ -274,7 +274,7 @@
         out_ref[pl.ds(index * group, group)] = result.reshape(group, planes, cells)
         return carry
 
-    lax.fori_loop(0, rows // group, step_zx, 0)
+    lax.fori_loop(0, rows // group, step_zx, 0, unroll=3)
 
 
 def forward(even, weights, own, inner, outer, along_z, high_x, low_x, after):
@@ -422,7 +422,7 @@
                 totals[pl.ds(number * rows + index * group, group)] = result.reshape(group, planes, LANES)
             return carry
 
-        lax.fori_loop(0, rows // group, step_zx, 0)
+        lax.fori_loop(0, rows // group, step_zx, 0, unroll=3)
 
     loads = [
         place_rows(even, own, inner, outer, number * half, buffers.at[number], sems.at[number], half)

time: 324 us -> 320 us (0.988)
  Pallas kernels: 124 us -> 119 us
  waiting for transfers between devices: 118 us -> 122 us
    pallas_call x3, Pallas kernels: 39.5 us -> 34.7 us  [back(): pl.pallas_call(functools.partial(back_kernel, taps, count, first), grid=(...]
    all_to_all x3, waiting for transfers between devices: 31.6 us -> 36 us  [move(): return lax.all_to_all(cells, 'tile', split_axis=0, concat_axis=0)]
  transfers between devices with their start and end apart: 28 -> 28, of which waited for: 16 -> 16; matrix products, arithmetic and copies ran while one was open for 1% -> 1% of each run, Pallas kernels for 34% -> 33%
where the time goes in v3:
time: 320 us; the launch traced here: 319 us
  waiting for transfers between devices  122 us (38%)
  Pallas kernels  119 us (37%)
  starting transfers between devices  46.6 us (15%)
  between operations  14.3 us (4%)
  local copies, waits for them, and re-layouts  13.7 us (4%)
    ppermute x15, waiting for transfers between devices, swap_views(): return lax.ppermute(cells, 'view', [(i, i ^ mask) for i in range(4)])  72.4 us
    all_to_all x3, waiting for transfers between devices, move(): return lax.all_to_all(cells, 'tile', split_axis=0, concat_axis=0)  36 us
    pallas_call x3, Pallas kernels, back(): pl.pallas_call(functools.partial(back_kernel, taps, count, first), grid=(...  34.7 us
    pallas_call x1, Pallas kernels, forward(): pl.pallas_call(functools.partial(forward_kernel, taps), in_specs=[SMEM, S...  20.2 us
    ppermute x15, starting transfers between devices, swap_views(): return lax.ppermute(cells, 'view', [(i, i ^ mask) for i in range(4)])  17.6 us
    all_to_all x3, starting transfers between devices, move(): return lax.all_to_all(cells, 'tile', split_axis=0, concat_axis=0)  17.3 us
    pallas_call x3, Pallas kernels, ratio(): pl.pallas_call(functools.partial(ratio_kernel, half, chunks, first), grid...  14.3 us
    ppermute x4, waiting for transfers between devices, exchange(): lax.ppermute(outer, 'tile', outer_pairs)  13.7 us
  transfers between devices with their start and end apart: 28, of which 16 were waited for; matrix products, arithmetic and copies ran while one was open for 1% of the time, Pallas kernels for 33%

profile of v3, /device:TPU:16, one launch (start us, length us, event | category | flops | bytes accessed | tf_op | source)
XLA Modules:
  0.0 318.9 jit_solution(13975616168772316265)
XLA Ops:
  7.1 4.9 %edge_rows.1 = (f32[128,8,512]{2,1,0:T(8,128)}, f32[32,8,512]{2,1,0:T(8,128)}) custom-call(s32[2]{0:T(128)} %pad_add_fusion.1.scalars, f32[128,24,512]{2,1,0:T(8,128)} %estimate_ref.5, f32[128,24,512]{2,1,0:T(8,128)} %estimate_ref.5), custom_call_target="tpu_custom_call" | custom-call | flops 5500000256 | bytes 18000000 | tf_op jit(solution)/shard_map/edge_rows/pallas_call | solution.py:116
  12.0 1.9 collective-permute-start
  13.9 1.7 collective-permute-start.1
  16.3 8.8 %prep.1 = (f32[8,800,128]{2,1,0:T(8,128)}, f32[8,384,128]{2,1,0:T(8,128)}, f32[8,384,128]{2,1,0:T(8,128)}, f32[8,128]{1,0:T(8,128)}) custom-call(s32[1]{0:T(128)S(6)} %copy.18.offsets, f32[16,192,512]{2,1,0:T(8,128)} %bitcast.7, f32[128,8,512]{2,1,0:T(8,128)} %get-tuple-element.46.after), custom_call_target="tpu_custom_call" | custom-call | flops 9900000256 | bytes 32400000 | tf_op jit(solution)/shard_map/prep/pallas_call | solution.py:91
  25.9 4.3 %all-to-all-start = ((f32[8,800,128]{2,1,0:T(8,128)}), f32[8,800,128]{2,1,0:T(8,128)S(1)}, u32[]{:S(2)}, u32[]{:S(2)}) async-start(f32[8,800,128]{2,1,0:T(8,128)} %gate.3), calls=%async_computation | async-start | bytes 6553600 | tf_op jit(solution)/shard_map/all_to_all | solution.py:664
  31.5 8.2 %swap.1.after.own = f32[24,128,512]{2,1,0:T(8,128)} custom-call(f32[128,24,512]{2,1,0:T(8,128)} %estimate_ref.5, f32[8,128]{1,0:T(8,128)} %get-tuple-element.51.after), custom_call_target="tpu_custom_call" | custom-call | flops 8800000000 | bytes 28800000 | tf_op jit(solution)/shard_map/swap/pallas_call | solution.py:143
  39.8 2.4 collective-permute-start.4
  43.2 1.9 pad_add_fusion.scalars
  45.1 3.6 %bands.1 = (bf16[256,256]{1,0:T(8,128)(2,1)}, bf16[256,256]{1,0:T(8,128)(2,1)}, bf16[512,512]{1,0:T(8,128)(2,1)}, bf16[512,512]{1,0:T(8,128)(2,1)}, bf16[4,256,256]{2,1,0:T(8,128)(2,1)}) custom-call(s32[4]{0:T(128)} %pad_add_fusion.scalars, f32[1,31]{1,0:T(1,128)} %profile_z.1, f32[1,15]{1,0:T(1,128)} %profile_y.1, f32[1,15]{1,0:T(1,128)} %profile_x.1, ...), custom_call_target="tpu_custom_call" | custom-call | flops 4400000000 | bytes 14400000 | tf_op jit(solution)/shard_map/bands/pallas_call | solution.py:623
  48.7 6.8 %collective-permute-done.4.d = f32[32,8,512]{2,1,0:T(8,128)S(1)} collective-permute-done((f32[32,8,512]{2,1,0:T(8,128)S(1)}, f32[32,8,512]{2,1,0:T(8,128)S(1)}, u32[]{:S(2)}, u32[]{:S(2)}) %collective-permute-start.4) | collective-permute-done | bytes 524320 | tf_op jit(solution)/shard_map/ppermute | solution.py:641
  55.5 10.4 %collective-permute-done.3.c = f32[32,8,512]{2,1,0:T(8,128)S(1)} collective-permute-done((f32[32,8,512]{2,1,0:T(8,128)S(1)}, f32[32,8,512]{2,1,0:T(8,128)S(1)}, u32[]{:S(2)}, u32[]{:S(2)}) %collective-permute-start.3) | collective-permute-done | bytes 524320 | tf_op jit(solution)/shard_map/ppermute | solution.py:641
  66.9 6.0 %swap_edges.1 = (f32[7,128,512]{2,1,0:T(8,128)}, f32[7,128,512]{2,1,0:T(8,128)}) custom-call(s32[2]{0:T(128)} %pad_add_fusion.1.scalars, f32[128,8,512]{2,1,0:T(8,128)} %collective-permute-done.1.inner_ref, f32[32,8,512]{2,1,0:T(8,128)} %copy-done.4, f32[32,8,512]{2,1,0:T(8,128)} %copy-done.11, f32[32,8,512]{2,1,0:T(8,128)} %copy-done.10, ...), custom_call_target="tpu_custom_call" | custom-call | flops 6600000000 | bytes 21600000 | tf_op jit(solution)/shard_map/swap_edges/pallas_call | solution.py:171
  72.9 20.2 %forward.1.refs_0_.refs_1_.refs_2_.refs_3_ = f32[24,128,512]{2,1,0:T(8,128)} custom-call(s32[4]{0:T(128)} %pad_add_fusion.scalars, f32[15]{0:T(128)} %bitcast.8, f32[24,128,512]{2,1,0:T(8,128)} %swap.1.after.own, f32[7,128,512]{2,1,0:T(8,128)} %get-tuple-element.53.inner, f32[7,128,512]{2,1,0:T(8,128)} %get-tuple-element.54.outer, ...), custom_call_target="tpu_custom_call" | custom-call | flops 32999999488 | bytes 108000000 | tf_op jit(solution)/shard_map/forward/pallas_call | solution.py:283
  93.1 8.2 %all-to-all-done.moved_ref = f32[8,800,128]{2,1,0:T(8,128)S(1)} async-done(((f32[8,800,128]{2,1,0:T(8,128)}), f32[8,800,128]{2,1,0:T(8,128)S(1)}, u32[]{:S(2)}, u32[]{:S(2)}) %all-to-all-start) | async-done | bytes 3276832 | tf_op jit(solution)/shard_map/all_to_all | solution.py:664
  101.3 1.7 copy-done
  103.0 7.1 %ratio.3 = (f32[24,128,128]{2,1,0:T(8,128)}, f32[24,128,128]{2,1,0:T(8,128)}, f32[15,128,128]{2,1,0:T(8,128)}, f32[15,128,128]{2,1,0:T(8,128)}, f32[24,128,128]{2,1,0:T(8,128)}) custom-call(s32[4]{0:T(128)} %pad_add_fusion.scalars, f32[8,800,128]{2,1,0:T(8,128)} %copy-done, f32[24,128,512]{2,1,0:T(8,128)} %forward.1.refs_0_.refs_1_.refs_2_.refs_3_, ...), custom_call_target="tpu_custom_call" | custom-call | flops 5500000256 | bytes 18000000 | tf_op jit(solution)/shard_map/ratio/pallas_call | solution.py:361
  110.1 2.4 collective-permute-start.6
  114.1 6.5 %all-to-all-start.1 = ((f32[8,384,128]{2,1,0:T(8,128)}), f32[8,384,128]{2,1,0:T(8,128)S(1)}, u32[]{:S(2)}, u32[]{:S(2)}) async-start(f32[8,384,128]{2,1,0:T(8,128)} %gate.4), calls=%async_computation.1 | async-start | bytes 3145728 | tf_op jit(solution)/shard_map/all_to_all | solution.py:664
  120.6 10.2 %collective-permute-done.6.outer = f32[15,128,128]{2,1,0:T(8,128)S(1)} collective-permute-done((f32[15,128,128]{2,1,0:T(8,128)}, f32[15,128,128]{2,1,0:T(8,128)S(1)}, u32[]{:S(2)}, u32[]{:S(2)}) %collective-permute-start.6) | collective-permute-done | bytes 983072 | tf_op jit(solution)/shard_map/ppermute | solution.py:660
  131.8 16.9 %back.3 = (bf16[24,128,128]{2,1,0:T(8,128)(2,1)}, bf16[24,128,128]{2,1,0:T(8,128)(2,1)}, f32[48,32,128]{2,1,0:T(8,128)}, f32[48,32,128]{2,1,0:T(8,128)}, f32[48,32,128]{2,1,0:T(8,128)}, /*index=5*/f32[48,32,128]{2,1,0:T(8,128)}) custom-call(s32[4]{0:T(128)} %pad_add_fusion.scalars, f32[15]{0:T(128)} %bitcast.9, f32[15,128,128]{2,1,0:T(8,128)} %copy-done.3, ...), custom_call_target="tpu_custom_call" | custom-call | flops 65999998976 | bytes 216000000 | tf_op jit(solution)/shard_map/back/pallas_call | solution.py:474
  148.7 1.6 collective-permute-start.9
  152.3 5.9 %all-to-all-done.1.moved_ref = f32[8,384,128]{2,1,0:T(8,128)S(1)} async-done(((f32[8,384,128]{2,1,0:T(8,128)}), f32[8,384,128]{2,1,0:T(8,128)S(1)}, u32[]{:S(2)}, u32[]{:S(2)}) %all-to-all-start.1) | async-done | bytes 1572896 | tf_op jit(solution)/shard_map/all_to_all | solution.py:664
  159.3 3.6 %ratio.4 = (f32[24,128,128]{2,1,0:T(8,128)}, f32[7,128,128]{2,1,0:T(8,128)}, f32[7,128,128]{2,1,0:T(8,128)}) custom-call(s32[4]{0:T(128)} %pad_add_fusion.scalars, f32[8,384,128]{2,1,0:T(8,128)} %copy-done.1, f32[24,128,512]{2,1,0:T(8,128)} %forward.1.refs_0_.refs_1_.refs_2_.refs_3_, bf16[24,128,128]{2,1,0:T(8,128)(2,1)} %get-tuple-element.64.refs_1_), custom_call_target="tpu_custom_call" | custom-call | flops 5500000256 | bytes 18000000 | tf_op jit(solution)/shard_map/ratio/pallas_call | solution.py:361
  162.8 3.3 %collective-permute-start.8 = (f32[7,128,128]{2,1,0:T(8,128)}, f32[7,128,128]{2,1,0:T(8,128)}, u32[]{:S(2)}, u32[]{:S(2)}) collective-permute-start(f32[7,128,128]{2,1,0:T(8,128)} %get-tuple-element.66), channel_id=1, source_target_pairs={{1,2},{3,4},{5,6},{2,1},{4,3},{6,5},{9,10},{11,12},{13,14},{10,9},... | collective-permute-start | bytes 1376264 | tf_op jit(solution)/shard_map/ppermute | solution.py:660
  166.1 1.7 collective-permute-done.9.b
  167.9 2.6 collective-permute-done.10.c
  170.5 15.4 %collective-permute-done.11.d = f32[48,32,128]{2,1,0:T(8,128)} collective-permute-done((f32[48,32,128]{2,1,0:T(8,128)}, f32[48,32,128]{2,1,0:T(8,128)}, u32[]{:S(2)}, u32[]{:S(2)}) %collective-permute-start.11) | collective-permute-done | bytes 786464 | tf_op jit(solution)/shard_map/ppermute | solution.py:641
  185.9 3.7 %merge.3.refs_3_ = f32[32,24,256]{2,1,0:T(8,128)} custom-call(s32[4]{0:T(128)} %pad_add_fusion.scalars, f32[128,24,512]{2,1,0:T(8,128)} %estimate_ref.5, f32[48,32,128]{2,1,0:T(8,128)} %get-tuple-element.69.a, f32[48,32,128]{2,1,0:T(8,128)} %copy-done.7, f32[48,32,128]{2,1,0:T(8,128)} %copy-done.8, f32[48,32,128]{2,1,0:T(8,128)} %collective-permute-done.11.d, ...), custom_call_target="tpu_custom_call" | custom-call | flops 32999999488 | bytes 108000000 | tf_op jit(solution)/shard_map/merge/pallas_call | solution.py:521
  190.4 6.4 %all-to-all-start.2 = ((f32[8,384,128]{2,1,0:T(8,128)}), f32[8,384,128]{2,1,0:T(8,128)S(1)}, u32[]{:S(2)}, u32[]{:S(2)}) async-start(f32[8,384,128]{2,1,0:T(8,128)} %gate.5), calls=%async_computation.2 | async-start | bytes 3145728 | tf_op jit(solution)/shard_map/all_to_all | solution.py:664
  196.8 9.0 %back.4 = (bf16[24,128,128]{2,1,0:T(8,128)(2,1)}, bf16[24,128,128]{2,1,0:T(8,128)(2,1)}, f32[24,32,128]{2,1,0:T(8,128)}, f32[24,32,128]{2,1,0:T(8,128)}, f32[24,32,128]{2,1,0:T(8,128)}, /*index=5*/f32[24,32,128]{2,1,0:T(8,128)}) custom-call(s32[4]{0:T(128)} %pad_add_fusion.scalars, f32[15]{0:T(128)} %bitcast.10, f32[7,128,128]{2,1,0:T(8,128)} %copy-done.12, ...), custom_call_target="tpu_custom_call" | custom-call | flops 65999998976 | bytes 216000000 | tf_op jit(solution)/shard_map/back/pallas_call | solution.py:474
  205.9 1.9 collective-permute-start.15
  207.8 1.6 collective-permute-start.16
  209.4 22.0 %all-to-all-done.2.moved_ref = f32[8,384,128]{2,1,0:T(8,128)S(1)} async-done(((f32[8,384,128]{2,1,0:T(8,128)}), f32[8,384,128]{2,1,0:T(8,128)S(1)}, u32[]{:S(2)}, u32[]{:S(2)}) %all-to-all-start.2) | async-done | bytes 1572896 | tf_op jit(solution)/shard_map/all_to_all | solution.py:664
  232.5 3.6 %ratio.5 = (f32[24,128,128]{2,1,0:T(8,128)}, f32[7,128,128]{2,1,0:T(8,128)}, f32[7,128,128]{2,1,0:T(8,128)}) custom-call(s32[4]{0:T(128)} %pad_add_fusion.scalars, f32[8,384,128]{2,1,0:T(8,128)} %copy-done.2, f32[24,128,512]{2,1,0:T(8,128)} %forward.1.refs_0_.refs_1_.refs_2_.refs_3_, bf16[24,128,128]{2,1,0:T(8,128)(2,1)} %get-tuple-element.73.refs_1_), custom_call_target="tpu_custom_call" | custom-call | flops 5500000256 | bytes 18000000 | tf_op jit(solution)/shard_map/ratio/pallas_call | solution.py:361
  236.1 2.4 collective-permute-start.13
  239.5 3.0 merge.4.refs_3_
  242.6 3.5 %collective-permute-done.13.outer = f32[7,128,128]{2,1,0:T(8,128)S(1)} collective-permute-done((f32[7,128,128]{2,1,0:T(8,128)}, f32[7,128,128]{2,1,0:T(8,128)S(1)}, u32[]{:S(2)}, u32[]{:S(2)}) %collective-permute-start.13) | collective-permute-done | bytes 458784 | tf_op jit(solution)/shard_map/ppermute | solution.py:660
  246.8 8.8 %back.5 = (bf16[24,128,128]{2,1,0:T(8,128)(2,1)}, bf16[24,128,128]{2,1,0:T(8,128)(2,1)}, f32[24,32,128]{2,1,0:T(8,128)}, f32[24,32,128]{2,1,0:T(8,128)}, f32[24,32,128]{2,1,0:T(8,128)}, /*index=5*/f32[24,32,128]{2,1,0:T(8,128)}) custom-call(s32[4]{0:T(128)} %pad_add_fusion.scalars, f32[15]{0:T(128)} %bitcast.11, f32[7,128,128]{2,1,0:T(8,128)} %copy-done.13, ...), custom_call_target="tpu_custom_call" | custom-call | flops 65999998976 | bytes 216000000 | tf_op jit(solution)/shard_map/back/pallas_call | solution.py:474
  255.9 1.9 collective-permute-start.18
  259.2 3.6 %assemble.3.after.refs_1_ = f32[128,24,512]{2,1,0:T(8,128)} custom-call(s32[4]{0:T(128)} %pad_add_fusion.scalars, f32[128,24,256]{2,1,0:T(8,128)} %all-gather.3.cloned.1.call-done.refs_0_, bf16[24,128,128]{2,1,0:T(8,128)(2,1)} %get-tuple-element.86.refs_1_), custom_call_target="tpu_custom_call" | custom-call | flops 11000000512 | bytes 36000000 | tf_op jit(solution)/shard_map/assemble/pallas_call | solution.py:558
  262.8 6.3 %collective-permute-done.17.b = f32[24,32,128]{2,1,0:T(8,128)S(1)} collective-permute-done((f32[24,32,128]{2,1,0:T(8,128)}, f32[24,32,128]{2,1,0:T(8,128)S(1)}, u32[]{:S(2)}, u32[]{:S(2)}) %collective-permute-start.17) | collective-permute-done | bytes 393248 | tf_op jit(solution)/shard_map/ppermute | solution.py:641
  269.2 15.2 %collective-permute-done.19.d = f32[24,32,128]{2,1,0:T(8,128)S(1)} collective-permute-done((f32[24,32,128]{2,1,0:T(8,128)}, f32[24,32,128]{2,1,0:T(8,128)S(1)}, u32[]{:S(2)}, u32[]{:S(2)}) %collective-permute-start.19) | collective-permute-done | bytes 393248 | tf_op jit(solution)/shard_map/ppermute | solution.py:641
  285.2 3.1 merge.5.refs_2_.refs_0_.refs_5_
  288.8 1.6 collective-permute-start.21
  291.7 2.6 assemble.4.refs_4_
  294.3 7.1 %collective-permute-done.22.refs_3_ = f32[32,24,128]{2,1,0:T(8,128)S(1)} collective-permute-done((f32[32,24,128]{2,1,0:T(8,128)}, f32[32,24,128]{2,1,0:T(8,128)S(1)}, u32[]{:S(2)}, u32[]{:S(2)}) %collective-permute-start.22) | collective-permute-done | bytes 393248 | tf_op jit(solution)/shard_map/ppermute | solution.py:641
  301.4 6.7 %collective-permute-done.21.refs_2_ = f32[32,24,128]{2,1,0:T(8,128)S(1)} collective-permute-done((f32[32,24,128]{2,1,0:T(8,128)}, f32[32,24,128]{2,1,0:T(8,128)S(1)}, u32[]{:S(2)}, u32[]{:S(2)}) %collective-permute-start.21) | collective-permute-done | bytes 393248 | tf_op jit(solution)/shard_map/ppermute | solution.py:641
  309.6 2.5 assemble.5
  (88 shorter events, 20.2 us)
Async XLA Ops:
  12.0 13.1 %collective-permute-start = (f32[32,8,512]{2,1,0:T(8,128)}, f32[32,8,512]{2,1,0:T(8,128)S(1)}, u32[]{:S(2)}, u32[]{:S(2)}) collective-permute-start(f32[32,8,512]{2,1,0:T(8,128)} %get-tuple-element.50), channel_id=1, source_target_pairs={{1,2},{3,4},{5,6},{2,1},{4,3},{6,5},{9,10},{11,12},{13,14},{10,9},... | collective-permute-start | bytes 1572872 | tf_op jit(solution)/shard_map/ppermute | solution.py:660
  13.9 52.0 %collective-permute-start.1 = (f32[128,8,512]{2,1,0:T(8,128)}, f32[128,8,512]{2,1,0:T(8,128)}, u32[]{:S(2)}, u32[]{:S(2)}) collective-permute-start(f32[128,8,512]{2,1,0:T(8,128)} %get-tuple-element.46.after), channel_id=1, source_target_pairs={{0,1},{1,0},{2,3},{3,2},{4,5},{5,4},{6,7},{7,6},{8,9},{9,8},{10,11... | collective-permute-start | bytes 6291464 | tf_op jit(solution)/shard_map/ppermute | solution.py:660
  25.1 0.8 copy-start.4
  25.9 4.3 %copy-start.24 = (s32[1,4]{1,0:T(1,128)S(1)}, s32[1,4]{1,0:T(1,128)}, u32[]{:S(2)}) copy-start(s32[1,4]{1,0:T(1,128)} %param.13) | copy-start | bytes 52
  25.9 75.4 %all-to-all-start = ((f32[8,800,128]{2,1,0:T(8,128)}), f32[8,800,128]{2,1,0:T(8,128)S(1)}, u32[]{:S(2)}, u32[]{:S(2)}) async-start(f32[8,800,128]{2,1,0:T(8,128)} %gate.3), calls=%async_computation | async-start | bytes 6553600 | tf_op jit(solution)/shard_map/all_to_all | solution.py:664
  31.5 8.2 %copy-start.5 = (f32[32,8,512]{2,1,0:T(8,128)S(1)}, f32[32,8,512]{2,1,0:T(8,128)}, u32[]{:S(2)}) copy-start(f32[32,8,512]{2,1,0:T(8,128)} %copy-done.4) | copy-start | bytes 1572868
  39.8 15.7 %collective-permute-start.4 = (f32[32,8,512]{2,1,0:T(8,128)S(1)}, f32[32,8,512]{2,1,0:T(8,128)S(1)}, u32[]{:S(2)}, u32[]{:S(2)}) collective-permute-start(f32[32,8,512]{2,1,0:T(8,128)S(1)} %copy-done.5), channel_id=1, source_target_pairs={{0,24},{8,16},{16,8},{24,0},{1,25},{9,17},{17,9},{25,1},{2,26},{10... | collective-permute-start | bytes 1572872 | tf_op jit(solution)/shard_map/ppermute | solution.py:641
  42.2 23.7 %collective-permute-start.3 = (f32[32,8,512]{2,1,0:T(8,128)S(1)}, f32[32,8,512]{2,1,0:T(8,128)S(1)}, u32[]{:S(2)}, u32[]{:S(2)}) collective-permute-start(f32[32,8,512]{2,1,0:T(8,128)S(1)} %copy-done.5), channel_id=1, source_target_pairs={{0,16},{8,24},{16,0},{24,8},{1,17},{9,25},{17,1},{25,9},{2,18},{10... | collective-permute-start | bytes 1572872 | tf_op jit(solution)/shard_map/ppermute | solution.py:641
  42.7 23.3 %collective-permute-start.2 = (f32[32,8,512]{2,1,0:T(8,128)S(1)}, f32[32,8,512]{2,1,0:T(8,128)S(1)}, u32[]{:S(2)}, u32[]{:S(2)}) collective-permute-start(f32[32,8,512]{2,1,0:T(8,128)S(1)} %copy-done.5), channel_id=1, source_target_pairs={{0,8},{8,0},{16,24},{24,16},{1,9},{9,1},{17,25},{25,17},{2,10},{10... | collective-permute-start | bytes 1572872 | tf_op jit(solution)/shard_map/ppermute | solution.py:641
  55.5 10.5 %copy-start.9 = (f32[32,8,512]{2,1,0:T(8,128)}, f32[32,8,512]{2,1,0:T(8,128)S(1)}, u32[]{:S(2)}) copy-start(f32[32,8,512]{2,1,0:T(8,128)S(1)} %collective-permute-done.4.d) | copy-start | bytes 1572868
  65.9 0.8 copy-start.10
  66.0 0.9 copy-start.11
  93.1 19.5 %copy-start.25 = (f32[1,15]{1,0:T(1,128)S(1)}, f32[1,15]{1,0:T(1,128)}, u32[]{:S(2)}) copy-start(f32[1,15]{1,0:T(1,128)} %profile_y.1) | copy-start | bytes 184
  101.3 1.7 copy-start
  110.1 3.0 collective-permute-start.5
  110.1 20.7 %collective-permute-start.6 = (f32[15,128,128]{2,1,0:T(8,128)}, f32[15,128,128]{2,1,0:T(8,128)S(1)}, u32[]{:S(2)}, u32[]{:S(2)}) collective-permute-start(f32[15,128,128]{2,1,0:T(8,128)} %get-tuple-element.59), channel_id=1, source_target_pairs={{1,2},{3,4},{5,6},{2,1},{4,3},{6,5},{9,10},{11,12},{13,14},{10,9},... | collective-permute-start | bytes 2949128 | tf_op jit(solution)/shard_map/ppermute | solution.py:660
  113.1 0.9 copy-start.3
  114.1 44.0 %all-to-all-start.1 = ((f32[8,384,128]{2,1,0:T(8,128)}), f32[8,384,128]{2,1,0:T(8,128)S(1)}, u32[]{:S(2)}, u32[]{:S(2)}) async-start(f32[8,384,128]{2,1,0:T(8,128)} %gate.4), calls=%async_computation.1 | async-start | bytes 3145728 | tf_op jit(solution)/shard_map/all_to_all | solution.py:664
  120.6 138.5 %all-gather.3.cloned.1.call-start = ((), (), s32[]{:S(2)}) async-start(), calls=%async_computation.3 | async-start | bytes 3932160 | tf_op jit(solution)/shard_map/all_gather | solution.py:669
  130.8 1.0 copy-start.6
  148.7 19.1 %collective-permute-start.9 = (f32[48,32,128]{2,1,0:T(8,128)}, f32[48,32,128]{2,1,0:T(8,128)S(1)}, u32[]{:S(2)}, u32[]{:S(2)}) collective-permute-start(f32[48,32,128]{2,1,0:T(8,128)} %get-tuple-element.70), channel_id=1, source_target_pairs={{0,8},{8,0},{16,24},{24,16},{1,9},{9,1},{17,25},{25,17},{2,10},{10... | collective-permute-start | bytes 2359304 | tf_op jit(solution)/shard_map/ppermute | solution.py:641
  150.3 20.2 %collective-permute-start.10 = (f32[48,32,128]{2,1,0:T(8,128)}, f32[48,32,128]{2,1,0:T(8,128)S(1)}, u32[]{:S(2)}, u32[]{:S(2)}) collective-permute-start(f32[48,32,128]{2,1,0:T(8,128)} %get-tuple-element.71), channel_id=1, source_target_pairs={{0,16},{8,24},{16,0},{24,8},{1,17},{9,25},{17,1},{25,9},{2,18},{10... | collective-permute-start | bytes 2359304 | tf_op jit(solution)/shard_map/ppermute | solution.py:641
  151.8 34.1 %collective-permute-start.11 = (f32[48,32,128]{2,1,0:T(8,128)}, f32[48,32,128]{2,1,0:T(8,128)}, u32[]{:S(2)}, u32[]{:S(2)}) collective-permute-start(f32[48,32,128]{2,1,0:T(8,128)} %get-tuple-element.72), channel_id=1, source_target_pairs={{0,24},{8,16},{16,8},{24,0},{1,25},{9,17},{17,9},{25,1},{2,26},{10... | collective-permute-start | bytes 2359304 | tf_op jit(solution)/shard_map/ppermute | solution.py:641
  158.1 1.1 copy-start.1
  162.8 26.8 %collective-permute-start.7 = (f32[7,128,128]{2,1,0:T(8,128)}, f32[7,128,128]{2,1,0:T(8,128)S(1)}, u32[]{:S(2)}, u32[]{:S(2)}) collective-permute-start(f32[7,128,128]{2,1,0:T(8,128)} %get-tuple-element.65), channel_id=1, source_target_pairs={{0,1},{1,0},{2,3},{3,2},{4,5},{5,4},{6,7},{7,6},{8,9},{9,8},{10,11... | collective-permute-start | bytes 1376264 | tf_op jit(solution)/shard_map/ppermute | solution.py:660
  162.8 33.9 %collective-permute-start.8 = (f32[7,128,128]{2,1,0:T(8,128)}, f32[7,128,128]{2,1,0:T(8,128)}, u32[]{:S(2)}, u32[]{:S(2)}) collective-permute-start(f32[7,128,128]{2,1,0:T(8,128)} %get-tuple-element.66), channel_id=1, source_target_pairs={{1,2},{3,4},{5,6},{2,1},{4,3},{6,5},{9,10},{11,12},{13,14},{10,9},... | collective-permute-start | bytes 1376264 | tf_op jit(solution)/shard_map/ppermute | solution.py:660
  167.8 18.0 %copy-start.7 = (f32[48,32,128]{2,1,0:T(8,128)}, f32[48,32,128]{2,1,0:T(8,128)S(1)}, u32[]{:S(2)}) copy-start(f32[48,32,128]{2,1,0:T(8,128)S(1)} %collective-permute-done.9.b) | copy-start | bytes 2359300
  170.5 15.4 %copy-start.8 = (f32[48,32,128]{2,1,0:T(8,128)}, f32[48,32,128]{2,1,0:T(8,128)S(1)}, u32[]{:S(2)}) copy-start(f32[48,32,128]{2,1,0:T(8,128)S(1)} %collective-permute-done.10.c) | copy-start | bytes 2359300
  190.4 41.0 %all-to-all-start.2 = ((f32[8,384,128]{2,1,0:T(8,128)}), f32[8,384,128]{2,1,0:T(8,128)S(1)}, u32[]{:S(2)}, u32[]{:S(2)}) async-start(f32[8,384,128]{2,1,0:T(8,128)} %gate.5), calls=%async_computation.2 | async-start | bytes 3145728 | tf_op jit(solution)/shard_map/all_to_all | solution.py:664
  196.8 95.0 %all-gather.5.cloned.1.call-start = ((), (), s32[]{:S(2)}) async-start(), calls=%async_computation.4 | async-start | bytes 1966080 | tf_op jit(solution)/shard_map/all_gather | solution.py:669
  205.8 32.6 %collective-permute-start.14 = (f32[24,32,128]{2,1,0:T(8,128)}, f32[24,32,128]{2,1,0:T(8,128)S(1)}, u32[]{:S(2)}, u32[]{:S(2)}) collective-permute-start(f32[24,32,128]{2,1,0:T(8,128)} %get-tuple-element.79), channel_id=1, source_target_pairs={{0,8},{8,0},{16,24},{24,16},{1,9},{9,1},{17,25},{25,17},{2,10},{10... | collective-permute-start | bytes 1179656 | tf_op jit(solution)/shard_map/ppermute | solution.py:641
  205.9 32.6 %collective-permute-start.15 = (f32[24,32,128]{2,1,0:T(8,128)}, f32[24,32,128]{2,1,0:T(8,128)S(1)}, u32[]{:S(2)}, u32[]{:S(2)}) collective-permute-start(f32[24,32,128]{2,1,0:T(8,128)} %get-tuple-element.80), channel_id=1, source_target_pairs={{0,16},{8,24},{16,0},{24,8},{1,17},{9,25},{17,1},{25,9},{2,18},{10... | collective-permute-start | bytes 1179656 | tf_op jit(solution)/shard_map/ppermute | solution.py:641
  207.8 30.7 %collective-permute-start.16 = (f32[24,32,128]{2,1,0:T(8,128)}, f32[24,32,128]{2,1,0:T(8,128)S(1)}, u32[]{:S(2)}, u32[]{:S(2)}) collective-permute-start(f32[24,32,128]{2,1,0:T(8,128)} %get-tuple-element.81), channel_id=1, source_target_pairs={{0,24},{8,16},{16,8},{24,0},{1,25},{9,17},{17,9},{25,1},{2,26},{10... | collective-permute-start | bytes 1179656 | tf_op jit(solution)/shard_map/ppermute | solution.py:641
  231.3 1.1 copy-start.2
  236.1 6.5 %collective-permute-start.12 = (f32[7,128,128]{2,1,0:T(8,128)}, f32[7,128,128]{2,1,0:T(8,128)S(1)}, u32[]{:S(2)}, u32[]{:S(2)}) collective-permute-start(f32[7,128,128]{2,1,0:T(8,128)} %get-tuple-element.74), channel_id=1, source_target_pairs={{0,1},{1,0},{2,3},{3,2},{4,5},{5,4},{6,7},{7,6},{8,9},{9,8},{10,11... | collective-permute-start | bytes 1376264 | tf_op jit(solution)/shard_map/ppermute | solution.py:660
  236.1 10.0 %collective-permute-start.13 = (f32[7,128,128]{2,1,0:T(8,128)}, f32[7,128,128]{2,1,0:T(8,128)S(1)}, u32[]{:S(2)}, u32[]{:S(2)}) collective-permute-start(f32[7,128,128]{2,1,0:T(8,128)} %get-tuple-element.75), channel_id=1, source_target_pairs={{1,2},{3,4},{5,6},{2,1},{4,3},{6,5},{9,10},{11,12},{13,14},{10,9},... | collective-permute-start | bytes 1376264 | tf_op jit(solution)/shard_map/ppermute | solution.py:660
  238.5 0.9 copy-start.16
  238.5 1.0 copy-start.17
  242.5 3.5 %copy-start.13 = (f32[7,128,128]{2,1,0:T(8,128)}, f32[7,128,128]{2,1,0:T(8,128)S(1)}, u32[]{:S(2)}) copy-start(f32[7,128,128]{2,1,0:T(8,128)S(1)} %collective-permute-done.12.inner) | copy-start | bytes 1376260
  255.6 13.5 %collective-permute-start.17 = (f32[24,32,128]{2,1,0:T(8,128)}, f32[24,32,128]{2,1,0:T(8,128)S(1)}, u32[]{:S(2)}, u32[]{:S(2)}) collective-permute-start(f32[24,32,128]{2,1,0:T(8,128)} %get-tuple-element.83), channel_id=1, source_target_pairs={{0,8},{8,0},{16,24},{24,16},{1,9},{9,1},{17,25},{25,17},{2,10},{10... | collective-permute-start | bytes 1179656 | tf_op jit(solution)/shard_map/ppermute | solution.py:641
  255.9 13.3 %collective-permute-start.18 = (f32[24,32,128]{2,1,0:T(8,128)}, f32[24,32,128]{2,1,0:T(8,128)S(1)}, u32[]{:S(2)}, u32[]{:S(2)}) collective-permute-start(f32[24,32,128]{2,1,0:T(8,128)} %get-tuple-element.84), channel_id=1, source_target_pairs={{0,16},{8,24},{16,0},{24,8},{1,17},{9,25},{17,1},{25,9},{2,18},{10... | collective-permute-start | bytes 1179656 | tf_op jit(solution)/shard_map/ppermute | solution.py:641
  257.8 26.7 %collective-permute-start.19 = (f32[24,32,128]{2,1,0:T(8,128)}, f32[24,32,128]{2,1,0:T(8,128)S(1)}, u32[]{:S(2)}, u32[]{:S(2)}) collective-permute-start(f32[24,32,128]{2,1,0:T(8,128)} %get-tuple-element.85), channel_id=1, source_target_pairs={{0,24},{8,16},{16,8},{24,0},{1,25},{9,17},{17,9},{25,1},{2,26},{10... | collective-permute-start | bytes 1179656 | tf_op jit(solution)/shard_map/ppermute | solution.py:641
  269.1 15.4 %copy-start.18 = (f32[24,32,128]{2,1,0:T(8,128)}, f32[24,32,128]{2,1,0:T(8,128)S(1)}, u32[]{:S(2)}) copy-start(f32[24,32,128]{2,1,0:T(8,128)S(1)} %collective-permute-done.17.b) | copy-start | bytes 1179652
  269.2 15.2 %copy-start.19 = (f32[24,32,128]{2,1,0:T(8,128)}, f32[24,32,128]{2,1,0:T(8,128)S(1)}, u32[]{:S(2)}) copy-start(f32[24,32,128]{2,1,0:T(8,128)S(1)} %collective-permute-done.18.c) | copy-start | bytes 1179652
  288.3 13.1 %collective-permute-start.22 = (f32[32,24,128]{2,1,0:T(8,128)}, f32[32,24,128]{2,1,0:T(8,128)S(1)}, u32[]{:S(2)}, u32[]{:S(2)}) collective-permute-start(f32[32,24,128]{2,1,0:T(8,128)} %merge.5.refs_2_.refs_0_.refs_5_), channel_id=1, source_target_pairs={{0,24},{8,16},{16,8},{24,0},{1,25},{9,17},{17,9},{25,1},{2,26},{10... | collective-permute-start | bytes 1179656 | tf_op jit(solution)/shard_map/ppermute | solution.py:641
  288.8 19.3 %collective-permute-start.21 = (f32[32,24,128]{2,1,0:T(8,128)}, f32[32,24,128]{2,1,0:T(8,128)S(1)}, u32[]{:S(2)}, u32[]{:S(2)}) collective-permute-start(f32[32,24,128]{2,1,0:T(8,128)} %merge.5.refs_2_.refs_0_.refs_5_), channel_id=1, source_target_pairs={{0,16},{8,24},{16,0},{24,8},{1,17},{9,25},{17,1},{25,9},{2,18},{10... | collective-permute-start | bytes 1179656 | tf_op jit(solution)/shard_map/ppermute | solution.py:641
  290.4 17.7 %collective-permute-start.20 = (f32[32,24,128]{2,1,0:T(8,128)}, f32[32,24,128]{2,1,0:T(8,128)S(1)}, u32[]{:S(2)}, u32[]{:S(2)}) collective-permute-start(f32[32,24,128]{2,1,0:T(8,128)} %merge.5.refs_2_.refs_0_.refs_5_), channel_id=1, source_target_pairs={{0,8},{8,0},{16,24},{24,16},{1,9},{9,1},{17,25},{25,17},{2,10},{10... | collective-permute-start | bytes 1179656 | tf_op jit(solution)/shard_map/ppermute | solution.py:641
  301.4 6.7 %copy-start.20 = (f32[32,24,128]{2,1,0:T(8,128)}, f32[32,24,128]{2,1,0:T(8,128)S(1)}, u32[]{:S(2)}) copy-start(f32[32,24,128]{2,1,0:T(8,128)S(1)} %collective-permute-done.22.refs_3_) | copy-start | bytes 1179652
  (6 other events, 4.5 us)
Sparse Core Ops, SparseCore 0:
  189.7 54.8 all-gather.2
  246.4 40.6 all-gather.4

commit v4 on v3

--- a/solution.py
+++ b/solution.py
@@ -274,7 +274,7 @@
         out_ref[pl.ds(index * group, group)] = result.reshape(group, planes, cells)
         return carry
 
-    lax.fori_loop(0, rows // group, step_zx, 0, unroll=3)
+    lax.fori_loop(0, rows // group, step_zx, 0, unroll=6)
 
 
 def forward(even, weights, own, inner, outer, along_z, high_x, low_x, after):
@@ -395,7 +395,7 @@
                 halves[r // 2, pl.ds(planes + planes_at, 16), lanes] = low
             return carry
 
-        lax.fori_loop(0, planes_count // 16, step_y, 0)
+        lax.fori_loop(0, planes_count // 16, step_y, 0, unroll=2)
 
     def blur_planes(slot, number):
         def step_zx(index, carry):
@@ -422,7 +422,7 @@
                 totals[pl.ds(number * rows + index * group, group)] = result.reshape(group, planes, LANES)
             return carry
 
-        lax.fori_loop(0, rows // group, step_zx, 0, unroll=3)
+        lax.fori_loop(0, rows // group, step_zx, 0, unroll=6)
 
     loads = [
         place_rows(even, own, inner, outer, number * half, buffers.at[number], sems.at[number], half)

time: 320 us -> 318 us (level)
  transfers between devices with their start and end apart: 28 -> 28, of which waited for: 16 -> 16; matrix products, arithmetic and copies ran while one was open for 1% -> 1% of each run, Pallas kernels for 33% -> 32%
where the time goes in v4:
time: 318 us; the launch traced here: 316 us
  waiting for transfers between devices  124 us (39%)
  Pallas kernels  116 us (36%)
  starting transfers between devices  45.9 us (14%)
  between operations  14.3 us (4%)
  local copies, waits for them, and re-layouts  13.7 us (4%)
    ppermute x15, waiting for transfers between devices, swap_views(): return lax.ppermute(cells, 'view', [(i, i ^ mask) for i in range(4)])  71.2 us
    all_to_all x3, waiting for transfers between devices, move(): return lax.all_to_all(cells, 'tile', split_axis=0, concat_axis=0)  38.6 us
    pallas_call x3, Pallas kernels, back(): pl.pallas_call(functools.partial(back_kernel, taps, count, first), grid=(...  31.5 us
    pallas_call x1, Pallas kernels, forward(): pl.pallas_call(functools.partial(forward_kernel, taps), in_specs=[SMEM, S...  20 us
    ppermute x15, starting transfers between devices, swap_views(): return lax.ppermute(cells, 'view', [(i, i ^ mask) for i in range(4)])  17.6 us
    all_to_all x3, starting transfers between devices, move(): return lax.all_to_all(cells, 'tile', split_axis=0, concat_axis=0)  17.3 us
    pallas_call x3, Pallas kernels, ratio(): pl.pallas_call(functools.partial(ratio_kernel, half, chunks, first), grid...  14.3 us
    ppermute x4, waiting for transfers between devices, exchange(): lax.ppermute(outer, 'tile', outer_pairs)  13.7 us
  transfers between devices with their start and end apart: 28, of which 16 were waited for; matrix products, arithmetic and copies ran while one was open for 1% of the time, Pallas kernels for 32%

profile of v4, /device:TPU:16, one launch (start us, length us, event | category | flops | bytes accessed | tf_op | source)
XLA Modules:
  0.0 316.3 jit_solution(7001155654512788471)
XLA Ops:
  7.1 4.9 %edge_rows.1 = (f32[128,8,512]{2,1,0:T(8,128)}, f32[32,8,512]{2,1,0:T(8,128)}) custom-call(s32[2]{0:T(128)} %pad_add_fusion.1.scalars, f32[128,24,512]{2,1,0:T(8,128)} %estimate_ref.5, f32[128,24,512]{2,1,0:T(8,128)} %estimate_ref.5), custom_call_target="tpu_custom_call" | custom-call | flops 5500000256 | bytes 18000000 | tf_op jit(solution)/shard_map/edge_rows/pallas_call | solution.py:116
  12.0 1.9 collective-permute-start
  13.9 1.7 collective-permute-start.1
  16.3 8.8 %prep.1 = (f32[8,800,128]{2,1,0:T(8,128)}, f32[8,384,128]{2,1,0:T(8,128)}, f32[8,384,128]{2,1,0:T(8,128)}, f32[8,128]{1,0:T(8,128)}) custom-call(s32[1]{0:T(128)S(6)} %copy.18.offsets, f32[16,192,512]{2,1,0:T(8,128)} %bitcast.7, f32[128,8,512]{2,1,0:T(8,128)} %get-tuple-element.46.after), custom_call_target="tpu_custom_call" | custom-call | flops 9900000256 | bytes 32400000 | tf_op jit(solution)/shard_map/prep/pallas_call | solution.py:91
  25.9 4.3 %all-to-all-start = ((f32[8,800,128]{2,1,0:T(8,128)}), f32[8,800,128]{2,1,0:T(8,128)S(1)}, u32[]{:S(2)}, u32[]{:S(2)}) async-start(f32[8,800,128]{2,1,0:T(8,128)} %gate.3), calls=%async_computation | async-start | bytes 6553600 | tf_op jit(solution)/shard_map/all_to_all | solution.py:664
  31.5 8.2 %swap.1.after.own = f32[24,128,512]{2,1,0:T(8,128)} custom-call(f32[128,24,512]{2,1,0:T(8,128)} %estimate_ref.5, f32[8,128]{1,0:T(8,128)} %get-tuple-element.51.after), custom_call_target="tpu_custom_call" | custom-call | flops 8800000000 | bytes 28800000 | tf_op jit(solution)/shard_map/swap/pallas_call | solution.py:143
  39.8 2.4 collective-permute-start.4
  43.2 1.9 pad_add_fusion.scalars
  45.1 3.6 %bands.1 = (bf16[256,256]{1,0:T(8,128)(2,1)}, bf16[256,256]{1,0:T(8,128)(2,1)}, bf16[512,512]{1,0:T(8,128)(2,1)}, bf16[512,512]{1,0:T(8,128)(2,1)}, bf16[4,256,256]{2,1,0:T(8,128)(2,1)}) custom-call(s32[4]{0:T(128)} %pad_add_fusion.scalars, f32[1,31]{1,0:T(1,128)} %profile_z.1, f32[1,15]{1,0:T(1,128)} %profile_y.1, f32[1,15]{1,0:T(1,128)} %profile_x.1, ...), custom_call_target="tpu_custom_call" | custom-call | flops 4400000000 | bytes 14400000 | tf_op jit(solution)/shard_map/bands/pallas_call | solution.py:623
  48.7 6.8 %collective-permute-done.4.d = f32[32,8,512]{2,1,0:T(8,128)S(1)} collective-permute-done((f32[32,8,512]{2,1,0:T(8,128)S(1)}, f32[32,8,512]{2,1,0:T(8,128)S(1)}, u32[]{:S(2)}, u32[]{:S(2)}) %collective-permute-start.4) | collective-permute-done | bytes 524320 | tf_op jit(solution)/shard_map/ppermute | solution.py:641
  55.5 10.4 %collective-permute-done.3.c = f32[32,8,512]{2,1,0:T(8,128)S(1)} collective-permute-done((f32[32,8,512]{2,1,0:T(8,128)S(1)}, f32[32,8,512]{2,1,0:T(8,128)S(1)}, u32[]{:S(2)}, u32[]{:S(2)}) %collective-permute-start.3) | collective-permute-done | bytes 524320 | tf_op jit(solution)/shard_map/ppermute | solution.py:641
  66.9 6.0 %swap_edges.1 = (f32[7,128,512]{2,1,0:T(8,128)}, f32[7,128,512]{2,1,0:T(8,128)}) custom-call(s32[2]{0:T(128)} %pad_add_fusion.1.scalars, f32[128,8,512]{2,1,0:T(8,128)} %collective-permute-done.1.inner_ref, f32[32,8,512]{2,1,0:T(8,128)} %copy-done.4, f32[32,8,512]{2,1,0:T(8,128)} %copy-done.11, f32[32,8,512]{2,1,0:T(8,128)} %copy-done.10, ...), custom_call_target="tpu_custom_call" | custom-call | flops 6600000000 | bytes 21600000 | tf_op jit(solution)/shard_map/swap_edges/pallas_call | solution.py:171
  72.9 20.0 %forward.1.refs_0_.refs_1_.refs_2_.refs_3_ = f32[24,128,512]{2,1,0:T(8,128)} custom-call(s32[4]{0:T(128)} %pad_add_fusion.scalars, f32[15]{0:T(128)} %bitcast.8, f32[24,128,512]{2,1,0:T(8,128)} %swap.1.after.own, f32[7,128,512]{2,1,0:T(8,128)} %get-tuple-element.53.inner, f32[7,128,512]{2,1,0:T(8,128)} %get-tuple-element.54.outer, ...), custom_call_target="tpu_custom_call" | custom-call | flops 32999999488 | bytes 108000000 | tf_op jit(solution)/shard_map/forward/pallas_call | solution.py:283
  92.9 8.4 %all-to-all-done.moved_ref = f32[8,800,128]{2,1,0:T(8,128)S(1)} async-done(((f32[8,800,128]{2,1,0:T(8,128)}), f32[8,800,128]{2,1,0:T(8,128)S(1)}, u32[]{:S(2)}, u32[]{:S(2)}) %all-to-all-start) | async-done | bytes 3276832 | tf_op jit(solution)/shard_map/all_to_all | solution.py:664
  101.3 1.7 copy-done
  103.0 7.1 %ratio.3 = (f32[24,128,128]{2,1,0:T(8,128)}, f32[24,128,128]{2,1,0:T(8,128)}, f32[15,128,128]{2,1,0:T(8,128)}, f32[15,128,128]{2,1,0:T(8,128)}, f32[24,128,128]{2,1,0:T(8,128)}) custom-call(s32[4]{0:T(128)} %pad_add_fusion.scalars, f32[8,800,128]{2,1,0:T(8,128)} %copy-done, f32[24,128,512]{2,1,0:T(8,128)} %forward.1.refs_0_.refs_1_.refs_2_.refs_3_, ...), custom_call_target="tpu_custom_call" | custom-call | flops 5500000256 | bytes 18000000 | tf_op jit(solution)/shard_map/ratio/pallas_call | solution.py:361
  110.1 2.4 collective-permute-start.6
  114.1 6.5 %all-to-all-start.1 = ((f32[8,384,128]{2,1,0:T(8,128)}), f32[8,384,128]{2,1,0:T(8,128)S(1)}, u32[]{:S(2)}, u32[]{:S(2)}) async-start(f32[8,384,128]{2,1,0:T(8,128)} %gate.4), calls=%async_computation.1 | async-start | bytes 3145728 | tf_op jit(solution)/shard_map/all_to_all | solution.py:664
  120.6 10.2 %collective-permute-done.6.outer = f32[15,128,128]{2,1,0:T(8,128)S(1)} collective-permute-done((f32[15,128,128]{2,1,0:T(8,128)}, f32[15,128,128]{2,1,0:T(8,128)S(1)}, u32[]{:S(2)}, u32[]{:S(2)}) %collective-permute-start.6) | collective-permute-done | bytes 983072 | tf_op jit(solution)/shard_map/ppermute | solution.py:660
  131.8 15.3 %back.3 = (bf16[24,128,128]{2,1,0:T(8,128)(2,1)}, bf16[24,128,128]{2,1,0:T(8,128)(2,1)}, f32[48,32,128]{2,1,0:T(8,128)}, f32[48,32,128]{2,1,0:T(8,128)}, f32[48,32,128]{2,1,0:T(8,128)}, /*index=5*/f32[48,32,128]{2,1,0:T(8,128)}) custom-call(s32[4]{0:T(128)} %pad_add_fusion.scalars, f32[15]{0:T(128)} %bitcast.9, f32[15,128,128]{2,1,0:T(8,128)} %copy-done.3, ...), custom_call_target="tpu_custom_call" | custom-call | flops 65999998976 | bytes 216000000 | tf_op jit(solution)/shard_map/back/pallas_call | solution.py:474
  147.1 1.6 collective-permute-start.9
  148.7 1.5 collective-permute-start.10
  150.7 7.5 %all-to-all-done.1.moved_ref = f32[8,384,128]{2,1,0:T(8,128)S(1)} async-done(((f32[8,384,128]{2,1,0:T(8,128)}), f32[8,384,128]{2,1,0:T(8,128)S(1)}, u32[]{:S(2)}, u32[]{:S(2)}) %all-to-all-start.1) | async-done | bytes 1572896 | tf_op jit(solution)/shard_map/all_to_all | solution.py:664
  159.3 3.6 %ratio.4 = (f32[24,128,128]{2,1,0:T(8,128)}, f32[7,128,128]{2,1,0:T(8,128)}, f32[7,128,128]{2,1,0:T(8,128)}) custom-call(s32[4]{0:T(128)} %pad_add_fusion.scalars, f32[8,384,128]{2,1,0:T(8,128)} %copy-done.1, f32[24,128,512]{2,1,0:T(8,128)} %forward.1.refs_0_.refs_1_.refs_2_.refs_3_, bf16[24,128,128]{2,1,0:T(8,128)(2,1)} %get-tuple-element.64.refs_1_), custom_call_target="tpu_custom_call" | custom-call | flops 5500000256 | bytes 18000000 | tf_op jit(solution)/shard_map/ratio/pallas_call | solution.py:361
  162.8 2.6 collective-permute-start.8
  166.2 2.6 collective-permute-done.10.c
  168.9 15.4 %collective-permute-done.11.d = f32[48,32,128]{2,1,0:T(8,128)} collective-permute-done((f32[48,32,128]{2,1,0:T(8,128)}, f32[48,32,128]{2,1,0:T(8,128)}, u32[]{:S(2)}, u32[]{:S(2)}) %collective-permute-start.11) | collective-permute-done | bytes 786464 | tf_op jit(solution)/shard_map/ppermute | solution.py:641
  184.2 3.7 %merge.3.refs_3_ = f32[32,24,256]{2,1,0:T(8,128)} custom-call(s32[4]{0:T(128)} %pad_add_fusion.scalars, f32[128,24,512]{2,1,0:T(8,128)} %estimate_ref.5, f32[48,32,128]{2,1,0:T(8,128)} %get-tuple-element.69.a, f32[48,32,128]{2,1,0:T(8,128)} %copy-done.7, f32[48,32,128]{2,1,0:T(8,128)} %copy-done.8, f32[48,32,128]{2,1,0:T(8,128)} %collective-permute-done.11.d, ...), custom_call_target="tpu_custom_call" | custom-call | flops 32999999488 | bytes 108000000 | tf_op jit(solution)/shard_map/merge/pallas_call | solution.py:521
  188.8 6.4 %all-to-all-start.2 = ((f32[8,384,128]{2,1,0:T(8,128)}), f32[8,384,128]{2,1,0:T(8,128)S(1)}, u32[]{:S(2)}, u32[]{:S(2)}) async-start(f32[8,384,128]{2,1,0:T(8,128)} %gate.5), calls=%async_computation.2 | async-start | bytes 3145728 | tf_op jit(solution)/shard_map/all_to_all | solution.py:664
  195.2 8.3 %back.4 = (bf16[24,128,128]{2,1,0:T(8,128)(2,1)}, bf16[24,128,128]{2,1,0:T(8,128)(2,1)}, f32[24,32,128]{2,1,0:T(8,128)}, f32[24,32,128]{2,1,0:T(8,128)}, f32[24,32,128]{2,1,0:T(8,128)}, /*index=5*/f32[24,32,128]{2,1,0:T(8,128)}) custom-call(s32[4]{0:T(128)} %pad_add_fusion.scalars, f32[15]{0:T(128)} %bitcast.10, f32[7,128,128]{2,1,0:T(8,128)} %copy-done.12, ...), custom_call_target="tpu_custom_call" | custom-call | flops 65999998976 | bytes 216000000 | tf_op jit(solution)/shard_map/back/pallas_call | solution.py:474
  203.5 1.9 collective-permute-start.15
  205.4 1.6 collective-permute-start.16
  207.0 22.7 %all-to-all-done.2.moved_ref = f32[8,384,128]{2,1,0:T(8,128)S(1)} async-done(((f32[8,384,128]{2,1,0:T(8,128)}), f32[8,384,128]{2,1,0:T(8,128)S(1)}, u32[]{:S(2)}, u32[]{:S(2)}) %all-to-all-start.2) | async-done | bytes 1572896 | tf_op jit(solution)/shard_map/all_to_all | solution.py:664
  230.9 3.6 %ratio.5 = (f32[24,128,128]{2,1,0:T(8,128)}, f32[7,128,128]{2,1,0:T(8,128)}, f32[7,128,128]{2,1,0:T(8,128)}) custom-call(s32[4]{0:T(128)} %pad_add_fusion.scalars, f32[8,384,128]{2,1,0:T(8,128)} %copy-done.2, f32[24,128,512]{2,1,0:T(8,128)} %forward.1.refs_0_.refs_1_.refs_2_.refs_3_, bf16[24,128,128]{2,1,0:T(8,128)(2,1)} %get-tuple-element.73.refs_1_), custom_call_target="tpu_custom_call" | custom-call | flops 5500000256 | bytes 18000000 | tf_op jit(solution)/shard_map/ratio/pallas_call | solution.py:361
  234.4 2.4 collective-permute-start.13
  237.8 3.0 merge.4.refs_3_
  240.9 3.5 %collective-permute-done.13.outer = f32[7,128,128]{2,1,0:T(8,128)S(1)} collective-permute-done((f32[7,128,128]{2,1,0:T(8,128)}, f32[7,128,128]{2,1,0:T(8,128)S(1)}, u32[]{:S(2)}, u32[]{:S(2)}) %collective-permute-start.13) | collective-permute-done | bytes 458784 | tf_op jit(solution)/shard_map/ppermute | solution.py:660
  245.2 8.0 %back.5 = (bf16[24,128,128]{2,1,0:T(8,128)(2,1)}, bf16[24,128,128]{2,1,0:T(8,128)(2,1)}, f32[24,32,128]{2,1,0:T(8,128)}, f32[24,32,128]{2,1,0:T(8,128)}, f32[24,32,128]{2,1,0:T(8,128)}, /*index=5*/f32[24,32,128]{2,1,0:T(8,128)}) custom-call(s32[4]{0:T(128)} %pad_add_fusion.scalars, f32[15]{0:T(128)} %bitcast.11, f32[7,128,128]{2,1,0:T(8,128)} %copy-done.13, ...), custom_call_target="tpu_custom_call" | custom-call | flops 65999998976 | bytes 216000000 | tf_op jit(solution)/shard_map/back/pallas_call | solution.py:474
  253.5 1.9 collective-permute-start.18
  256.8 3.6 %assemble.3.after.refs_1_ = f32[128,24,512]{2,1,0:T(8,128)} custom-call(s32[4]{0:T(128)} %pad_add_fusion.scalars, f32[128,24,256]{2,1,0:T(8,128)} %all-gather.3.cloned.1.call-done.refs_0_, bf16[24,128,128]{2,1,0:T(8,128)(2,1)} %get-tuple-element.86.refs_1_), custom_call_target="tpu_custom_call" | custom-call | flops 11000000512 | bytes 36000000 | tf_op jit(solution)/shard_map/assemble/pallas_call | solution.py:558
  260.4 7.1 %collective-permute-done.17.b = f32[24,32,128]{2,1,0:T(8,128)S(1)} collective-permute-done((f32[24,32,128]{2,1,0:T(8,128)}, f32[24,32,128]{2,1,0:T(8,128)S(1)}, u32[]{:S(2)}, u32[]{:S(2)}) %collective-permute-start.17) | collective-permute-done | bytes 393248 | tf_op jit(solution)/shard_map/ppermute | solution.py:641
  267.6 14.2 %collective-permute-done.19.d = f32[24,32,128]{2,1,0:T(8,128)S(1)} collective-permute-done((f32[24,32,128]{2,1,0:T(8,128)}, f32[24,32,128]{2,1,0:T(8,128)S(1)}, u32[]{:S(2)}, u32[]{:S(2)}) %collective-permute-start.19) | collective-permute-done | bytes 393248 | tf_op jit(solution)/shard_map/ppermute | solution.py:641
  282.6 3.1 merge.5.refs_2_.refs_0_.refs_5_
  286.3 1.5 collective-permute-start.21
  289.1 2.6 assemble.4.refs_4_
  291.7 7.1 %collective-permute-done.22.refs_3_ = f32[32,24,128]{2,1,0:T(8,128)S(1)} collective-permute-done((f32[32,24,128]{2,1,0:T(8,128)}, f32[32,24,128]{2,1,0:T(8,128)S(1)}, u32[]{:S(2)}, u32[]{:S(2)}) %collective-permute-start.22) | collective-permute-done | bytes 393248 | tf_op jit(solution)/shard_map/ppermute | solution.py:641
  298.8 6.7 %collective-permute-done.21.refs_2_ = f32[32,24,128]{2,1,0:T(8,128)S(1)} collective-permute-done((f32[32,24,128]{2,1,0:T(8,128)}, f32[32,24,128]{2,1,0:T(8,128)S(1)}, u32[]{:S(2)}, u32[]{:S(2)}) %collective-permute-start.21) | collective-permute-done | bytes 393248 | tf_op jit(solution)/shard_map/ppermute | solution.py:641
  306.9 2.5 assemble.5
  (88 shorter events, 19.5 us)
Async XLA Ops:
  12.0 13.1 %collective-permute-start = (f32[32,8,512]{2,1,0:T(8,128)}, f32[32,8,512]{2,1,0:T(8,128)S(1)}, u32[]{:S(2)}, u32[]{:S(2)}) collective-permute-start(f32[32,8,512]{2,1,0:T(8,128)} %get-tuple-element.50), channel_id=1, source_target_pairs={{1,2},{3,4},{5,6},{2,1},{4,3},{6,5},{9,10},{11,12},{13,14},{10,9},... | collective-permute-start | bytes 1572872 | tf_op jit(solution)/shard_map/ppermute | solution.py:660
  13.9 52.0 %collective-permute-start.1 = (f32[128,8,512]{2,1,0:T(8,128)}, f32[128,8,512]{2,1,0:T(8,128)}, u32[]{:S(2)}, u32[]{:S(2)}) collective-permute-start(f32[128,8,512]{2,1,0:T(8,128)} %get-tuple-element.46.after), channel_id=1, source_target_pairs={{0,1},{1,0},{2,3},{3,2},{4,5},{5,4},{6,7},{7,6},{8,9},{9,8},{10,11... | collective-permute-start | bytes 6291464 | tf_op jit(solution)/shard_map/ppermute | solution.py:660
  25.1 0.8 copy-start.4
  25.9 4.3 %copy-start.24 = (s32[1,4]{1,0:T(1,128)S(1)}, s32[1,4]{1,0:T(1,128)}, u32[]{:S(2)}) copy-start(s32[1,4]{1,0:T(1,128)} %param.13) | copy-start | bytes 52
  25.9 75.4 %all-to-all-start = ((f32[8,800,128]{2,1,0:T(8,128)}), f32[8,800,128]{2,1,0:T(8,128)S(1)}, u32[]{:S(2)}, u32[]{:S(2)}) async-start(f32[8,800,128]{2,1,0:T(8,128)} %gate.3), calls=%async_computation | async-start | bytes 6553600 | tf_op jit(solution)/shard_map/all_to_all | solution.py:664
  31.5 8.2 %copy-start.5 = (f32[32,8,512]{2,1,0:T(8,128)S(1)}, f32[32,8,512]{2,1,0:T(8,128)}, u32[]{:S(2)}) copy-start(f32[32,8,512]{2,1,0:T(8,128)} %copy-done.4) | copy-start | bytes 1572868
  39.8 15.7 %collective-permute-start.4 = (f32[32,8,512]{2,1,0:T(8,128)S(1)}, f32[32,8,512]{2,1,0:T(8,128)S(1)}, u32[]{:S(2)}, u32[]{:S(2)}) collective-permute-start(f32[32,8,512]{2,1,0:T(8,128)S(1)} %copy-done.5), channel_id=1, source_target_pairs={{0,24},{8,16},{16,8},{24,0},{1,25},{9,17},{17,9},{25,1},{2,26},{10... | collective-permute-start | bytes 1572872 | tf_op jit(solution)/shard_map/ppermute | solution.py:641
  42.2 23.7 %collective-permute-start.3 = (f32[32,8,512]{2,1,0:T(8,128)S(1)}, f32[32,8,512]{2,1,0:T(8,128)S(1)}, u32[]{:S(2)}, u32[]{:S(2)}) collective-permute-start(f32[32,8,512]{2,1,0:T(8,128)S(1)} %copy-done.5), channel_id=1, source_target_pairs={{0,16},{8,24},{16,0},{24,8},{1,17},{9,25},{17,1},{25,9},{2,18},{10... | collective-permute-start | bytes 1572872 | tf_op jit(solution)/shard_map/ppermute | solution.py:641
  42.7 23.3 %collective-permute-start.2 = (f32[32,8,512]{2,1,0:T(8,128)S(1)}, f32[32,8,512]{2,1,0:T(8,128)S(1)}, u32[]{:S(2)}, u32[]{:S(2)}) collective-permute-start(f32[32,8,512]{2,1,0:T(8,128)S(1)} %copy-done.5), channel_id=1, source_target_pairs={{0,8},{8,0},{16,24},{24,16},{1,9},{9,1},{17,25},{25,17},{2,10},{10... | collective-permute-start | bytes 1572872 | tf_op jit(solution)/shard_map/ppermute | solution.py:641
  55.5 10.5 %copy-start.9 = (f32[32,8,512]{2,1,0:T(8,128)}, f32[32,8,512]{2,1,0:T(8,128)S(1)}, u32[]{:S(2)}) copy-start(f32[32,8,512]{2,1,0:T(8,128)S(1)} %collective-permute-done.4.d) | copy-start | bytes 1572868
  65.9 0.8 copy-start.10
  66.0 0.9 copy-start.11
  92.9 19.6 %copy-start.25 = (f32[1,15]{1,0:T(1,128)S(1)}, f32[1,15]{1,0:T(1,128)}, u32[]{:S(2)}) copy-start(f32[1,15]{1,0:T(1,128)} %profile_y.1) | copy-start | bytes 184
  101.3 1.7 copy-start
  110.1 3.0 collective-permute-start.5
  110.1 20.7 %collective-permute-start.6 = (f32[15,128,128]{2,1,0:T(8,128)}, f32[15,128,128]{2,1,0:T(8,128)S(1)}, u32[]{:S(2)}, u32[]{:S(2)}) collective-permute-start(f32[15,128,128]{2,1,0:T(8,128)} %get-tuple-element.59), channel_id=1, source_target_pairs={{1,2},{3,4},{5,6},{2,1},{4,3},{6,5},{9,10},{11,12},{13,14},{10,9},... | collective-permute-start | bytes 2949128 | tf_op jit(solution)/shard_map/ppermute | solution.py:660
  113.1 0.9 copy-start.3
  114.1 44.0 %all-to-all-start.1 = ((f32[8,384,128]{2,1,0:T(8,128)}), f32[8,384,128]{2,1,0:T(8,128)S(1)}, u32[]{:S(2)}, u32[]{:S(2)}) async-start(f32[8,384,128]{2,1,0:T(8,128)} %gate.4), calls=%async_computation.1 | async-start | bytes 3145728 | tf_op jit(solution)/shard_map/all_to_all | solution.py:664
  120.6 136.1 %all-gather.3.cloned.1.call-start = ((), (), s32[]{:S(2)}) async-start(), calls=%async_computation.3 | async-start | bytes 3932160 | tf_op jit(solution)/shard_map/all_gather | solution.py:669
  130.8 1.0 copy-start.6
  147.1 19.1 %collective-permute-start.9 = (f32[48,32,128]{2,1,0:T(8,128)}, f32[48,32,128]{2,1,0:T(8,128)S(1)}, u32[]{:S(2)}, u32[]{:S(2)}) collective-permute-start(f32[48,32,128]{2,1,0:T(8,128)} %get-tuple-element.70), channel_id=1, source_target_pairs={{0,8},{8,0},{16,24},{24,16},{1,9},{9,1},{17,25},{25,17},{2,10},{10... | collective-permute-start | bytes 2359304 | tf_op jit(solution)/shard_map/ppermute | solution.py:641
  148.7 20.2 %collective-permute-start.10 = (f32[48,32,128]{2,1,0:T(8,128)}, f32[48,32,128]{2,1,0:T(8,128)S(1)}, u32[]{:S(2)}, u32[]{:S(2)}) collective-permute-start(f32[48,32,128]{2,1,0:T(8,128)} %get-tuple-element.71), channel_id=1, source_target_pairs={{0,16},{8,24},{16,0},{24,8},{1,17},{9,25},{17,1},{25,9},{2,18},{10... | collective-permute-start | bytes 2359304 | tf_op jit(solution)/shard_map/ppermute | solution.py:641
  150.2 34.1 %collective-permute-start.11 = (f32[48,32,128]{2,1,0:T(8,128)}, f32[48,32,128]{2,1,0:T(8,128)}, u32[]{:S(2)}, u32[]{:S(2)}) collective-permute-start(f32[48,32,128]{2,1,0:T(8,128)} %get-tuple-element.72), channel_id=1, source_target_pairs={{0,24},{8,16},{16,8},{24,0},{1,25},{9,17},{17,9},{25,1},{2,26},{10... | collective-permute-start | bytes 2359304 | tf_op jit(solution)/shard_map/ppermute | solution.py:641
  158.1 1.1 copy-start.1
  162.8 25.1 %collective-permute-start.7 = (f32[7,128,128]{2,1,0:T(8,128)}, f32[7,128,128]{2,1,0:T(8,128)S(1)}, u32[]{:S(2)}, u32[]{:S(2)}) collective-permute-start(f32[7,128,128]{2,1,0:T(8,128)} %get-tuple-element.65), channel_id=1, source_target_pairs={{0,1},{1,0},{2,3},{3,2},{4,5},{5,4},{6,7},{7,6},{8,9},{9,8},{10,11... | collective-permute-start | bytes 1376264 | tf_op jit(solution)/shard_map/ppermute | solution.py:660
  162.8 32.3 %collective-permute-start.8 = (f32[7,128,128]{2,1,0:T(8,128)}, f32[7,128,128]{2,1,0:T(8,128)}, u32[]{:S(2)}, u32[]{:S(2)}) collective-permute-start(f32[7,128,128]{2,1,0:T(8,128)} %get-tuple-element.66), channel_id=1, source_target_pairs={{1,2},{3,4},{5,6},{2,1},{4,3},{6,5},{9,10},{11,12},{13,14},{10,9},... | collective-permute-start | bytes 1376264 | tf_op jit(solution)/shard_map/ppermute | solution.py:660
  166.2 18.0 %copy-start.7 = (f32[48,32,128]{2,1,0:T(8,128)}, f32[48,32,128]{2,1,0:T(8,128)S(1)}, u32[]{:S(2)}) copy-start(f32[48,32,128]{2,1,0:T(8,128)S(1)} %collective-permute-done.9.b) | copy-start | bytes 2359300
  168.9 15.4 %copy-start.8 = (f32[48,32,128]{2,1,0:T(8,128)}, f32[48,32,128]{2,1,0:T(8,128)S(1)}, u32[]{:S(2)}) copy-start(f32[48,32,128]{2,1,0:T(8,128)S(1)} %collective-permute-done.10.c) | copy-start | bytes 2359300
  188.8 41.0 %all-to-all-start.2 = ((f32[8,384,128]{2,1,0:T(8,128)}), f32[8,384,128]{2,1,0:T(8,128)S(1)}, u32[]{:S(2)}, u32[]{:S(2)}) async-start(f32[8,384,128]{2,1,0:T(8,128)} %gate.5), calls=%async_computation.2 | async-start | bytes 3145728 | tf_op jit(solution)/shard_map/all_to_all | solution.py:664
  195.2 94.0 %all-gather.5.cloned.1.call-start = ((), (), s32[]{:S(2)}) async-start(), calls=%async_computation.4 | async-start | bytes 1966080 | tf_op jit(solution)/shard_map/all_gather | solution.py:669
  203.4 33.4 %collective-permute-start.14 = (f32[24,32,128]{2,1,0:T(8,128)}, f32[24,32,128]{2,1,0:T(8,128)S(1)}, u32[]{:S(2)}, u32[]{:S(2)}) collective-permute-start(f32[24,32,128]{2,1,0:T(8,128)} %get-tuple-element.79), channel_id=1, source_target_pairs={{0,8},{8,0},{16,24},{24,16},{1,9},{9,1},{17,25},{25,17},{2,10},{10... | collective-permute-start | bytes 1179656 | tf_op jit(solution)/shard_map/ppermute | solution.py:641
  203.5 33.3 %collective-permute-start.15 = (f32[24,32,128]{2,1,0:T(8,128)}, f32[24,32,128]{2,1,0:T(8,128)S(1)}, u32[]{:S(2)}, u32[]{:S(2)}) collective-permute-start(f32[24,32,128]{2,1,0:T(8,128)} %get-tuple-element.80), channel_id=1, source_target_pairs={{0,16},{8,24},{16,0},{24,8},{1,17},{9,25},{17,1},{25,9},{2,18},{10... | collective-permute-start | bytes 1179656 | tf_op jit(solution)/shard_map/ppermute | solution.py:641
  205.4 31.5 %collective-permute-start.16 = (f32[24,32,128]{2,1,0:T(8,128)}, f32[24,32,128]{2,1,0:T(8,128)S(1)}, u32[]{:S(2)}, u32[]{:S(2)}) collective-permute-start(f32[24,32,128]{2,1,0:T(8,128)} %get-tuple-element.81), channel_id=1, source_target_pairs={{0,24},{8,16},{16,8},{24,0},{1,25},{9,17},{17,9},{25,1},{2,26},{10... | collective-permute-start | bytes 1179656 | tf_op jit(solution)/shard_map/ppermute | solution.py:641
  229.7 1.1 copy-start.2
  234.4 6.5 %collective-permute-start.12 = (f32[7,128,128]{2,1,0:T(8,128)}, f32[7,128,128]{2,1,0:T(8,128)S(1)}, u32[]{:S(2)}, u32[]{:S(2)}) collective-permute-start(f32[7,128,128]{2,1,0:T(8,128)} %get-tuple-element.74), channel_id=1, source_target_pairs={{0,1},{1,0},{2,3},{3,2},{4,5},{5,4},{6,7},{7,6},{8,9},{9,8},{10,11... | collective-permute-start | bytes 1376264 | tf_op jit(solution)/shard_map/ppermute | solution.py:660
  234.4 10.0 %collective-permute-start.13 = (f32[7,128,128]{2,1,0:T(8,128)}, f32[7,128,128]{2,1,0:T(8,128)S(1)}, u32[]{:S(2)}, u32[]{:S(2)}) collective-permute-start(f32[7,128,128]{2,1,0:T(8,128)} %get-tuple-element.75), channel_id=1, source_target_pairs={{1,2},{3,4},{5,6},{2,1},{4,3},{6,5},{9,10},{11,12},{13,14},{10,9},... | collective-permute-start | bytes 1376264 | tf_op jit(solution)/shard_map/ppermute | solution.py:660
  236.8 0.9 copy-start.16
  236.9 1.0 copy-start.17
  240.9 3.5 %copy-start.13 = (f32[7,128,128]{2,1,0:T(8,128)}, f32[7,128,128]{2,1,0:T(8,128)S(1)}, u32[]{:S(2)}) copy-start(f32[7,128,128]{2,1,0:T(8,128)S(1)} %collective-permute-done.12.inner) | copy-start | bytes 1376260
  253.2 14.2 %collective-permute-start.17 = (f32[24,32,128]{2,1,0:T(8,128)}, f32[24,32,128]{2,1,0:T(8,128)S(1)}, u32[]{:S(2)}, u32[]{:S(2)}) collective-permute-start(f32[24,32,128]{2,1,0:T(8,128)} %get-tuple-element.83), channel_id=1, source_target_pairs={{0,8},{8,0},{16,24},{24,16},{1,9},{9,1},{17,25},{25,17},{2,10},{10... | collective-permute-start | bytes 1179656 | tf_op jit(solution)/shard_map/ppermute | solution.py:641
  253.5 14.1 %collective-permute-start.18 = (f32[24,32,128]{2,1,0:T(8,128)}, f32[24,32,128]{2,1,0:T(8,128)S(1)}, u32[]{:S(2)}, u32[]{:S(2)}) collective-permute-start(f32[24,32,128]{2,1,0:T(8,128)} %get-tuple-element.84), channel_id=1, source_target_pairs={{0,16},{8,24},{16,0},{24,8},{1,17},{9,25},{17,1},{25,9},{2,18},{10... | collective-permute-start | bytes 1179656 | tf_op jit(solution)/shard_map/ppermute | solution.py:641
  255.4 26.5 %collective-permute-start.19 = (f32[24,32,128]{2,1,0:T(8,128)}, f32[24,32,128]{2,1,0:T(8,128)S(1)}, u32[]{:S(2)}, u32[]{:S(2)}) collective-permute-start(f32[24,32,128]{2,1,0:T(8,128)} %get-tuple-element.85), channel_id=1, source_target_pairs={{0,24},{8,16},{16,8},{24,0},{1,25},{9,17},{17,9},{25,1},{2,26},{10... | collective-permute-start | bytes 1179656 | tf_op jit(solution)/shard_map/ppermute | solution.py:641
  267.5 14.3 %copy-start.18 = (f32[24,32,128]{2,1,0:T(8,128)}, f32[24,32,128]{2,1,0:T(8,128)S(1)}, u32[]{:S(2)}) copy-start(f32[24,32,128]{2,1,0:T(8,128)S(1)} %collective-permute-done.17.b) | copy-start | bytes 1179652
  267.6 14.3 %copy-start.19 = (f32[24,32,128]{2,1,0:T(8,128)}, f32[24,32,128]{2,1,0:T(8,128)S(1)}, u32[]{:S(2)}) copy-start(f32[24,32,128]{2,1,0:T(8,128)S(1)} %collective-permute-done.18.c) | copy-start | bytes 1179652
  285.6 13.1 %collective-permute-start.22 = (f32[32,24,128]{2,1,0:T(8,128)}, f32[32,24,128]{2,1,0:T(8,128)S(1)}, u32[]{:S(2)}, u32[]{:S(2)}) collective-permute-start(f32[32,24,128]{2,1,0:T(8,128)} %merge.5.refs_2_.refs_0_.refs_5_), channel_id=1, source_target_pairs={{0,24},{8,16},{16,8},{24,0},{1,25},{9,17},{17,9},{25,1},{2,26},{10... | collective-permute-start | bytes 1179656 | tf_op jit(solution)/shard_map/ppermute | solution.py:641
  286.3 19.2 %collective-permute-start.21 = (f32[32,24,128]{2,1,0:T(8,128)}, f32[32,24,128]{2,1,0:T(8,128)S(1)}, u32[]{:S(2)}, u32[]{:S(2)}) collective-permute-start(f32[32,24,128]{2,1,0:T(8,128)} %merge.5.refs_2_.refs_0_.refs_5_), channel_id=1, source_target_pairs={{0,16},{8,24},{16,0},{24,8},{1,17},{9,25},{17,1},{25,9},{2,18},{10... | collective-permute-start | bytes 1179656 | tf_op jit(solution)/shard_map/ppermute | solution.py:641
  287.8 17.7 %collective-permute-start.20 = (f32[32,24,128]{2,1,0:T(8,128)}, f32[32,24,128]{2,1,0:T(8,128)S(1)}, u32[]{:S(2)}, u32[]{:S(2)}) collective-permute-start(f32[32,24,128]{2,1,0:T(8,128)} %merge.5.refs_2_.refs_0_.refs_5_), channel_id=1, source_target_pairs={{0,8},{8,0},{16,24},{24,16},{1,9},{9,1},{17,25},{25,17},{2,10},{10... | collective-permute-start | bytes 1179656 | tf_op jit(solution)/shard_map/ppermute | solution.py:641
  298.8 6.7 %copy-start.20 = (f32[32,24,128]{2,1,0:T(8,128)}, f32[32,24,128]{2,1,0:T(8,128)S(1)}, u32[]{:S(2)}) copy-start(f32[32,24,128]{2,1,0:T(8,128)S(1)} %collective-permute-done.22.refs_3_) | copy-start | bytes 1179652
  (6 other events, 4.5 us)
Sparse Core Ops, SparseCore 0:
  188.1 55.0 all-gather.2
  245.0 40.3 all-gather.4
